TPU v7x, 1024 devices: a whole 8x8x8 slice. The times are simulated.
1024 devices in a mesh: seq: 32 (over y, x_lo), fsdp: 32 (over z, x_hi, core).
Axes of the slice: x: 8 (x_hi: 2, x_lo: 4; x = x_hi * 4 + x_lo), y: 8, z: 8, core: 2. Of those that a mesh axis runs over, the one named last changes fastest.
Arguments:
- queries: bfloat16 [4096, 8192], P('seq', 'fsdp'), may hold values from -120 to 120
- keys: bfloat16 [4096, 1024], P('seq'), may hold values from -4 to 4
- values: bfloat16 [4096, 1024], P('seq'), may hold values from -6 to 6
- out_weight: bfloat16 [8192, 8192], P(None, 'fsdp'), may hold values from -0.09375 to 0.09375
- block_mask: int32 [64, 64], P(None, 'fsdp'), may hold values 0 or 1
Outputs:
- mixed: bfloat16 [4096, 8192], P('seq', 'fsdp')
All inputs are finite; a program needn't handle non-finite values. No bound on the sum of `block_mask` on one device may be relied on, other than what follows from the above.
Results may differ from a plain program's by a relative error of at most 0.0085.
Values may be sent and summed in bfloat16 or wider, within the bound.
No kernel may reach another device: no remote copies, remote signals or barrier semaphores. Data moves between devices by JAX's collectives and lax.ppermute only.
A program may use at most 32 MiB of HBM per device.

v0:
```python
import math

import jax
import jax.numpy as jnp
from jax import lax
from jax.sharding import PartitionSpec as P

HD = 128
BLOCK = 128
GROUP = 8


def update_block(carry, query_block, query_start, key_piece, value_piece, heads_dev):
    top, total, summed = carry
    rows = query_block.shape[0]
    width = key_piece.shape[0]
    scale = 1.0 / math.sqrt(HD)
    split_heads = query_block.reshape(rows, heads_dev, HD)
    score = (
        jnp.einsum("rhd,pd->hrp", split_heads, key_piece, preferred_element_type=jnp.float32)
        * scale
    )
    query_pos = query_start + jnp.arange(rows, dtype=jnp.int32)
    key_pos = jnp.arange(width, dtype=jnp.int32)
    allowed = (query_pos[:, None] >= key_pos[None, :])[None]
    score = jnp.where(allowed, score, jnp.float32(-1e30))
    new_top = jnp.maximum(top, jnp.max(score, axis=2))
    expo = jnp.where(allowed, jnp.exp(score - new_top[:, :, None]), jnp.float32(0.0))
    total = jnp.sum(expo, axis=2)
    product = jnp.einsum(
        "hrp,pd->hrd", expo.astype(jnp.bfloat16), value_piece, preferred_element_type=jnp.float32
    )
    summed = product
    return (new_top, total, summed)


def per_device(queries, keys, values, out_weight, block_mask):
    seq_index = lax.axis_index("seq")
    head_index = lax.axis_index("fsdp")
    rows = queries.shape[0]
    heads_dev = queries.shape[1] // HD
    kv_column = head_index * heads_dev // GROUP * HD
    key_rows = lax.dynamic_slice_in_dim(keys, kv_column, HD, 1)
    value_rows = lax.dynamic_slice_in_dim(values, kv_column, HD, 1)
    own_start = seq_index * rows
    query_blocks = [(queries, own_start)]
    initial = tuple(
        (
            (
                jnp.full((heads_dev, block.shape[0]), -1e30, jnp.float32),
                jnp.zeros((heads_dev, block.shape[0]), jnp.float32),
                jnp.zeros((heads_dev, block.shape[0], HD), jnp.float32),
            )
            for block, start in query_blocks
        )
    )
    key_start = jnp.int32(0)
    key_piece = lax.all_gather(key_rows, "seq", axis=0, tiled=True)
    value_piece = lax.all_gather(value_rows, "seq", axis=0, tiled=True)
    result = []
    for carry, (block, start) in zip(initial, query_blocks):
        needed = key_start <= start + block.shape[0] - 1
        carry = lax.cond(
            needed,
            lambda state: update_block(state, block, start, key_piece, value_piece, heads_dev),
            lambda state: state,
            carry,
        )
        result.append(carry)
    folded = tuple(result)
    finished = []
    for top, total, summed in folded:
        normed = summed / total[:, :, None]
        finished.append(
            normed.transpose(1, 0, 2).reshape(normed.shape[1], heads_dev * HD).astype(jnp.bfloat16)
        )
    heads_out = finished[0]
    keep = jnp.repeat(jnp.repeat(block_mask, BLOCK, axis=0), BLOCK, axis=1)
    pruned = out_weight * keep.astype(out_weight.dtype)
    mixed = jnp.dot(
        lax.all_gather(heads_out, "fsdp", axis=1, tiled=True),
        pruned,
        preferred_element_type=jnp.float32,
    )
    return mixed.astype(jnp.bfloat16)


def solution(mesh):
    return jax.shard_map(
        per_device,
        mesh=mesh,
        in_specs=(
            P("seq", "fsdp"),
            P("seq", None),
            P("seq", None),
            P(None, "fsdp"),
            P(None, "fsdp"),
        ),
        out_specs=P("seq", "fsdp"),
        check_vma=False,
    )
```

profile of v0, /device:TPU:1, one launch (start us, length us, event | category | flops | bytes accessed | tf_op | source)
XLA Modules:
  0.0 472.9 jit_solution(15186502538824779789)
XLA Ops:
  6.5 0.0 copy-start
  6.5 0.0 all-gather.4.cloned.1.call-start
  6.5 0.9 copy-done
  7.5 0.6 constant_dynamic-slice_fusion.1
  8.1 0.0 all-gather.4.cloned.1.call-update
  8.1 0.0 all-gather.6.cloned.1.call-start
  8.2 1.4 constant_dynamic-slice_fusion
  9.6 0.0 all-gather.6.cloned.1.call-update
  9.6 0.0 all-gather.8.cloned.1.call-start
  9.6 147.1 %all-gather.4.cloned.1.call-done = bf16[4096,128]{1,0:T(8,128)(2,1)} async-done(((bf16[128,128]{1,0:T(8,128)(2,1)}), bf16[4096,128]{1,0:T(8,128)(2,1)}) %all-gather.4.cloned.1.call-update) | async-done | bytes 1048592 | tf_op jit(solution)/shard_map/all_gather | solution.py:58
  156.7 159.2 %all-gather.6.cloned.1.call-done = bf16[4096,128]{1,0:T(8,128)(2,1)} async-done(((bf16[128,128]{1,0:T(8,128)(2,1)}), bf16[4096,128]{1,0:T(8,128)(2,1)}) %all-gather.6.cloned.1.call-update) | async-done | bytes 1048592 | tf_op jit(solution)/shard_map/all_gather | solution.py:59
  316.0 0.0 copy-start.4
  316.0 4.3 conditional.1
  316.0 0.0 copy-start.3
  316.0 0.3 iota_compare_fusion
  316.3 2.1 fusion.17
  318.4 0.0 copy-done.3
  318.5 0.9 fusion.4
  319.4 0.8 fusion.3
  320.2 0.6 divide_convert_fusion
  320.9 0.0 all-gather.8.cloned.1.call-update
  320.9 0.0 copy-done.4
  320.9 0.1 copy.13
  321.0 120.0 %all-gather.8.cloned.1.call-done = bf16[128,8192]{0,1:T(8,128)(2,1)} async-done(((bf16[128,256]{0,1:T(8,128)(2,1)}), bf16[128,8192]{0,1:T(8,128)(2,1)}) %all-gather.8.cloned.1.call-update) | async-done | bytes 2097168 | tf_op jit(solution)/shard_map/all_gather | solution.py:81
  441.1 0.0 copy-start.1
  441.1 0.0 copy-start.2
  441.1 0.3 broadcast_in_dim.38
  441.3 23.2 %broadcast_in_dim.39 = bf16[8192,2,128]{2,1,0:T(2,128)(2,1)S(1)} broadcast(bf16[8192,2]{1,0:T(8,128)(2,1)S(1)} %bitcast.33), dimensions={0,1} | broadcast | bytes 4227072 | tf_op jit(solution)/shard_map/broadcast_in_dim | solution.py:78
  464.6 0.0 copy-done.1
  464.6 0.0 copy-done.2
  464.6 1.7 fusion.16
  (3 shorter events, 0.0 us)
Async XLA Ops:
  6.5 1.0 copy-start
  6.5 150.2 %all-gather.4.cloned.1.call-start = ((), (), s32[]{:S(2)}) async-start(), calls=%async_computation | async-start | bytes 1081344 | tf_op jit(solution)/shard_map/all_gather | solution.py:58
  8.1 307.8 %all-gather.6.cloned.1.call-start = ((), (), s32[]{:S(2)}) async-start(), calls=%async_computation.1 | async-start | bytes 1081344 | tf_op jit(solution)/shard_map/all_gather | solution.py:59
  9.6 431.5 %all-gather.8.cloned.1.call-start = ((), (), s32[]{:S(2)}) async-start(), calls=%async_computation.2 | async-start | bytes 2162688 | tf_op jit(solution)/shard_map/all_gather | solution.py:81
  316.0 4.9 %copy-start.4 = (s32[64,2]{0,1:T(2,128)S(1)}, s32[64,2]{0,1:T(2,128)}, u32[]{:S(2)}) copy-start(s32[64,2]{0,1:T(2,128)} %param.11) | copy-start | bytes 1540
  316.0 2.5 copy-start.3
  441.1 23.5 %copy-start.1 = (bf16[8192,256]{1,0:T(8,128)(2,1)S(1)}, bf16[8192,256]{1,0:T(8,128)(2,1)}, u32[]{:S(2)}) copy-start(bf16[8192,256]{1,0:T(8,128)(2,1)} %param.10) | copy-start | bytes 12582916
  441.1 23.5 %copy-start.2 = (bf16[128,8192]{0,1:T(8,128)(2,1)S(1)}, bf16[128,8192]{0,1:T(8,128)(2,1)}, u32[]{:S(2)}) copy-start(bf16[128,8192]{0,1:T(8,128)(2,1)} %all-gather.8.cloned.1.call-done) | copy-start | bytes 6291460
Sparse Core Ops, SparseCore 0:
  10.0 146.6 all-gather.3
  159.4 156.5 all-gather.5
  321.0 119.9 all-gather.7
where the time goes:
time: 475 us; the launch traced here: 473 us
  waiting for transfers between devices  426 us (90%)
  local copies, waits for them, and re-layouts  26.6 us (6%)
  between operations  13.2 us (3%)
  matrix products  4.79 us (1%)
    all_gather x1, waiting for transfers between devices, per_device(): value_piece = lax.all_gather(value_rows, 'seq', axis=0, tiled=True)  159 us
    all_gather x1, waiting for transfers between devices, per_device(): key_piece = lax.all_gather(key_rows, 'seq', axis=0, tiled=True)  147 us
    all_gather x1, waiting for transfers between devices, per_device(): lax.all_gather(heads_out, 'fsdp', axis=1, tiled=True)  120 us
    broadcast_in_dim x2, local copies, waits for them, and re-layouts, per_device(): keep = jnp.repeat(jnp.repeat(block_mask, BLOCK, axis=0), BLOCK, axis=1)  23.5 us
  transfers between devices with their start and end apart: 3, of which 3 were waited for; matrix products, arithmetic and copies ran while one was open for 0% of the time, Pallas kernels for 0%

commit v1 on v0

v1 whole, which is shorter than its diff:
```python
import math

import jax
import jax.numpy as jnp
from jax import lax
from jax.experimental import pallas as pl
from jax.experimental.pallas import tpu as pltpu
from jax.sharding import Mesh
from jax.sharding import PartitionSpec as P

HD = 128
BLOCK = 128
SIZES = (8, 4, 8, 2, 2)
AXES = ("y", "xl", "z", "xh", "core")
SEQ = ("y", "xl")
FSDP = ("z", "xh", "core")
N_SEQ = 32
N_CHIP = 16
CHUNK = 16
FACTOR = math.log2(math.e) / math.sqrt(HD)
LOWEST = -1e30
ANY = pl.BlockSpec(memory_space=pl.ANY)
VMEM = pl.BlockSpec(memory_space=pltpu.VMEM)
SMEM = pl.BlockSpec(memory_space=pltpu.SMEM)


def spread_kernel(keys_ref, values_ref, out_ref, piece, sems):
    half = piece.shape[0]
    column = pl.multiple_of(lax.axis_index("z") * HD, HD)
    row = pl.multiple_of(lax.axis_index("core") * half, half)
    place = (pl.ds(row, half), pl.ds(column, HD))
    key_copy = pltpu.make_async_copy(keys_ref.at[place], piece.at[:, :HD], sems.at[0])
    value_copy = pltpu.make_async_copy(values_ref.at[place], piece.at[:, HD:], sems.at[1])
    key_copy.start()
    value_copy.start()
    key_copy.wait()
    value_copy.wait()
    block = piece[...]
    for i in range(N_SEQ):
        out_ref[i] = block


def attend(queries_ref, kv_ref, from_core, top, total, summed):
    rows = queries_ref.shape[0]
    half = kv_ref.shape[1]
    width = CHUNK * half
    own = (lax.axis_index("y") * SIZES[1] + lax.axis_index("xl")) * rows
    q = jnp.concatenate([queries_ref[:, :HD], queries_ref[:, HD:]], axis=0)
    query_pos = own + lax.broadcasted_iota(jnp.int32, (2 * rows, width), 0) % rows
    column = lax.broadcasted_iota(jnp.int32, (2 * rows, width), 1)
    key_pos = column // half * rows + column % half + from_core * half
    ahead = query_pos - key_pos
    for first in range(0, N_SEQ, CHUNK):
        key = kv_ref[first : first + CHUNK, :, :HD].reshape(width, HD)
        value = kv_ref[first : first + CHUNK, :, HD:].reshape(width, HD)
        score = lax.dot_general(
            q, key, (((1,), (1,)), ((), ())), preferred_element_type=jnp.float32
        )
        score = jnp.where(ahead >= first * rows, score, jnp.float32(LOWEST))
        new_top = jnp.max(score, axis=1, keepdims=True)
        if top is not None:
            new_top = jnp.maximum(top, new_top)
        expo = jnp.exp2((score - new_top) * FACTOR)
        part = jnp.sum(expo, axis=1, keepdims=True)
        product = jnp.dot(expo.astype(jnp.bfloat16), value, preferred_element_type=jnp.float32)
        if top is None:
            total, summed = part, product
        else:
            fix = jnp.exp2((top - new_top) * FACTOR)
            total, summed = total * fix + part, summed * fix + product
        top = new_top
    return top, total, summed


def attention_own_kernel(queries_ref, kv_ref, top_ref, total_ref, summed_ref):
    top, total, summed = attend(queries_ref, kv_ref, lax.axis_index("core"), None, None, None)
    top_ref[...] = jnp.broadcast_to(top, top_ref.shape)
    total_ref[...] = jnp.broadcast_to(total, total_ref.shape)
    summed_ref[...] = summed


def attention_other_kernel(queries_ref, kv_ref, top_ref, total_ref, summed_ref, out_ref):
    rows = queries_ref.shape[0]
    _, total, summed = attend(
        queries_ref,
        kv_ref,
        1 - lax.axis_index("core"),
        top_ref[:, :1],
        total_ref[:, :1],
        summed_ref[...],
    )
    normed = (summed / total).astype(jnp.bfloat16)
    heads = jnp.concatenate([normed[:rows], normed[rows:]], axis=1)
    for i in range(N_CHIP):
        out_ref[i] = heads


def project(mask_ref, heads_ref, weight_ref, from_core):
    columns = weight_ref.shape[1]
    total = jnp.zeros((heads_ref.shape[1], columns), jnp.float32)
    for chip in range(N_CHIP):
        rows = []
        for i in range(2):
            block = (chip * 2 + from_core) * 2 + i
            at = pl.ds(pl.multiple_of(block * BLOCK, BLOCK), BLOCK)
            line = []
            for j in range(columns // BLOCK):
                keep = mask_ref[j, block].astype(jnp.float32).astype(jnp.bfloat16)
                line.append(weight_ref[at, j * BLOCK : (j + 1) * BLOCK] * keep)
            rows.append(jnp.concatenate(line, axis=1))
        pruned = jnp.concatenate(rows, axis=0)
        total += jnp.dot(heads_ref[chip], pruned, preferred_element_type=jnp.float32)
    return total


def project_own_kernel(mask_ref, heads_ref, weight_ref, out_ref):
    out_ref[...] = project(mask_ref, heads_ref, weight_ref, lax.axis_index("core"))


def project_other_kernel(mask_ref, heads_ref, weight_ref, part_ref, out_ref):
    rest = project(mask_ref, heads_ref, weight_ref, 1 - lax.axis_index("core"))
    out_ref[...] = (part_ref[...] + rest).astype(out_ref.dtype)


def per_device(queries, keys, values, out_weight, block_mask):
    rows = queries.shape[0]
    columns = out_weight.shape[1]
    half = rows // 2
    mask = block_mask.T
    params = pltpu.CompilerParams(vmem_limit_bytes=32 * 2**20)
    shape = jax.ShapeDtypeStruct
    spread = pl.pallas_call(
        spread_kernel,
        out_shape=shape((N_SEQ, half, 2 * HD), jnp.bfloat16),
        in_specs=[ANY, ANY],
        out_specs=VMEM,
        scratch_shapes=[pltpu.VMEM((half, 2 * HD), jnp.bfloat16), pltpu.SemaphoreType.DMA((2,))],
        name="spread_kv",
    )(keys, values)
    swap = [(0, 1), (1, 0)]
    own = lax.all_to_all(spread, SEQ, 0, 0, tiled=True)
    other = lax.ppermute(own, "core", swap)
    state = shape((2 * rows, HD), jnp.float32)
    carry = pl.pallas_call(
        attention_own_kernel,
        out_shape=[state] * 3,
        in_specs=[VMEM] * 2,
        out_specs=[VMEM] * 3,
        compiler_params=params,
        cost_estimate=pl.CostEstimate(flops=2**29, bytes_accessed=2**21, transcendentals=2**19),
        name="attention_own",
    )(queries, own)
    heads = pl.pallas_call(
        attention_other_kernel,
        out_shape=shape((N_CHIP, rows, 2 * HD), jnp.bfloat16),
        in_specs=[VMEM] * 5,
        out_specs=VMEM,
        compiler_params=params,
        cost_estimate=pl.CostEstimate(flops=2**29, bytes_accessed=2**21, transcendentals=2**19),
        name="attention_other",
    )(queries, other, *carry)
    own_heads = lax.all_to_all(heads, ("z", "xh"), 0, 0, tiled=True)
    other_heads = lax.ppermute(own_heads, "core", swap)
    part = pl.pallas_call(
        project_own_kernel,
        out_shape=shape((rows, columns), jnp.float32),
        in_specs=[SMEM, VMEM, VMEM],
        out_specs=VMEM,
        compiler_params=params,
        cost_estimate=pl.CostEstimate(flops=2**28, bytes_accessed=2**22, transcendentals=0),
        name="project_own",
    )(mask, own_heads, out_weight)
    return pl.pallas_call(
        project_other_kernel,
        out_shape=shape((rows, columns), jnp.bfloat16),
        in_specs=[SMEM, VMEM, VMEM, VMEM],
        out_specs=VMEM,
        compiler_params=params,
        cost_estimate=pl.CostEstimate(flops=2**28, bytes_accessed=2**22, transcendentals=0),
        name="project_other",
    )(mask, other_heads, out_weight, part)


def solution(mesh):
    fine = Mesh(mesh.devices.reshape(SIZES), AXES)
    return jax.shard_map(
        per_device,
        mesh=fine,
        in_specs=(P(SEQ, FSDP), P(SEQ, None), P(SEQ, None), P(None, FSDP), P(None, FSDP)),
        out_specs=P(SEQ, FSDP),
        check_vma=False,
    )
```

time: 475 us -> 109 us (0.23)
  the two profiles are of different devices: /device:TPU:1 before, /device:TPU:5 now
where the time goes in v1:
time: 109 us
  blocking collectives  90.8 us (83%)
  starting transfers between devices  8.31 us (8%)
  Pallas kernels  7.43 us (7%)
  waiting for transfers between devices  1.34 us (1%)
    all_to_all x1, blocking collectives, per_device(): own_heads = lax.all_to_all(heads, ('z', 'xh'), 0, 0, tiled=True)  55.4 us
    all_to_all x1, blocking collectives, per_device(): own = lax.all_to_all(spread, SEQ, 0, 0, tiled=True)  35.4 us
    ppermute x1, starting transfers between devices, per_device(): other = lax.ppermute(own, 'core', swap)  5.25 us
    ppermute x1, starting transfers between devices, per_device(): other_heads = lax.ppermute(own_heads, 'core', swap)  3.06 us
  transfers between devices with their start and end apart: 2, of which 2 were waited for; matrix products, arithmetic and copies ran while one was open for 0% of the time, Pallas kernels for 2%

profile of v1, /device:TPU:5, one launch (start us, length us, event | category | flops | bytes accessed | tf_op | source)
XLA Modules:
  0.0 108.8 jit_solution(11103297603469016809)
XLA Ops:
  0.0 0.0 copy-start.2
  0.0 1.9 %spread_kv.1 = bf16[32,64,256]{2,1,0:T(8,128)(2,1)} custom-call(bf16[128,1024]{1,0:T(8,128)(2,1)} %keys_ref.1, bf16[128,1024]{1,0:T(8,128)(2,1)} %values_ref.1), custom_call_target="tpu_custom_call" | custom-call | tf_op jit(solution)/shard_map/spread_kv/pallas_call | solution.py:132
  1.9 0.0 copy-start
  1.9 35.4 %all_to_all.10.kv_ref = bf16[32,64,256]{2,1,0:T(8,128)(2,1)S(1)} all-to-all(bf16[32,64,256]{2,1,0:T(8,128)(2,1)} %spread_kv.1), channel_id=1, replica_groups=mesh['y'=8,'xl'=4,'z'=8,'xh'=2,'core'=2] {'y','xl'}, dimensions={0} | all-to-all | bytes 2097152 | tf_op jit(solution)/shard_map/all_to_all | solution.py:141
  37.3 5.3 %collective-permute-start = (bf16[32,64,256]{2,1,0:T(8,128)(2,1)S(1)}, bf16[32,64,256]{2,1,0:T(8,128)(2,1)S(1)}, u32[]{:S(2)}, u32[]{:S(2)}) collective-permute-start(bf16[32,64,256]{2,1,0:T(8,128)(2,1)S(1)} %all_to_all.10.kv_ref), channel_id=1, source_target_pairs={{0,1},{1,0},{2,3},{3,2},{4,5},{5,4},{6,7},{7,6},{8,9},{9,8},{10,11... | collective-permute-start | bytes 3145736 | tf_op jit(solution)/shard_map/ppermute | solution.py:142
  42.6 0.0 copy-start.1
  42.6 0.8 copy-done.1
  43.4 1.2 %attention_own.1 = (f32[256,128]{1,0:T(8,128)S(1)}, f32[256,128]{1,0:T(8,128)S(1)}, f32[256,128]{1,0:T(8,128)S(1)}) custom-call(bf16[128,256]{1,0:T(8,128)(2,1)S(1)} %copy-done.1, bf16[32,64,256]{2,1,0:T(8,128)(2,1)S(1)} %all_to_all.10.kv_ref), custom_call_target="tpu_custom_call" | custom-call | flops 536870912 | bytes 2097152 | tf_op jit(solution)/shard_map/attention_own/pallas_call | solution.py:144
  44.7 0.2 collective-permute-done.kv_ref
  44.8 1.6 %attention_other.1 = bf16[16,128,256]{2,1,0:T(8,128)(2,1)S(1)} custom-call(bf16[128,256]{1,0:T(8,128)(2,1)S(1)} %copy-done.1, bf16[32,64,256]{2,1,0:T(8,128)(2,1)S(1)} %collective-permute-done.kv_ref, f32[256,128]{1,0:T(8,128)S(1)} %get-tuple-element.8.top_ref, f32[256,128]{1,0:T(8,128)S(1)} %get-tuple-element.9.total_ref, ...), custom_call_target="tpu_custom_call" | custom-call | flops 536870912 | bytes 2097152 | tf_op jit(solution)/shard_map/attention_other/pallas_call | solution.py:153
  46.4 55.4 %all_to_all.11.heads_ref = bf16[16,128,256]{2,1,0:T(8,128)(2,1)S(1)} all-to-all(bf16[16,128,256]{2,1,0:T(8,128)(2,1)S(1)} %attention_other.1), channel_id=1, replica_groups=mesh['y'=8,'xl'=4,'z'=8,'xh'=2,'core'=2] {'z','xh'}, dimensions={0} | all-to-all | bytes 2097152 | tf_op jit(solution)/shard_map/all_to_all | solution.py:162
  101.8 3.1 %collective-permute-start.1 = (bf16[16,128,256]{2,1,0:T(8,128)(2,1)S(1)}, bf16[16,128,256]{2,1,0:T(8,128)(2,1)S(1)}, u32[]{:S(2)}, u32[]{:S(2)}) collective-permute-start(bf16[16,128,256]{2,1,0:T(8,128)(2,1)S(1)} %all_to_all.11.heads_ref), channel_id=1, source_target_pairs={{0,1},{1,0},{2,3},{3,2},{4,5},{5,4},{6,7},{7,6},{8,9},{9,8},{10,11... | collective-permute-start | bytes 3145736 | tf_op jit(solution)/shard_map/ppermute | solution.py:163
  104.9 0.0 copy-done.2
  104.9 0.0 copy-done
  104.9 1.1 project_own.1.part_ref
  106.0 1.2 %collective-permute-done.1.heads_ref = bf16[16,128,256]{2,1,0:T(8,128)(2,1)S(1)} collective-permute-done((bf16[16,128,256]{2,1,0:T(8,128)(2,1)S(1)}, bf16[16,128,256]{2,1,0:T(8,128)(2,1)S(1)}, u32[]{:S(2)}, u32[]{:S(2)}) %collective-permute-start.1) | collective-permute-done | bytes 1048608 | tf_op jit(solution)/shard_map/ppermute | solution.py:163
  107.1 1.7 %project_other.1 = bf16[128,256]{1,0:T(8,128)(2,1)} custom-call(s32[2,64]{1,0:T(2,128)S(1)} %bitcast.2, bf16[16,128,256]{2,1,0:T(8,128)(2,1)S(1)} %collective-permute-done.1.heads_ref, bf16[8192,256]{1,0:T(8,128)(2,1)S(1)} %copy-done, f32[128,256]{1,0:T(8,128)S(1)} %project_own.1.part_ref), custom_call_target="tpu_custom_call" | custom-call | flops 268435456 | bytes 4194304 | tf_op jit(solution)/shard_map/project_other/pallas_call | solution.py:173
Async XLA Ops:
  0.0 104.9 %copy-start.2 = (s32[64,2]{0,1:T(2,128)S(1)}, s32[64,2]{0,1:T(2,128)}, u32[]{:S(2)}) copy-start(s32[64,2]{0,1:T(2,128)} %param.9) | copy-start | bytes 1540
  1.9 103.0 %copy-start = (bf16[8192,256]{1,0:T(8,128)(2,1)S(1)}, bf16[8192,256]{1,0:T(8,128)(2,1)}, u32[]{:S(2)}) copy-start(bf16[8192,256]{1,0:T(8,128)(2,1)} %weight_ref.3) | copy-start | bytes 12582916
  37.3 7.5 %collective-permute-start = (bf16[32,64,256]{2,1,0:T(8,128)(2,1)S(1)}, bf16[32,64,256]{2,1,0:T(8,128)(2,1)S(1)}, u32[]{:S(2)}, u32[]{:S(2)}) collective-permute-start(bf16[32,64,256]{2,1,0:T(8,128)(2,1)S(1)} %all_to_all.10.kv_ref), channel_id=1, source_target_pairs={{0,1},{1,0},{2,3},{3,2},{4,5},{5,4},{6,7},{7,6},{8,9},{9,8},{10,11... | collective-permute-start | bytes 3145736 | tf_op jit(solution)/shard_map/ppermute | solution.py:142
  42.6 0.8 copy-start.1
  101.8 5.3 %collective-permute-start.1 = (bf16[16,128,256]{2,1,0:T(8,128)(2,1)S(1)}, bf16[16,128,256]{2,1,0:T(8,128)(2,1)S(1)}, u32[]{:S(2)}, u32[]{:S(2)}) collective-permute-start(bf16[16,128,256]{2,1,0:T(8,128)(2,1)S(1)} %all_to_all.11.heads_ref), channel_id=1, source_target_pairs={{0,1},{1,0},{2,3},{3,2},{4,5},{5,4},{6,7},{7,6},{8,9},{9,8},{10,11... | collective-permute-start | bytes 3145736 | tf_op jit(solution)/shard_map/ppermute | solution.py:163

commit v2 on v1

v2 whole, which is shorter than its diff:
```python
import math

import jax
import jax.numpy as jnp
from jax import lax
from jax.experimental import pallas as pl
from jax.experimental.pallas import tpu as pltpu
from jax.sharding import Mesh
from jax.sharding import PartitionSpec as P

HD = 128
BLOCK = 128
SIZES = (8, 4, 8, 2, 2)
AXES = ("y", "xl", "z", "xh", "core")
SEQ = ("y", "xl")
FSDP = ("z", "xh", "core")
N_SEQ = 32
N_CHIP = 16
FACTOR = math.log2(math.e) / math.sqrt(HD)
LOWEST = -1e30
ANY = pl.BlockSpec(memory_space=pl.ANY)
VMEM = pl.BlockSpec(memory_space=pltpu.VMEM)
SMEM = pl.BlockSpec(memory_space=pltpu.SMEM)


def spread_kernel(queries_ref, keys_ref, values_ref, own_ref, out_ref, pieces, sems):
    rows = keys_ref.shape[0]
    part = pieces.shape[1]
    column = pl.multiple_of(lax.axis_index("z") * HD, HD)
    core = lax.axis_index("core")
    copies = [pltpu.make_async_copy(queries_ref, own_ref, sems.at[4])]
    for parity in range(2):
        row = pl.multiple_of(parity * (rows // 2) + core * part, part)
        place = (pl.ds(row, part), pl.ds(column, HD))
        for i, source in enumerate((keys_ref, values_ref)):
            target = pieces.at[parity, :, i * HD : (i + 1) * HD]
            copies.append(pltpu.make_async_copy(source.at[place], target, sems.at[parity * 2 + i]))
    for copy in copies:
        copy.start()
    for copy in copies:
        copy.wait()
    blocks = pieces[0], pieces[1]
    for i in range(N_SEQ):
        out_ref[i] = blocks[i % 2]


def attend(queries_ref, kv_ref, of_partner, from_core, state):
    rows = queries_ref.shape[0]
    part = kv_ref.shape[1]
    width = N_SEQ * part
    xl = lax.axis_index("xl")
    parity = lax.rem(xl, 2)
    start = (lax.axis_index("y") * SIZES[1] + xl) * rows
    if of_partner:
        start = start + (1 - 2 * parity) * rows
    q = jnp.concatenate([queries_ref[:, :HD], queries_ref[:, HD:]], axis=0)
    query_pos = start + lax.broadcasted_iota(jnp.int32, (2 * rows, 1), 0) % rows
    column = lax.broadcasted_iota(jnp.int32, (1, width), 1)
    key_pos = column // part * rows + column % part + (parity * 2 + from_core) * part
    key = kv_ref[:, :, :HD].reshape(width, HD)
    value = kv_ref[:, :, HD:].reshape(width, HD)
    score = lax.dot_general(q, key, (((1,), (1,)), ((), ())), preferred_element_type=jnp.float32)
    score = jnp.where(query_pos >= key_pos, score, jnp.float32(LOWEST))
    new_top = jnp.max(score, axis=1, keepdims=True)
    if state is not None:
        new_top = jnp.maximum(state[0], new_top)
    expo = jnp.exp2((score - new_top) * FACTOR)
    total = jnp.sum(expo, axis=1, keepdims=True)
    summed = jnp.dot(expo.astype(jnp.bfloat16), value, preferred_element_type=jnp.float32)
    if state is not None:
        fix = jnp.exp2((state[0] - new_top) * FACTOR)
        total = total + state[1] * fix
        summed = summed + state[2] * fix
    return new_top, total, summed


def attention_own_kernel(queries_ref, kv_ref, top_ref, total_ref, summed_ref):
    state = attend(queries_ref, kv_ref, False, lax.axis_index("core"), None)
    for ref, value in zip((top_ref, total_ref, summed_ref), state):
        ref[...] = jnp.broadcast_to(value, ref.shape)


def bf16_pieces(value):
    pieces = []
    for _ in range(3):
        piece = value.astype(jnp.bfloat16)
        pieces.append(piece)
        value = value - piece.astype(jnp.float32)
    return pieces


def attention_other_kernel(
    queries_ref, partner_ref, own_ref, other_ref, top_in, total_in, summed_in,
    top_ref, total_ref, summed_ref, sent_ref,
):
    rows = queries_ref.shape[0]
    core = lax.axis_index("core")
    state = top_in[:, :1], total_in[:, :1], summed_in[...]
    state = attend(queries_ref, other_ref, False, 1 - core, state)
    for ref, value in zip((top_ref, total_ref, summed_ref), state):
        ref[...] = jnp.broadcast_to(value, ref.shape)
    state = attend(partner_ref, own_ref, True, core, None)
    top, total, summed = attend(partner_ref, other_ref, True, 1 - core, state)
    lane = lax.broadcasted_iota(jnp.int32, (rows, HD), 1)
    notes = jnp.zeros((rows, HD), jnp.float32)
    for head in range(2):
        at = slice(head * rows, (head + 1) * rows)
        sent_ref[:, head * HD : (head + 1) * HD] = summed[at].astype(jnp.bfloat16)
        pieces = bf16_pieces(top[at]) + bf16_pieces(total[at])
        for i, piece in enumerate(pieces):
            notes = jnp.where(lane == head * 8 + i, piece.astype(jnp.float32), notes)
    sent_ref[:, 2 * HD :] = notes.astype(jnp.bfloat16)


def merge_kernel(top_ref, total_ref, summed_ref, got_ref, out_ref):
    rows = got_ref.shape[0]
    notes = got_ref[:, 2 * HD :].astype(jnp.float32)
    heads = []
    for head in range(2):
        at = slice(head * rows, (head + 1) * rows)
        own_top, own_total = top_ref[at, :1], total_ref[at, :1]
        first = head * 8
        top = notes[:, first : first + 1] + notes[:, first + 1 : first + 2] + notes[:, first + 2 : first + 3]
        total = notes[:, first + 3 : first + 4] + notes[:, first + 4 : first + 5] + notes[:, first + 5 : first + 6]
        new_top = jnp.maximum(own_top, top)
        own_fix = jnp.exp2((own_top - new_top) * FACTOR)
        fix = jnp.exp2((top - new_top) * FACTOR)
        summed = got_ref[:, head * HD : (head + 1) * HD].astype(jnp.float32)
        summed = summed_ref[at] * own_fix + summed * fix
        heads.append((summed / (own_total * own_fix + total * fix)).astype(jnp.bfloat16))
    block = jnp.concatenate(heads, axis=1)
    for i in range(N_CHIP):
        out_ref[i] = block


def project(mask_ref, heads_ref, weight_ref, from_core):
    columns = weight_ref.shape[1]
    total = jnp.zeros((heads_ref.shape[1], columns), jnp.float32)
    for chip in range(N_CHIP):
        rows = []
        for i in range(2):
            block = (chip * 2 + from_core) * 2 + i
            at = pl.ds(pl.multiple_of(block * BLOCK, BLOCK), BLOCK)
            line = []
            for j in range(columns // BLOCK):
                keep = mask_ref[j, block].astype(jnp.float32).astype(jnp.bfloat16)
                line.append(weight_ref[at, j * BLOCK : (j + 1) * BLOCK] * keep)
            rows.append(jnp.concatenate(line, axis=1))
        pruned = jnp.concatenate(rows, axis=0)
        total += jnp.dot(heads_ref[chip], pruned, preferred_element_type=jnp.float32)
    return total


def project_own_kernel(mask_ref, heads_ref, weight_ref, out_ref):
    out_ref[...] = project(mask_ref, heads_ref, weight_ref, lax.axis_index("core"))


def project_other_kernel(mask_ref, heads_ref, weight_ref, part_ref, out_ref):
    rest = project(mask_ref, heads_ref, weight_ref, 1 - lax.axis_index("core"))
    out_ref[...] = (part_ref[...] + rest).astype(out_ref.dtype)


def per_device(queries, keys, values, out_weight, block_mask):
    rows = queries.shape[0]
    columns = out_weight.shape[1]
    part = rows // 4
    mask = block_mask.T
    params = pltpu.CompilerParams(vmem_limit_bytes=32 * 2**20)
    shape = jax.ShapeDtypeStruct
    cost = pl.CostEstimate(flops=2**29, bytes_accessed=2**21, transcendentals=2**19)
    own_queries, spread = pl.pallas_call(
        spread_kernel,
        out_shape=[
            shape((rows, 2 * HD), jnp.bfloat16),
            shape((N_SEQ, part, 2 * HD), jnp.bfloat16),
        ],
        in_specs=[ANY] * 3,
        out_specs=[VMEM] * 2,
        scratch_shapes=[
            pltpu.VMEM((2, part, 2 * HD), jnp.bfloat16),
            pltpu.SemaphoreType.DMA((5,)),
        ],
        name="spread_kv",
    )(queries, keys, values)
    swap = [(0, 1), (1, 0)]
    swap_x = [(0, 1), (1, 0), (2, 3), (3, 2)]
    partner_queries = lax.ppermute(queries, "xl", swap_x)
    spread, partner_queries = lax.optimization_barrier((spread, partner_queries))
    own = lax.all_to_all(spread, SEQ, 0, 0, tiled=True)
    other = lax.ppermute(own, "core", swap)
    state = pl.pallas_call(
        attention_own_kernel,
        out_shape=[shape((2 * rows, HD), jnp.float32)] * 3,
        in_specs=[VMEM] * 2,
        out_specs=[VMEM] * 3,
        compiler_params=params,
        cost_estimate=cost,
        name="attention_own",
    )(own_queries, own)
    *state, sent = pl.pallas_call(
        attention_other_kernel,
        out_shape=[shape((2 * rows, HD), jnp.float32)] * 3 + [shape((rows, 3 * HD), jnp.bfloat16)],
        in_specs=[VMEM] * 7,
        out_specs=[VMEM] * 4,
        compiler_params=params,
        cost_estimate=cost,
        name="attention_other",
    )(own_queries, partner_queries, own, other, *state)
    got = lax.ppermute(sent, "xl", swap_x)
    heads = pl.pallas_call(
        merge_kernel,
        out_shape=shape((N_CHIP, rows, 2 * HD), jnp.bfloat16),
        in_specs=[VMEM] * 4,
        out_specs=VMEM,
        compiler_params=params,
        name="merge",
    )(*state, got)
    own_heads = lax.all_to_all(heads, ("z", "xh"), 0, 0, tiled=True)
    other_heads = lax.ppermute(own_heads, "core", swap)
    part = pl.pallas_call(
        project_own_kernel,
        out_shape=shape((rows, columns), jnp.float32),
        in_specs=[SMEM, VMEM, VMEM],
        out_specs=VMEM,
        compiler_params=params,
        cost_estimate=pl.CostEstimate(flops=2**28, bytes_accessed=2**22, transcendentals=0),
        name="project_own",
    )(mask, own_heads, out_weight)
    return pl.pallas_call(
        project_other_kernel,
        out_shape=shape((rows, columns), jnp.bfloat16),
        in_specs=[SMEM, VMEM, VMEM, VMEM],
        out_specs=VMEM,
        compiler_params=params,
        cost_estimate=pl.CostEstimate(flops=2**28, bytes_accessed=2**22, transcendentals=0),
        name="project_other",
    )(mask, other_heads, out_weight, part)


def solution(mesh):
    fine = Mesh(mesh.devices.reshape(SIZES), AXES)
    return jax.shard_map(
        per_device,
        mesh=fine,
        in_specs=(P(SEQ, FSDP), P(SEQ, None), P(SEQ, None), P(None, FSDP), P(None, FSDP)),
        out_specs=P(SEQ, FSDP),
        check_vma=False,
    )
```

time: 109 us -> 108 us (level)
  blocking collectives: 90.8 us -> 72.3 us
  starting transfers between devices: 8.31 us -> 22.4 us
  waiting for transfers between devices: 1.34 us -> 4.16 us
    all_to_all x1, blocking collectives: 35.4 us -> 21.9 us  [per_device(): own = lax.all_to_all(spread, SEQ, 0, 0, tiled=True)]
    ppermute x1, starting transfers between devices: 5.25 us -> 12.5 us  [per_device(): other = lax.ppermute(own, 'core', swap)]
    ppermute x0 -> x2, starting transfers between devices: none -> 6.59 us  [the longest x1 3.48 us: per_device(): got = lax.ppermute(sent, 'xl', swap_x)]
    all_to_all x1, blocking collectives: 55.4 us -> 50.4 us  [per_device(): own_heads = lax.all_to_all(heads, ('z', 'xh'), 0, 0, tiled=True)]
    ppermute x0 -> x2, waiting for transfers between devices: none -> 3.01 us  [the longest x1 2.68 us: per_device(): got = lax.ppermute(sent, 'xl', swap_x)]
    pallas_call x3 -> x4, Pallas kernels: 4.68 us -> 4.86 us  [the longest x1 1.87 us: per_device(): pl.pallas_call(attention_other_kernel, out_shape=[shape((2 * rows, HD), j...]
  transfers between devices with their start and end apart: 2 -> 4, of which waited for: 2 -> 3; matrix products, arithmetic and copies ran while one was open for 0% -> 0% of each run, Pallas kernels for 2% -> 3%
where the time goes in v2:
time: 108 us; the launch traced here: 107 us
  blocking collectives  72.3 us (67%)
  starting transfers between devices  22.4 us (21%)
  Pallas kernels  7.63 us (7%)
  waiting for transfers between devices  4.16 us (4%)
    all_to_all x1, blocking collectives, per_device(): own_heads = lax.all_to_all(heads, ('z', 'xh'), 0, 0, tiled=True)  50.4 us
    all_to_all x1, blocking collectives, per_device(): own = lax.all_to_all(spread, SEQ, 0, 0, tiled=True)  21.9 us
    ppermute x1, starting transfers between devices, per_device(): other = lax.ppermute(own, 'core', swap)  12.5 us
    ppermute x1, starting transfers between devices, per_device(): got = lax.ppermute(sent, 'xl', swap_x)  3.48 us
    ppermute x1, starting transfers between devices, per_device(): other_heads = lax.ppermute(own_heads, 'core', swap)  3.28 us
    ppermute x1, starting transfers between devices, per_device(): partner_queries = lax.ppermute(queries, 'xl', swap_x)  3.11 us
    ppermute x1, waiting for transfers between devices, per_device(): got = lax.ppermute(sent, 'xl', swap_x)  2.68 us
  transfers between devices with their start and end apart: 4, of which 3 were waited for; matrix products, arithmetic and copies ran while one was open for 0% of the time, Pallas kernels for 3%

profile of v2, /device:TPU:5, one launch (start us, length us, event | category | flops | bytes accessed | tf_op | source)
XLA Modules:
  0.0 107.4 jit_solution(8091212549796659967)
XLA Ops:
  0.0 3.1 %collective-permute-start = (bf16[128,256]{1,0:T(8,128)(2,1)}, bf16[128,256]{1,0:T(8,128)(2,1)S(1)}, u32[]{:S(2)}, u32[]{:S(2)}) collective-permute-start(bf16[128,256]{1,0:T(8,128)(2,1)} %queries_ref.1), channel_id=1, source_target_pairs={{0,32},{32,0},{64,96},{96,64},{1,33},{33,1},{65,97},{97,65},{2,34}... | collective-permute-start | bytes 196616 | tf_op jit(solution)/shard_map/ppermute | solution.py:187
  3.1 1.7 %spread_kv.1 = (bf16[128,256]{1,0:T(8,128)(2,1)}, bf16[32,32,256]{2,1,0:T(8,128)(2,1)}) custom-call(bf16[128,256]{1,0:T(8,128)(2,1)} %queries_ref.1, bf16[128,1024]{1,0:T(8,128)(2,1)} %keys_ref.1, bf16[128,1024]{1,0:T(8,128)(2,1)} %values_ref.1), custom_call_target="tpu_custom_call" | custom-call | tf_op jit(solution)/shard_map/spread_kv/pallas_call | solution.py:171
  4.9 0.3 collective-permute-done.partner_ref
  5.2 0.0 copy-start
  5.2 0.0 copy-start.1
  5.2 21.9 %all_to_all.10.kv_ref.own_ref = bf16[32,32,256]{2,1,0:T(8,128)(2,1)S(1)} all-to-all(bf16[32,32,256]{2,1,0:T(8,128)(2,1)} %get-tuple-element.19), channel_id=1, replica_groups=mesh['y'=8,'xl'=4,'z'=8,'xh'=2,'core'=2] {'y','xl'}, dimensions={0} | all-to-all | bytes 1048576 | tf_op jit(solution)/shard_map/all_to_all | solution.py:189
  27.1 12.5 %collective-permute-start.1 = (bf16[32,32,256]{2,1,0:T(8,128)(2,1)S(1)}, bf16[32,32,256]{2,1,0:T(8,128)(2,1)S(1)}, u32[]{:S(2)}, u32[]{:S(2)}) collective-permute-start(bf16[32,32,256]{2,1,0:T(8,128)(2,1)S(1)} %all_to_all.10.kv_ref.own_ref), channel_id=1, source_target_pairs={{0,1},{1,0},{2,3},{3,2},{4,5},{5,4},{6,7},{7,6},{8,9},{9,8},{10,11... | collective-permute-start | bytes 1572872 | tf_op jit(solution)/shard_map/ppermute | solution.py:190
  39.7 0.0 copy-start.2
  39.7 0.8 copy-done.2
  40.5 0.7 attention_own.1
  41.2 0.0 collective-permute-done.1.other_ref
  41.2 1.9 %attention_other.1 = (f32[256,128]{1,0:T(8,128)S(1)}, f32[256,128]{1,0:T(8,128)S(1)}, f32[256,128]{1,0:T(8,128)S(1)}, bf16[128,384]{1,0:T(8,128)(2,1)S(1)}) custom-call(bf16[128,256]{1,0:T(8,128)(2,1)S(1)} %copy-done.2, bf16[128,256]{1,0:T(8,128)(2,1)S(1)} %collective-permute-done.partner_ref, bf16[32,32,256]{2,1,0:T(8,128)(2,1)S(1)} %all_to_all.10.kv_ref.own_ref, ...), custom_call_target="tpu_custom_call" | custom-call | flops 536870912 | bytes 2097152 | tf_op jit(solution)/shard_map/attention_other/pallas_call | solution.py:200
  43.1 3.5 %collective-permute-start.2 = (bf16[128,384]{1,0:T(8,128)(2,1)S(1)}, bf16[128,384]{1,0:T(8,128)(2,1)S(1)}, u32[]{:S(2)}, u32[]{:S(2)}) collective-permute-start(bf16[128,384]{1,0:T(8,128)(2,1)S(1)} %get-tuple-element.26), channel_id=1, source_target_pairs={{0,32},{32,0},{64,96},{96,64},{1,33},{33,1},{65,97},{97,65},{2,34}... | collective-permute-start | bytes 294920 | tf_op jit(solution)/shard_map/ppermute | solution.py:209
  46.6 2.7 %collective-permute-done.2.got_ref = bf16[128,384]{1,0:T(8,128)(2,1)S(1)} collective-permute-done((bf16[128,384]{1,0:T(8,128)(2,1)S(1)}, bf16[128,384]{1,0:T(8,128)(2,1)S(1)}, u32[]{:S(2)}, u32[]{:S(2)}) %collective-permute-start.2) | collective-permute-done | bytes 98336 | tf_op jit(solution)/shard_map/ppermute | solution.py:209
  49.2 0.6 merge.1
  49.8 50.4 %all_to_all.11.heads_ref = bf16[16,128,256]{2,1,0:T(8,128)(2,1)S(1)} all-to-all(bf16[16,128,256]{2,1,0:T(8,128)(2,1)S(1)} %merge.1), channel_id=1, replica_groups=mesh['y'=8,'xl'=4,'z'=8,'xh'=2,'core'=2] {'z','xh'}, dimensions={0} | all-to-all | bytes 2097152 | tf_op jit(solution)/shard_map/all_to_all | solution.py:218
  100.2 3.3 %collective-permute-start.3 = (bf16[16,128,256]{2,1,0:T(8,128)(2,1)S(1)}, bf16[16,128,256]{2,1,0:T(8,128)(2,1)S(1)}, u32[]{:S(2)}, u32[]{:S(2)}) collective-permute-start(bf16[16,128,256]{2,1,0:T(8,128)(2,1)S(1)} %all_to_all.11.heads_ref), channel_id=1, source_target_pairs={{0,1},{1,0},{2,3},{3,2},{4,5},{5,4},{6,7},{7,6},{8,9},{9,8},{10,11... | collective-permute-start | bytes 3145736 | tf_op jit(solution)/shard_map/ppermute | solution.py:219
  103.5 0.0 copy-done
  103.5 0.0 copy-done.1
  103.5 1.1 %project_own.1.part_ref = f32[128,256]{1,0:T(8,128)S(1)} custom-call(s32[2,64]{1,0:T(2,128)S(1)} %bitcast.1, bf16[16,128,256]{2,1,0:T(8,128)(2,1)S(1)} %all_to_all.11.heads_ref, bf16[8192,256]{1,0:T(8,128)(2,1)S(1)} %copy-done), custom_call_target="tpu_custom_call" | custom-call | flops 268435456 | bytes 4194304 | tf_op jit(solution)/shard_map/project_own/pallas_call | solution.py:220
  104.6 1.1 %collective-permute-done.3.heads_ref = bf16[16,128,256]{2,1,0:T(8,128)(2,1)S(1)} collective-permute-done((bf16[16,128,256]{2,1,0:T(8,128)(2,1)S(1)}, bf16[16,128,256]{2,1,0:T(8,128)(2,1)S(1)}, u32[]{:S(2)}, u32[]{:S(2)}) %collective-permute-start.3) | collective-permute-done | bytes 1048608 | tf_op jit(solution)/shard_map/ppermute | solution.py:219
  105.8 1.7 %project_other.1 = bf16[128,256]{1,0:T(8,128)(2,1)} custom-call(s32[2,64]{1,0:T(2,128)S(1)} %bitcast.2, bf16[16,128,256]{2,1,0:T(8,128)(2,1)S(1)} %collective-permute-done.3.heads_ref, bf16[8192,256]{1,0:T(8,128)(2,1)S(1)} %copy-done, f32[128,256]{1,0:T(8,128)S(1)} %project_own.1.part_ref), custom_call_target="tpu_custom_call" | custom-call | flops 268435456 | bytes 4194304 | tf_op jit(solution)/shard_map/project_other/pallas_call | solution.py:229
Async XLA Ops:
  0.0 5.2 %collective-permute-start = (bf16[128,256]{1,0:T(8,128)(2,1)}, bf16[128,256]{1,0:T(8,128)(2,1)S(1)}, u32[]{:S(2)}, u32[]{:S(2)}) collective-permute-start(bf16[128,256]{1,0:T(8,128)(2,1)} %queries_ref.1), channel_id=1, source_target_pairs={{0,32},{32,0},{64,96},{96,64},{1,33},{33,1},{65,97},{97,65},{2,34}... | collective-permute-start | bytes 196616 | tf_op jit(solution)/shard_map/ppermute | solution.py:187
  5.2 98.3 %copy-start = (bf16[8192,256]{1,0:T(8,128)(2,1)S(1)}, bf16[8192,256]{1,0:T(8,128)(2,1)}, u32[]{:S(2)}) copy-start(bf16[8192,256]{1,0:T(8,128)(2,1)} %weight_ref.3) | copy-start | bytes 12582916
  5.2 98.3 %copy-start.1 = (s32[64,2]{0,1:T(2,128)S(1)}, s32[64,2]{0,1:T(2,128)}, u32[]{:S(2)}) copy-start(s32[64,2]{0,1:T(2,128)} %param.9) | copy-start | bytes 1540
  27.1 14.0 %collective-permute-start.1 = (bf16[32,32,256]{2,1,0:T(8,128)(2,1)S(1)}, bf16[32,32,256]{2,1,0:T(8,128)(2,1)S(1)}, u32[]{:S(2)}, u32[]{:S(2)}) collective-permute-start(bf16[32,32,256]{2,1,0:T(8,128)(2,1)S(1)} %all_to_all.10.kv_ref.own_ref), channel_id=1, source_target_pairs={{0,1},{1,0},{2,3},{3,2},{4,5},{5,4},{6,7},{7,6},{8,9},{9,8},{10,11... | collective-permute-start | bytes 1572872 | tf_op jit(solution)/shard_map/ppermute | solution.py:190
  39.7 0.8 copy-start.2
  43.1 6.2 %collective-permute-start.2 = (bf16[128,384]{1,0:T(8,128)(2,1)S(1)}, bf16[128,384]{1,0:T(8,128)(2,1)S(1)}, u32[]{:S(2)}, u32[]{:S(2)}) collective-permute-start(bf16[128,384]{1,0:T(8,128)(2,1)S(1)} %get-tuple-element.26), channel_id=1, source_target_pairs={{0,32},{32,0},{64,96},{96,64},{1,33},{33,1},{65,97},{97,65},{2,34}... | collective-permute-start | bytes 294920 | tf_op jit(solution)/shard_map/ppermute | solution.py:209
  100.2 5.5 %collective-permute-start.3 = (bf16[16,128,256]{2,1,0:T(8,128)(2,1)S(1)}, bf16[16,128,256]{2,1,0:T(8,128)(2,1)S(1)}, u32[]{:S(2)}, u32[]{:S(2)}) collective-permute-start(bf16[16,128,256]{2,1,0:T(8,128)(2,1)S(1)} %all_to_all.11.heads_ref), channel_id=1, source_target_pairs={{0,1},{1,0},{2,3},{3,2},{4,5},{5,4},{6,7},{7,6},{8,9},{9,8},{10,11... | collective-permute-start | bytes 3145736 | tf_op jit(solution)/shard_map/ppermute | solution.py:219

commit v3 on v1

v3 whole, which is shorter than its diff:
```python
import math

import jax
import jax.numpy as jnp
from jax import lax
from jax.experimental import pallas as pl
from jax.experimental.pallas import tpu as pltpu
from jax.sharding import Mesh
from jax.sharding import PartitionSpec as P

HD = 128
BLOCK = 128
SIZES = (8, 4, 8, 2, 2)
AXES = ("y", "xl", "z", "xh", "core")
SEQ = ("y", "xl")
FSDP = ("z", "xh", "core")
N_SEQ = 32
N_Z = 8
FACTOR = math.log2(math.e) / math.sqrt(HD)
LOWEST = -1e30
ANY = pl.BlockSpec(memory_space=pl.ANY)
VMEM = pl.BlockSpec(memory_space=pltpu.VMEM)
SMEM = pl.BlockSpec(memory_space=pltpu.SMEM)


def spread_kernel(keys_ref, values_ref, out_ref, piece, sems):
    half = piece.shape[0]
    column = pl.multiple_of(lax.axis_index("z") * HD, HD)
    row = pl.multiple_of(lax.axis_index("core") * half, half)
    place = (pl.ds(row, half), pl.ds(column, HD))
    copies = [
        pltpu.make_async_copy(keys_ref.at[place], piece.at[:, :HD], sems.at[0]),
        pltpu.make_async_copy(values_ref.at[place], piece.at[:, HD:], sems.at[1]),
    ]
    for copy in copies:
        copy.start()
    for copy in copies:
        copy.wait()
    block = piece[...]
    for i in range(N_SEQ):
        out_ref[i] = block


def attend(queries_ref, kv_ref, from_core, state):
    rows = queries_ref.shape[0]
    half = kv_ref.shape[1]
    width = N_SEQ * half
    start = (lax.axis_index("y") * SIZES[1] + lax.axis_index("xl")) * rows
    q = jnp.concatenate([queries_ref[:, :HD], queries_ref[:, HD:]], axis=0)
    query_pos = start + lax.broadcasted_iota(jnp.int32, (2 * rows, 1), 0) % rows
    column = lax.broadcasted_iota(jnp.int32, (1, width), 1)
    key_pos = column // half * rows + column % half + from_core * half
    key = kv_ref[:, :, :HD].reshape(width, HD)
    value = kv_ref[:, :, HD:].reshape(width, HD)
    score = lax.dot_general(q, key, (((1,), (1,)), ((), ())), preferred_element_type=jnp.float32)
    score = jnp.where(query_pos >= key_pos, score, jnp.float32(LOWEST))
    top = jnp.max(score, axis=1, keepdims=True)
    if state is not None:
        top = jnp.maximum(state[0], top)
    expo = jnp.exp2((score - top) * FACTOR)
    total = jnp.sum(expo, axis=1, keepdims=True)
    summed = jnp.dot(expo.astype(jnp.bfloat16), value, preferred_element_type=jnp.float32)
    if state is not None:
        fix = jnp.exp2((state[0] - top) * FACTOR)
        total = total + state[1] * fix
        summed = summed + state[2] * fix
    return top, total, summed


def finish(state):
    _, total, summed = state
    rows = total.shape[0] // 2
    normed = (summed / total).astype(jnp.bfloat16)
    return jnp.concatenate([normed[:rows], normed[rows:]], axis=1)


def attention_first_kernel(queries_ref, kv_ref, top_ref, total_ref, summed_ref):
    state = attend(queries_ref, kv_ref, lax.axis_index("core"), None)
    for ref, value in zip((top_ref, total_ref, summed_ref), state):
        ref[...] = jnp.broadcast_to(value, ref.shape)


def attention_second_kernel(queries_ref, kv_ref, top_ref, total_ref, summed_ref, out_ref):
    state = top_ref[:, :1], total_ref[:, :1], summed_ref[...]
    out_ref[...] = finish(attend(queries_ref, kv_ref, 1 - lax.axis_index("core"), state))


def attention_partner_kernel(queries_ref, own_ref, other_ref, heads_ref, out_ref):
    core = lax.axis_index("core")
    state = attend(queries_ref, own_ref, core, None)
    partner = finish(attend(queries_ref, other_ref, 1 - core, state))
    heads = jnp.concatenate([heads_ref[...], partner], axis=1)
    for i in range(N_Z):
        out_ref[i] = heads


def project(mask_ref, heads_ref, weight_ref, from_core):
    columns = weight_ref.shape[1]
    total = jnp.zeros((heads_ref.shape[1], columns), jnp.float32)
    xh = lax.axis_index("xh")
    for z in range(N_Z):
        rows = []
        for chip in (z * 2 + xh, z * 2 + 1 - xh):
            for i in range(2):
                block = (chip * 2 + from_core) * 2 + i
                at = pl.ds(pl.multiple_of(block * BLOCK, BLOCK), BLOCK)
                line = []
                for j in range(columns // BLOCK):
                    keep = mask_ref[j, block].astype(jnp.float32).astype(jnp.bfloat16)
                    line.append(weight_ref[at, j * BLOCK : (j + 1) * BLOCK] * keep)
                rows.append(jnp.concatenate(line, axis=1))
        pruned = jnp.concatenate(rows, axis=0)
        total += jnp.dot(heads_ref[z], pruned, preferred_element_type=jnp.float32)
    return total


def project_own_kernel(mask_ref, heads_ref, weight_ref, out_ref):
    out_ref[...] = project(mask_ref, heads_ref, weight_ref, lax.axis_index("core"))


def project_other_kernel(mask_ref, heads_ref, weight_ref, part_ref, out_ref):
    rest = project(mask_ref, heads_ref, weight_ref, 1 - lax.axis_index("core"))
    out_ref[...] = (part_ref[...] + rest).astype(out_ref.dtype)


def per_device(queries, keys, values, out_weight, block_mask):
    rows = queries.shape[0]
    columns = out_weight.shape[1]
    half = rows // 2
    mask = block_mask.T
    params = pltpu.CompilerParams(vmem_limit_bytes=32 * 2**20)
    shape = jax.ShapeDtypeStruct
    cost = pl.CostEstimate(flops=2**28, bytes_accessed=2**21, transcendentals=2**19)
    spread = pl.pallas_call(
        spread_kernel,
        out_shape=shape((N_SEQ, half, 2 * HD), jnp.bfloat16),
        in_specs=[ANY] * 2,
        out_specs=VMEM,
        scratch_shapes=[pltpu.VMEM((half, 2 * HD), jnp.bfloat16), pltpu.SemaphoreType.DMA((2,))],
        name="spread_kv",
    )(keys, values)
    swap = [(0, 1), (1, 0)]
    partner_queries = lax.ppermute(queries, "xh", swap)
    own = lax.all_to_all(spread, SEQ, 0, 0, tiled=True)
    other = lax.ppermute(own, "core", swap)
    state = pl.pallas_call(
        attention_first_kernel,
        out_shape=[shape((2 * rows, HD), jnp.float32)] * 3,
        in_specs=[VMEM] * 2,
        out_specs=[VMEM] * 3,
        compiler_params=params,
        cost_estimate=cost,
        name="attention_first",
    )(queries, own)
    own_heads = pl.pallas_call(
        attention_second_kernel,
        out_shape=shape((rows, 2 * HD), jnp.bfloat16),
        in_specs=[VMEM] * 5,
        out_specs=VMEM,
        compiler_params=params,
        cost_estimate=cost,
        name="attention_second",
    )(queries, other, *state)
    heads = pl.pallas_call(
        attention_partner_kernel,
        out_shape=shape((N_Z, rows, 4 * HD), jnp.bfloat16),
        in_specs=[VMEM] * 4,
        out_specs=VMEM,
        compiler_params=params,
        cost_estimate=cost,
        name="attention_partner",
    )(partner_queries, own, other, own_heads)
    own_heads = lax.all_to_all(heads, "z", 0, 0, tiled=True)
    other_heads = lax.ppermute(own_heads, "core", swap)
    part = pl.pallas_call(
        project_own_kernel,
        out_shape=shape((rows, columns), jnp.float32),
        in_specs=[SMEM, VMEM, VMEM],
        out_specs=VMEM,
        compiler_params=params,
        cost_estimate=pl.CostEstimate(flops=2**28, bytes_accessed=2**22, transcendentals=0),
        name="project_own",
    )(mask, own_heads, out_weight)
    return pl.pallas_call(
        project_other_kernel,
        out_shape=shape((rows, columns), jnp.bfloat16),
        in_specs=[SMEM, VMEM, VMEM, VMEM],
        out_specs=VMEM,
        compiler_params=params,
        cost_estimate=pl.CostEstimate(flops=2**28, bytes_accessed=2**22, transcendentals=0),
        name="project_other",
    )(mask, other_heads, out_weight, part)


def solution(mesh):
    fine = Mesh(mesh.devices.reshape(SIZES), AXES)
    return jax.shard_map(
        per_device,
        mesh=fine,
        in_specs=(P(SEQ, FSDP), P(SEQ, None), P(SEQ, None), P(None, FSDP), P(None, FSDP)),
        out_specs=P(SEQ, FSDP),
        check_vma=False,
    )
```

time: 109 us -> 110 us (level)
  the two profiles are of different devices: /device:TPU:5 before, /device:TPU:15 now
where the time goes in v3:
time: 110 us; the launch traced here: 109 us
  blocking collectives  82.3 us (75%)
  starting transfers between devices  12.8 us (12%)
  Pallas kernels  9.19 us (8%)
  waiting for transfers between devices  3.85 us (4%)
    all_to_all x1, blocking collectives, per_device(): own_heads = lax.all_to_all(heads, 'z', 0, 0, tiled=True)  44.6 us
    all_to_all x1, blocking collectives, per_device(): own = lax.all_to_all(spread, SEQ, 0, 0, tiled=True)  37.7 us
    ppermute x1, starting transfers between devices, per_device(): partner_queries = lax.ppermute(queries, 'xh', swap)  5.09 us
    ppermute x1, starting transfers between devices, per_device(): other_heads = lax.ppermute(own_heads, 'core', swap)  4.09 us
    ppermute x1, starting transfers between devices, per_device(): other = lax.ppermute(own, 'core', swap)  3.66 us
    ppermute x1, waiting for transfers between devices, per_device(): partner_queries = lax.ppermute(queries, 'xh', swap)  2.67 us
  transfers between devices with their start and end apart: 3, of which 2 were waited for; matrix products, arithmetic and copies ran while one was open for 0% of the time, Pallas kernels for 3%

profile of v3, /device:TPU:15, one launch (start us, length us, event | category | flops | bytes accessed | tf_op | source)
XLA Modules:
  0.0 109.2 jit_solution(15238193291384036558)
XLA Ops:
  0.0 1.8 %spread_kv.1 = bf16[32,64,256]{2,1,0:T(8,128)(2,1)} custom-call(bf16[128,1024]{1,0:T(8,128)(2,1)} %keys_ref.1, bf16[128,1024]{1,0:T(8,128)(2,1)} %values_ref.1), custom_call_target="tpu_custom_call" | custom-call | tf_op jit(solution)/shard_map/spread_kv/pallas_call | solution.py:134
  1.8 0.0 copy-start.2
  1.9 37.7 %all_to_all.10.kv_ref.own_ref = bf16[32,64,256]{2,1,0:T(8,128)(2,1)S(1)} all-to-all(bf16[32,64,256]{2,1,0:T(8,128)(2,1)} %spread_kv.1), channel_id=1, replica_groups=mesh['y'=8,'xl'=4,'z'=8,'xh'=2,'core'=2] {'y','xl'}, dimensions={0} | all-to-all | bytes 2097152 | tf_op jit(solution)/shard_map/all_to_all | solution.py:144
  39.6 0.0 copy-start
  39.6 3.7 %collective-permute-start.1 = (bf16[32,64,256]{2,1,0:T(8,128)(2,1)S(1)}, bf16[32,64,256]{2,1,0:T(8,128)(2,1)S(1)}, u32[]{:S(2)}, u32[]{:S(2)}) collective-permute-start(bf16[32,64,256]{2,1,0:T(8,128)(2,1)S(1)} %all_to_all.10.kv_ref.own_ref), channel_id=1, source_target_pairs={{0,1},{1,0},{2,3},{3,2},{4,5},{5,4},{6,7},{7,6},{8,9},{9,8},{10,11... | collective-permute-start | bytes 3145736 | tf_op jit(solution)/shard_map/ppermute | solution.py:145
  43.3 5.1 %collective-permute-start = (bf16[128,256]{1,0:T(8,128)(2,1)}, bf16[128,256]{1,0:T(8,128)(2,1)S(1)}, u32[]{:S(2)}, u32[]{:S(2)}) collective-permute-start(bf16[128,256]{1,0:T(8,128)(2,1)} %queries_ref.3), channel_id=1, source_target_pairs={{0,2},{2,0},{1,3},{3,1},{4,6},{6,4},{5,7},{7,5},{8,10},{10,8},{9,1... | collective-permute-start | bytes 196616 | tf_op jit(solution)/shard_map/ppermute | solution.py:143
  48.4 0.0 copy-start.1
  48.4 0.8 copy-done.1
  49.2 1.2 %attention_first.1 = (f32[256,128]{1,0:T(8,128)S(1)}, f32[256,128]{1,0:T(8,128)S(1)}, f32[256,128]{1,0:T(8,128)S(1)}) custom-call(bf16[128,256]{1,0:T(8,128)(2,1)S(1)} %copy-done.1, bf16[32,64,256]{2,1,0:T(8,128)(2,1)S(1)} %all_to_all.10.kv_ref.own_ref), custom_call_target="tpu_custom_call" | custom-call | flops 268435456 | bytes 2097152 | tf_op jit(solution)/shard_map/attention_first/pallas_call | solution.py:146
  50.4 0.0 collective-permute-done.1.kv_ref.other_ref
  50.4 1.3 %attention_second.1.heads_ref = bf16[128,256]{1,0:T(8,128)(2,1)S(1)} custom-call(bf16[128,256]{1,0:T(8,128)(2,1)S(1)} %copy-done.1, bf16[32,64,256]{2,1,0:T(8,128)(2,1)S(1)} %collective-permute-done.1.kv_ref.other_ref, f32[256,128]{1,0:T(8,128)S(1)} %get-tuple-element.8.top_ref, f32[256,128]{1,0:T(8,128)S(1)} %get-tuple-element.9.total_ref, ...), custom_call_target="tpu_custom_call" | custom-call | flops 268435456 | bytes 2097152 | tf_op jit(solution)/shard_map/attention_second/pallas_call | solution.py:155
  51.7 2.7 %collective-permute-done.queries_ref = bf16[128,256]{1,0:T(8,128)(2,1)S(1)} collective-permute-done((bf16[128,256]{1,0:T(8,128)(2,1)}, bf16[128,256]{1,0:T(8,128)(2,1)S(1)}, u32[]{:S(2)}, u32[]{:S(2)}) %collective-permute-start) | collective-permute-done | bytes 65568 | tf_op jit(solution)/shard_map/ppermute | solution.py:143
  54.4 2.1 %attention_partner.1 = bf16[8,128,512]{2,1,0:T(8,128)(2,1)S(1)} custom-call(bf16[128,256]{1,0:T(8,128)(2,1)S(1)} %collective-permute-done.queries_ref, bf16[32,64,256]{2,1,0:T(8,128)(2,1)S(1)} %all_to_all.10.kv_ref.own_ref, bf16[32,64,256]{2,1,0:T(8,128)(2,1)S(1)} %collective-permute-done.1.kv_ref.other_ref, bf16[128,256]{1,0:T(8,128)(2,1)S(1)} %attention_second.1.heads_ref), custom_call_target="tpu_custom_call" | custom-call | flops 268435456 | bytes 2097152 | tf_op jit(solution)/shard_map/attention_partner/pallas_call | solution.py:164
  56.5 44.6 %all_to_all.11.heads_ref = bf16[8,128,512]{2,1,0:T(8,128)(2,1)S(1)} all-to-all(bf16[8,128,512]{2,1,0:T(8,128)(2,1)S(1)} %attention_partner.1), channel_id=1, replica_groups=mesh['y'=8,'xl'=4,'z'=8,'xh'=2,'core'=2] {'z'}, dimensions={0} | all-to-all | bytes 2097152 | tf_op jit(solution)/shard_map/all_to_all | solution.py:173
  101.1 4.1 %collective-permute-start.2 = (bf16[8,128,512]{2,1,0:T(8,128)(2,1)S(1)}, bf16[8,128,512]{2,1,0:T(8,128)(2,1)S(1)}, u32[]{:S(2)}, u32[]{:S(2)}) collective-permute-start(bf16[8,128,512]{2,1,0:T(8,128)(2,1)S(1)} %all_to_all.11.heads_ref), channel_id=1, source_target_pairs={{0,1},{1,0},{2,3},{3,2},{4,5},{5,4},{6,7},{7,6},{8,9},{9,8},{10,11... | collective-permute-start | bytes 3145736 | tf_op jit(solution)/shard_map/ppermute | solution.py:174
  105.2 0.0 copy-done.2
  105.2 0.0 copy-done
  105.2 1.1 project_own.1.part_ref
  106.3 1.2 %collective-permute-done.2.heads_ref = bf16[8,128,512]{2,1,0:T(8,128)(2,1)S(1)} collective-permute-done((bf16[8,128,512]{2,1,0:T(8,128)(2,1)S(1)}, bf16[8,128,512]{2,1,0:T(8,128)(2,1)S(1)}, u32[]{:S(2)}, u32[]{:S(2)}) %collective-permute-start.2) | collective-permute-done | bytes 1048608 | tf_op jit(solution)/shard_map/ppermute | solution.py:174
  107.5 1.7 %project_other.1 = bf16[128,256]{1,0:T(8,128)(2,1)} custom-call(s32[2,64]{1,0:T(2,128)S(1)} %bitcast.2, bf16[8,128,512]{2,1,0:T(8,128)(2,1)S(1)} %collective-permute-done.2.heads_ref, bf16[8192,256]{1,0:T(8,128)(2,1)S(1)} %copy-done, f32[128,256]{1,0:T(8,128)S(1)} %project_own.1.part_ref), custom_call_target="tpu_custom_call" | custom-call | flops 268435456 | bytes 4194304 | tf_op jit(solution)/shard_map/project_other/pallas_call | solution.py:184
Async XLA Ops:
  1.8 103.4 %copy-start.2 = (s32[64,2]{0,1:T(2,128)S(1)}, s32[64,2]{0,1:T(2,128)}, u32[]{:S(2)}) copy-start(s32[64,2]{0,1:T(2,128)} %param.9) | copy-start | bytes 1540
  39.6 65.6 %copy-start = (bf16[8192,256]{1,0:T(8,128)(2,1)S(1)}, bf16[8192,256]{1,0:T(8,128)(2,1)}, u32[]{:S(2)}) copy-start(bf16[8192,256]{1,0:T(8,128)(2,1)} %weight_ref.3) | copy-start | bytes 12582916
  39.6 10.8 %collective-permute-start.1 = (bf16[32,64,256]{2,1,0:T(8,128)(2,1)S(1)}, bf16[32,64,256]{2,1,0:T(8,128)(2,1)S(1)}, u32[]{:S(2)}, u32[]{:S(2)}) collective-permute-start(bf16[32,64,256]{2,1,0:T(8,128)(2,1)S(1)} %all_to_all.10.kv_ref.own_ref), channel_id=1, source_target_pairs={{0,1},{1,0},{2,3},{3,2},{4,5},{5,4},{6,7},{7,6},{8,9},{9,8},{10,11... | collective-permute-start | bytes 3145736 | tf_op jit(solution)/shard_map/ppermute | solution.py:145
  43.3 11.1 %collective-permute-start = (bf16[128,256]{1,0:T(8,128)(2,1)}, bf16[128,256]{1,0:T(8,128)(2,1)S(1)}, u32[]{:S(2)}, u32[]{:S(2)}) collective-permute-start(bf16[128,256]{1,0:T(8,128)(2,1)} %queries_ref.3), channel_id=1, source_target_pairs={{0,2},{2,0},{1,3},{3,1},{4,6},{6,4},{5,7},{7,5},{8,10},{10,8},{9,1... | collective-permute-start | bytes 196616 | tf_op jit(solution)/shard_map/ppermute | solution.py:143
  48.4 0.9 copy-start.1
  101.1 6.4 %collective-permute-start.2 = (bf16[8,128,512]{2,1,0:T(8,128)(2,1)S(1)}, bf16[8,128,512]{2,1,0:T(8,128)(2,1)S(1)}, u32[]{:S(2)}, u32[]{:S(2)}) collective-permute-start(bf16[8,128,512]{2,1,0:T(8,128)(2,1)S(1)} %all_to_all.11.heads_ref), channel_id=1, source_target_pairs={{0,1},{1,0},{2,3},{3,2},{4,5},{5,4},{6,7},{7,6},{8,9},{9,8},{10,11... | collective-permute-start | bytes 3145736 | tf_op jit(solution)/shard_map/ppermute | solution.py:174

commit v4 on v3

--- a/solution.py
+++ b/solution.py
@@ -10,9 +10,11 @@
 
 HD = 128
 BLOCK = 128
-SIZES = (8, 4, 8, 2, 2)
-AXES = ("y", "xl", "z", "xh", "core")
-SEQ = ("y", "xl")
+SIZES = (4, 2, 2, 2, 8, 2, 2)
+AXES = ("y", "yp", "xl", "xp", "z", "xh", "core")
+SEQ = ("y", "yp", "xl", "xp")
+SQUARE = ("yp", "xp")
+N_SQUARE = 4
 FSDP = ("z", "xh", "core")
 N_SEQ = 32
 N_Z = 8
@@ -23,35 +25,47 @@
 SMEM = pl.BlockSpec(memory_space=pltpu.SMEM)
 
 
-def spread_kernel(keys_ref, values_ref, out_ref, piece, sems):
-    half = piece.shape[0]
+def spread_kernel(keys_ref, values_ref, out_ref, block, sems):
+    part = out_ref.shape[1]
     column = pl.multiple_of(lax.axis_index("z") * HD, HD)
-    row = pl.multiple_of(lax.axis_index("core") * half, half)
-    place = (pl.ds(row, half), pl.ds(column, HD))
+    core = lax.axis_index("core")
     copies = [
-        pltpu.make_async_copy(keys_ref.at[place], piece.at[:, :HD], sems.at[0]),
-        pltpu.make_async_copy(values_ref.at[place], piece.at[:, HD:], sems.at[1]),
+        pltpu.make_async_copy(
+            source.at[:, pl.ds(column, HD)], block.at[:, i * HD : (i + 1) * HD], sems.at[i]
+        )
+        for i, source in enumerate((keys_ref, values_ref))
     ]
     for copy in copies:
         copy.start()
     for copy in copies:
         copy.wait()
-    block = piece[...]
+    pieces = [
+        block[pl.ds(pl.multiple_of((place * 2 + core) * part, part), part), :]
+        for place in range(N_SQUARE)
+    ]
     for i in range(N_SEQ):
-        out_ref[i] = block
+        out_ref[i] = pieces[i // 4 % 2 * 2 + i % 2]
+
+
+def square_kernel(piece_ref, out_ref):
+    for i in range(N_SQUARE):
+        out_ref[i] = piece_ref[...]
 
 
 def attend(queries_ref, kv_ref, from_core, state):
     rows = queries_ref.shape[0]
-    half = kv_ref.shape[1]
-    width = N_SEQ * half
-    start = (lax.axis_index("y") * SIZES[1] + lax.axis_index("xl")) * rows
+    part = kv_ref.shape[2]
+    width = N_SQUARE * N_SEQ * part
+    seq = lax.axis_index("y") * 8 + lax.axis_index("yp") * 4 + lax.axis_index("xl") * 2
+    start = (seq + lax.axis_index("xp")) * rows
     q = jnp.concatenate([queries_ref[:, :HD], queries_ref[:, HD:]], axis=0)
     query_pos = start + lax.broadcasted_iota(jnp.int32, (2 * rows, 1), 0) % rows
     column = lax.broadcasted_iota(jnp.int32, (1, width), 1)
-    key_pos = column // half * rows + column % half + from_core * half
-    key = kv_ref[:, :, :HD].reshape(width, HD)
-    value = kv_ref[:, :, HD:].reshape(width, HD)
+    block = column // part
+    place = block // N_SEQ * 2 + from_core
+    key_pos = block % N_SEQ * rows + place * part + column % part
+    key = kv_ref[:, :, :, :HD].reshape(width, HD)
+    value = kv_ref[:, :, :, HD:].reshape(width, HD)
     score = lax.dot_general(q, key, (((1,), (1,)), ((), ())), preferred_element_type=jnp.float32)
     score = jnp.where(query_pos >= key_pos, score, jnp.float32(LOWEST))
     top = jnp.max(score, axis=1, keepdims=True)
@@ -74,22 +88,20 @@
     return jnp.concatenate([normed[:rows], normed[rows:]], axis=1)
 
 
-def attention_first_kernel(queries_ref, kv_ref, top_ref, total_ref, summed_ref):
-    state = attend(queries_ref, kv_ref, lax.axis_index("core"), None)
-    for ref, value in zip((top_ref, total_ref, summed_ref), state):
-        ref[...] = jnp.broadcast_to(value, ref.shape)
-
-
-def attention_second_kernel(queries_ref, kv_ref, top_ref, total_ref, summed_ref, out_ref):
-    state = top_ref[:, :1], total_ref[:, :1], summed_ref[...]
-    out_ref[...] = finish(attend(queries_ref, kv_ref, 1 - lax.axis_index("core"), state))
-
-
-def attention_partner_kernel(queries_ref, own_ref, other_ref, heads_ref, out_ref):
+def attention_first_kernel(queries_ref, partner_ref, kv_ref, *state_refs):
     core = lax.axis_index("core")
-    state = attend(queries_ref, own_ref, core, None)
-    partner = finish(attend(queries_ref, other_ref, 1 - core, state))
-    heads = jnp.concatenate([heads_ref[...], partner], axis=1)
+    for i, queries in enumerate((queries_ref, partner_ref)):
+        for ref, value in zip(state_refs, attend(queries, kv_ref, core, None)):
+            ref[i] = jnp.broadcast_to(value, ref.shape[1:])
+
+
+def attention_second_kernel(queries_ref, partner_ref, kv_ref, top_ref, total_ref, summed_ref, out_ref):
+    core = lax.axis_index("core")
+    heads = []
+    for i, queries in enumerate((queries_ref, partner_ref)):
+        state = top_ref[i, :, :1], total_ref[i, :, :1], summed_ref[i]
+        heads.append(finish(attend(queries, kv_ref, 1 - core, state)))
+    heads = jnp.concatenate(heads, axis=1)
     for i in range(N_Z):
         out_ref[i] = heads
 
@@ -126,50 +138,51 @@
 def per_device(queries, keys, values, out_weight, block_mask):
     rows = queries.shape[0]
     columns = out_weight.shape[1]
-    half = rows // 2
+    part = rows // (2 * N_SQUARE)
     mask = block_mask.T
     params = pltpu.CompilerParams(vmem_limit_bytes=32 * 2**20)
     shape = jax.ShapeDtypeStruct
-    cost = pl.CostEstimate(flops=2**28, bytes_accessed=2**21, transcendentals=2**19)
+    cost = pl.CostEstimate(flops=2**29, bytes_accessed=2**21, transcendentals=2**20)
+    swap = [(0, 1), (1, 0)]
+    partner_queries = lax.ppermute(queries, "xh", swap)
     spread = pl.pallas_call(
         spread_kernel,
-        out_shape=shape((N_SEQ, half, 2 * HD), jnp.bfloat16),
+        out_shape=shape((N_SEQ, part, 2 * HD), jnp.bfloat16),
         in_specs=[ANY] * 2,
         out_specs=VMEM,
-        scratch_shapes=[pltpu.VMEM((half, 2 * HD), jnp.bfloat16), pltpu.SemaphoreType.DMA((2,))],
+        scratch_shapes=[pltpu.VMEM((rows, 2 * HD), jnp.bfloat16), pltpu.SemaphoreType.DMA((2,))],
         name="spread_kv",
     )(keys, values)
-    swap = [(0, 1), (1, 0)]
-    partner_queries = lax.ppermute(queries, "xh", swap)
-    own = lax.all_to_all(spread, SEQ, 0, 0, tiled=True)
+    piece = lax.all_to_all(spread, SEQ, 0, 0, tiled=True)
+    piece, partner_queries = lax.optimization_barrier((piece, partner_queries))
+    square = pl.pallas_call(
+        square_kernel,
+        out_shape=shape((N_SQUARE, N_SEQ, part, 2 * HD), jnp.bfloat16),
+        in_specs=[VMEM],
+        out_specs=VMEM,
+        compiler_params=params,
+        name="square",
+    )(piece)
+    own = lax.all_to_all(square, SQUARE, 0, 0, tiled=True)
     other = lax.ppermute(own, "core", swap)
     state = pl.pallas_call(
         attention_first_kernel,
-        out_shape=[shape((2 * rows, HD), jnp.float32)] * 3,
-        in_specs=[VMEM] * 2,
+        out_shape=[shape((2, 2 * rows, HD), jnp.float32)] * 3,
+        in_specs=[VMEM] * 3,
         out_specs=[VMEM] * 3,
         compiler_params=params,
         cost_estimate=cost,
         name="attention_first",
-    )(queries, own)
-    own_heads = pl.pallas_call(
+    )(queries, partner_queries, own)
+    heads = pl.pallas_call(
         attention_second_kernel,
-        out_shape=shape((rows, 2 * HD), jnp.bfloat16),
-        in_specs=[VMEM] * 5,
+        out_shape=shape((N_Z, rows, 4 * HD), jnp.bfloat16),
+        in_specs=[VMEM] * 6,
         out_specs=VMEM,
         compiler_params=params,
         cost_estimate=cost,
         name="attention_second",
-    )(queries, other, *state)
-    heads = pl.pallas_call(
-        attention_partner_kernel,
-        out_shape=shape((N_Z, rows, 4 * HD), jnp.bfloat16),
-        in_specs=[VMEM] * 4,
-        out_specs=VMEM,
-        compiler_params=params,
-        cost_estimate=cost,
-        name="attention_partner",
-    )(partner_queries, own, other, own_heads)
+    )(queries, partner_queries, other, *state)
     own_heads = lax.all_to_all(heads, "z", 0, 0, tiled=True)
     other_heads = lax.ppermute(own_heads, "core", swap)
     part = pl.pallas_call(

time: 110 us -> 100 us (0.909)
  the two profiles are of different devices: /device:TPU:15 before, /device:TPU:1 now
where the time goes in v4:
time: 100 us
  blocking collectives  53.2 us (53%)
  starting transfers between devices  30.3 us (30%)
  Pallas kernels  8.69 us (9%)
  waiting for transfers between devices  7.84 us (8%)
    all_to_all x1, blocking collectives, per_device(): own_heads = lax.all_to_all(heads, 'z', 0, 0, tiled=True)  41.7 us
    all_to_all x1, blocking collectives, per_device(): own = lax.all_to_all(square, SQUARE, 0, 0, tiled=True)  11.5 us
    all_to_all x1, starting transfers between devices, per_device(): piece = lax.all_to_all(spread, SEQ, 0, 0, tiled=True)  11.3 us
    ppermute x1, starting transfers between devices, per_device(): other = lax.ppermute(own, 'core', swap)  11 us
    ppermute x1, waiting for transfers between devices, per_device(): partner_queries = lax.ppermute(queries, 'xh', swap)  4.81 us
    ppermute x1, starting transfers between devices, per_device(): partner_queries = lax.ppermute(queries, 'xh', swap)  4.42 us
    ppermute x1, starting transfers between devices, per_device(): other_heads = lax.ppermute(own_heads, 'core', swap)  3.63 us
    pallas_call x1, Pallas kernels, per_device(): pl.pallas_call(attention_second_kernel, out_shape=shape((N_Z, rows, 4 * H...  2.29 us
  transfers between devices with their start and end apart: 4, of which 4 were waited for; matrix products, arithmetic and copies ran while one was open for 0% of the time, Pallas kernels for 3%

profile of v4, /device:TPU:1, one launch (start us, length us, event | category | flops | bytes accessed | tf_op | source)
XLA Modules:
  0.0 100.1 jit_solution(743977208448503897)
XLA Ops:
  0.0 0.0 copy-start.1
  0.0 1.5 %spread_kv.1 = bf16[32,16,256]{2,1,0:T(8,128)(2,1)} custom-call(bf16[128,1024]{1,0:T(8,128)(2,1)} %keys_ref.1, bf16[128,1024]{1,0:T(8,128)(2,1)} %values_ref.1), custom_call_target="tpu_custom_call" | custom-call | tf_op jit(solution)/shard_map/spread_kv/pallas_call | solution.py:148
  1.5 11.3 %all-to-all-start = ((bf16[32,16,256]{2,1,0:T(8,128)(2,1)}), bf16[32,16,256]{2,1,0:T(8,128)(2,1)S(1)}, u32[]{:S(2)}, u32[]{:S(2)}) async-start(bf16[32,16,256]{2,1,0:T(8,128)(2,1)} %spread_kv.1), calls=%async_computation | async-start | bytes 524288 | tf_op jit(solution)/shard_map/all_to_all | solution.py:156
  12.8 4.4 %collective-permute-start = (bf16[128,256]{1,0:T(8,128)(2,1)}, bf16[128,256]{1,0:T(8,128)(2,1)S(1)}, u32[]{:S(2)}, u32[]{:S(2)}) collective-permute-start(bf16[128,256]{1,0:T(8,128)(2,1)} %queries_ref.3), channel_id=1, source_target_pairs={{0,2},{2,0},{1,3},{3,1},{4,6},{6,4},{5,7},{7,5},{8,10},{10,8},{9,1... | collective-permute-start | bytes 196616 | tf_op jit(solution)/shard_map/ppermute | solution.py:147
  17.3 4.8 %collective-permute-done.partner_ref = bf16[128,256]{1,0:T(8,128)(2,1)S(1)} collective-permute-done((bf16[128,256]{1,0:T(8,128)(2,1)}, bf16[128,256]{1,0:T(8,128)(2,1)S(1)}, u32[]{:S(2)}, u32[]{:S(2)}) %collective-permute-start) | collective-permute-done | bytes 65568 | tf_op jit(solution)/shard_map/ppermute | solution.py:147
  22.1 1.7 %all-to-all-done.piece_ref = bf16[32,16,256]{2,1,0:T(8,128)(2,1)S(1)} async-done(((bf16[32,16,256]{2,1,0:T(8,128)(2,1)}), bf16[32,16,256]{2,1,0:T(8,128)(2,1)S(1)}, u32[]{:S(2)}, u32[]{:S(2)}) %all-to-all-start) | async-done | bytes 262176 | tf_op jit(solution)/shard_map/all_to_all | solution.py:156
  23.7 0.1 square.1
  23.8 0.0 copy-start
  23.8 0.0 copy-start.2
  23.8 11.5 %all_to_all.15.kv_ref = bf16[4,32,16,256]{3,2,1,0:T(8,128)(2,1)S(1)} all-to-all(bf16[4,32,16,256]{3,2,1,0:T(8,128)(2,1)S(1)} %square.1), channel_id=1, replica_groups=mesh['y'=4,'yp'=2,'xl'=2,'xp'=2,'z'=8,'xh'=2,'core'=2] {'yp','xp'}, dimensions={0} | all-to-all | bytes 2097152 | tf_op jit(solution)/shard_map/all_to_all | solution.py:166
  35.3 11.0 %collective-permute-start.1 = (bf16[4,32,16,256]{3,2,1,0:T(8,128)(2,1)S(1)}, bf16[4,32,16,256]{3,2,1,0:T(8,128)(2,1)S(1)}, u32[]{:S(2)}, u32[]{:S(2)}) collective-permute-start(bf16[4,32,16,256]{3,2,1,0:T(8,128)(2,1)S(1)} %all_to_all.15.kv_ref), channel_id=1, source_target_pairs={{0,1},{1,0},{2,3},{3,2},{4,5},{5,4},{6,7},{7,6},{8,9},{9,8},{10,11... | collective-permute-start | bytes 3145736 | tf_op jit(solution)/shard_map/ppermute | solution.py:167
  46.3 0.0 copy-done.1
  46.3 2.0 %attention_first.1 = (f32[2,256,128]{2,1,0:T(8,128)S(1)}, f32[2,256,128]{2,1,0:T(8,128)S(1)}, f32[2,256,128]{2,1,0:T(8,128)S(1)}) custom-call(bf16[128,256]{1,0:T(8,128)(2,1)S(1)} %copy-done.1, bf16[128,256]{1,0:T(8,128)(2,1)S(1)} %collective-permute-done.partner_ref, bf16[4,32,16,256]{3,2,1,0:T(8,128)(2,1)S(1)} %all_to_all.15.kv_ref), custom_call_target="tpu_custom_call" | custom-call | flops 536870912 | bytes 2097152 | tf_op jit(solution)/shard_map/attention_first/pallas_call | solution.py:168
  48.3 0.2 collective-permute-done.1.kv_ref
  48.5 2.3 %attention_second.1 = bf16[8,128,512]{2,1,0:T(8,128)(2,1)S(1)} custom-call(bf16[128,256]{1,0:T(8,128)(2,1)S(1)} %copy-done.1, bf16[128,256]{1,0:T(8,128)(2,1)S(1)} %collective-permute-done.partner_ref, bf16[4,32,16,256]{3,2,1,0:T(8,128)(2,1)S(1)} %collective-permute-done.1.kv_ref, f32[2,256,128]{2,1,0:T(8,128)S(1)} %get-tuple-element.12.top_ref, ...), custom_call_target="tpu_custom_call" | custom-call | flops 536870912 | bytes 2097152 | tf_op jit(solution)/shard_map/attention_second/pallas_call | solution.py:177
  50.8 41.7 %all_to_all.16.heads_ref = bf16[8,128,512]{2,1,0:T(8,128)(2,1)S(1)} all-to-all(bf16[8,128,512]{2,1,0:T(8,128)(2,1)S(1)} %attention_second.1), channel_id=1, replica_groups=mesh['y'=4,'yp'=2,'xl'=2,'xp'=2,'z'=8,'xh'=2,'core'=2] {'z'}, dimensions={0} | all-to-all | bytes 2097152 | tf_op jit(solution)/shard_map/all_to_all | solution.py:186
  92.5 3.6 %collective-permute-start.2 = (bf16[8,128,512]{2,1,0:T(8,128)(2,1)S(1)}, bf16[8,128,512]{2,1,0:T(8,128)(2,1)S(1)}, u32[]{:S(2)}, u32[]{:S(2)}) collective-permute-start(bf16[8,128,512]{2,1,0:T(8,128)(2,1)S(1)} %all_to_all.16.heads_ref), channel_id=1, source_target_pairs={{0,1},{1,0},{2,3},{3,2},{4,5},{5,4},{6,7},{7,6},{8,9},{9,8},{10,11... | collective-permute-start | bytes 3145736 | tf_op jit(solution)/shard_map/ppermute | solution.py:187
  96.2 0.0 copy-done
  96.2 0.0 copy-done.2
  96.2 1.1 %project_own.1.part_ref = f32[128,256]{1,0:T(8,128)S(1)} custom-call(s32[2,64]{1,0:T(2,128)S(1)} %bitcast.1, bf16[8,128,512]{2,1,0:T(8,128)(2,1)S(1)} %all_to_all.16.heads_ref, bf16[8192,256]{1,0:T(8,128)(2,1)S(1)} %copy-done), custom_call_target="tpu_custom_call" | custom-call | flops 268435456 | bytes 4194304 | tf_op jit(solution)/shard_map/project_own/pallas_call | solution.py:188
  97.3 1.1 %collective-permute-done.2.heads_ref = bf16[8,128,512]{2,1,0:T(8,128)(2,1)S(1)} collective-permute-done((bf16[8,128,512]{2,1,0:T(8,128)(2,1)S(1)}, bf16[8,128,512]{2,1,0:T(8,128)(2,1)S(1)}, u32[]{:S(2)}, u32[]{:S(2)}) %collective-permute-start.2) | collective-permute-done | bytes 1048608 | tf_op jit(solution)/shard_map/ppermute | solution.py:187
  98.4 1.7 %project_other.1 = bf16[128,256]{1,0:T(8,128)(2,1)} custom-call(s32[2,64]{1,0:T(2,128)S(1)} %bitcast.2, bf16[8,128,512]{2,1,0:T(8,128)(2,1)S(1)} %collective-permute-done.2.heads_ref, bf16[8192,256]{1,0:T(8,128)(2,1)S(1)} %copy-done, f32[128,256]{1,0:T(8,128)S(1)} %project_own.1.part_ref), custom_call_target="tpu_custom_call" | custom-call | flops 268435456 | bytes 4194304 | tf_op jit(solution)/shard_map/project_other/pallas_call | solution.py:197
Async XLA Ops:
  0.0 46.3 %copy-start.1 = (bf16[128,256]{1,0:T(8,128)(2,1)S(1)}, bf16[128,256]{1,0:T(8,128)(2,1)}, u32[]{:S(2)}) copy-start(bf16[128,256]{1,0:T(8,128)(2,1)} %queries_ref.3) | copy-start | bytes 196612
  1.5 22.2 %all-to-all-start = ((bf16[32,16,256]{2,1,0:T(8,128)(2,1)}), bf16[32,16,256]{2,1,0:T(8,128)(2,1)S(1)}, u32[]{:S(2)}, u32[]{:S(2)}) async-start(bf16[32,16,256]{2,1,0:T(8,128)(2,1)} %spread_kv.1), calls=%async_computation | async-start | bytes 524288 | tf_op jit(solution)/shard_map/all_to_all | solution.py:156
  12.8 9.2 %collective-permute-start = (bf16[128,256]{1,0:T(8,128)(2,1)}, bf16[128,256]{1,0:T(8,128)(2,1)S(1)}, u32[]{:S(2)}, u32[]{:S(2)}) collective-permute-start(bf16[128,256]{1,0:T(8,128)(2,1)} %queries_ref.3), channel_id=1, source_target_pairs={{0,2},{2,0},{1,3},{3,1},{4,6},{6,4},{5,7},{7,5},{8,10},{10,8},{9,1... | collective-permute-start | bytes 196616 | tf_op jit(solution)/shard_map/ppermute | solution.py:147
  23.8 72.4 %copy-start = (bf16[8192,256]{1,0:T(8,128)(2,1)S(1)}, bf16[8192,256]{1,0:T(8,128)(2,1)}, u32[]{:S(2)}) copy-start(bf16[8192,256]{1,0:T(8,128)(2,1)} %weight_ref.3) | copy-start | bytes 12582916
  23.8 72.4 %copy-start.2 = (s32[64,2]{0,1:T(2,128)S(1)}, s32[64,2]{0,1:T(2,128)}, u32[]{:S(2)}) copy-start(s32[64,2]{0,1:T(2,128)} %param.9) | copy-start | bytes 1540
  35.3 13.2 %collective-permute-start.1 = (bf16[4,32,16,256]{3,2,1,0:T(8,128)(2,1)S(1)}, bf16[4,32,16,256]{3,2,1,0:T(8,128)(2,1)S(1)}, u32[]{:S(2)}, u32[]{:S(2)}) collective-permute-start(bf16[4,32,16,256]{3,2,1,0:T(8,128)(2,1)S(1)} %all_to_all.15.kv_ref), channel_id=1, source_target_pairs={{0,1},{1,0},{2,3},{3,2},{4,5},{5,4},{6,7},{7,6},{8,9},{9,8},{10,11... | collective-permute-start | bytes 3145736 | tf_op jit(solution)/shard_map/ppermute | solution.py:167
  92.5 5.9 %collective-permute-start.2 = (bf16[8,128,512]{2,1,0:T(8,128)(2,1)S(1)}, bf16[8,128,512]{2,1,0:T(8,128)(2,1)S(1)}, u32[]{:S(2)}, u32[]{:S(2)}) collective-permute-start(bf16[8,128,512]{2,1,0:T(8,128)(2,1)S(1)} %all_to_all.16.heads_ref), channel_id=1, source_target_pairs={{0,1},{1,0},{2,3},{3,2},{4,5},{5,4},{6,7},{7,6},{8,9},{9,8},{10,11... | collective-permute-start | bytes 3145736 | tf_op jit(solution)/shard_map/ppermute | solution.py:187

commit v5 on v4

--- a/solution.py
+++ b/solution.py
@@ -154,7 +154,6 @@
         name="spread_kv",
     )(keys, values)
     piece = lax.all_to_all(spread, SEQ, 0, 0, tiled=True)
-    piece, partner_queries = lax.optimization_barrier((piece, partner_queries))
     square = pl.pallas_call(
         square_kernel,
         out_shape=shape((N_SQUARE, N_SEQ, part, 2 * HD), jnp.bfloat16),
@@ -164,6 +163,7 @@
         name="square",
     )(piece)
     own = lax.all_to_all(square, SQUARE, 0, 0, tiled=True)
+    own, partner_queries = lax.optimization_barrier((own, partner_queries))
     other = lax.ppermute(own, "core", swap)
     state = pl.pallas_call(
         attention_first_kernel,

time: 100 us -> 106 us (1.060)
  blocking collectives: 53.2 us -> 66.6 us
  starting transfers between devices: 30.3 us -> 17.5 us
  waiting for transfers between devices: 7.84 us -> 11.3 us
    all_to_all x1, blocking collectives: 11.5 us -> 22.2 us  [per_device(): piece = lax.all_to_all(spread, SEQ, 0, 0, tiled=True)]
    all_to_all x1, starting transfers between devices: 11.3 us -> 3.65 us  [per_device(): own = lax.all_to_all(square, SQUARE, 0, 0, tiled=True)]
    ppermute x1, starting transfers between devices: 11 us -> 5.52 us  [per_device(): other = lax.ppermute(own, 'core', swap)]
    ppermute x1, waiting for transfers between devices: 4.81 us -> 9.88 us  [per_device(): partner_queries = lax.ppermute(queries, 'xh', swap)]
    all_to_all x1, blocking collectives: 41.7 us -> 44.4 us  [per_device(): own_heads = lax.all_to_all(heads, 'z', 0, 0, tiled=True)]
    all_to_all x1, waiting for transfers between devices: 1.66 us -> 0.01 us  [per_device(): own = lax.all_to_all(square, SQUARE, 0, 0, tiled=True)]
  transfers between devices with their start and end apart: 4 -> 4, of which waited for: 4 -> 3; matrix products, arithmetic and copies ran while one was open for 0% -> 0% of each run, Pallas kernels for 3% -> 3%
where the time goes in v5:
time: 106 us; the launch traced here: 105 us
  blocking collectives  66.6 us (63%)
  starting transfers between devices  17.5 us (17%)
  waiting for transfers between devices  11.3 us (11%)
  Pallas kernels  9.73 us (9%)
    all_to_all x1, blocking collectives, per_device(): own_heads = lax.all_to_all(heads, 'z', 0, 0, tiled=True)  44.4 us
    all_to_all x1, blocking collectives, per_device(): piece = lax.all_to_all(spread, SEQ, 0, 0, tiled=True)  22.2 us
    ppermute x1, waiting for transfers between devices, per_device(): partner_queries = lax.ppermute(queries, 'xh', swap)  9.88 us
    ppermute x1, starting transfers between devices, per_device(): other = lax.ppermute(own, 'core', swap)  5.52 us
    ppermute x1, starting transfers between devices, per_device(): partner_queries = lax.ppermute(queries, 'xh', swap)  4.72 us
    all_to_all x1, starting transfers between devices, per_device(): own = lax.all_to_all(square, SQUARE, 0, 0, tiled=True)  3.65 us
    ppermute x1, starting transfers between devices, per_device(): other_heads = lax.ppermute(own_heads, 'core', swap)  3.61 us
    pallas_call x1, Pallas kernels, per_device(): pl.pallas_call(attention_second_kernel, out_shape=shape((N_Z, rows, 4 * H...  2.35 us
  transfers between devices with their start and end apart: 4, of which 3 were waited for; matrix products, arithmetic and copies ran while one was open for 0% of the time, Pallas kernels for 3%

profile of v5, /device:TPU:1, one launch (start us, length us, event | category | flops | bytes accessed | tf_op | source)
XLA Modules:
  0.0 105.1 jit_solution(7849863528767378435)
XLA Ops:
  0.0 0.0 copy-start.1
  0.0 1.5 %spread_kv.1 = bf16[32,16,256]{2,1,0:T(8,128)(2,1)} custom-call(bf16[128,1024]{1,0:T(8,128)(2,1)} %keys_ref.1, bf16[128,1024]{1,0:T(8,128)(2,1)} %values_ref.1), custom_call_target="tpu_custom_call" | custom-call | tf_op jit(solution)/shard_map/spread_kv/pallas_call | solution.py:148
  1.5 22.2 %all_to_all.15.piece_ref = bf16[32,16,256]{2,1,0:T(8,128)(2,1)S(1)} all-to-all(bf16[32,16,256]{2,1,0:T(8,128)(2,1)} %spread_kv.1), channel_id=1, replica_groups=mesh['y'=4,'yp'=2,'xl'=2,'xp'=2,'z'=8,'xh'=2,'core'=2] {'y','yp','xl','xp'}, dimensions={0} | all-to-all | bytes 524288 | tf_op jit(solution)/shard_map/all_to_all | solution.py:156
  23.7 1.0 square.1
  24.8 0.0 copy-start.2
  24.8 3.6 %all-to-all-start.1 = ((bf16[4,32,16,256]{3,2,1,0:T(8,128)(2,1)}), bf16[4,32,16,256]{3,2,1,0:T(8,128)(2,1)S(1)}, u32[]{:S(2)}, u32[]{:S(2)}) async-start(bf16[4,32,16,256]{3,2,1,0:T(8,128)(2,1)} %square.1), calls=%async_computation.1 | async-start | bytes 2097152 | tf_op jit(solution)/shard_map/all_to_all | solution.py:165
  28.4 0.0 copy-done.1
  28.4 4.7 %collective-permute-start = (bf16[128,256]{1,0:T(8,128)(2,1)S(1)}, bf16[128,256]{1,0:T(8,128)(2,1)S(1)}, u32[]{:S(2)}, u32[]{:S(2)}) collective-permute-start(bf16[128,256]{1,0:T(8,128)(2,1)S(1)} %copy-done.1), channel_id=1, source_target_pairs={{0,2},{2,0},{1,3},{3,1},{4,6},{6,4},{5,7},{7,5},{8,10},{10,8},{9,1... | collective-permute-start | bytes 196616 | tf_op jit(solution)/shard_map/ppermute | solution.py:147
  33.1 9.9 %collective-permute-done.partner_ref = bf16[128,256]{1,0:T(8,128)(2,1)S(1)} collective-permute-done((bf16[128,256]{1,0:T(8,128)(2,1)S(1)}, bf16[128,256]{1,0:T(8,128)(2,1)S(1)}, u32[]{:S(2)}, u32[]{:S(2)}) %collective-permute-start) | collective-permute-done | bytes 65568 | tf_op jit(solution)/shard_map/ppermute | solution.py:147
  43.0 0.0 all-to-all-done.1.kv_ref
  43.0 0.0 copy-start
  43.0 5.5 %collective-permute-start.1 = (bf16[4,32,16,256]{3,2,1,0:T(8,128)(2,1)S(1)}, bf16[4,32,16,256]{3,2,1,0:T(8,128)(2,1)S(1)}, u32[]{:S(2)}, u32[]{:S(2)}) collective-permute-start(bf16[4,32,16,256]{3,2,1,0:T(8,128)(2,1)S(1)} %all-to-all-done.1.kv_ref), channel_id=1, source_target_pairs={{0,1},{1,0},{2,3},{3,2},{4,5},{5,4},{6,7},{7,6},{8,9},{9,8},{10,11... | collective-permute-start | bytes 3145736 | tf_op jit(solution)/shard_map/ppermute | solution.py:167
  48.6 2.1 %attention_first.1 = (f32[2,256,128]{2,1,0:T(8,128)S(1)}, f32[2,256,128]{2,1,0:T(8,128)S(1)}, f32[2,256,128]{2,1,0:T(8,128)S(1)}) custom-call(bf16[128,256]{1,0:T(8,128)(2,1)S(1)} %copy-done.1, bf16[128,256]{1,0:T(8,128)(2,1)S(1)} %collective-permute-done.partner_ref, bf16[4,32,16,256]{3,2,1,0:T(8,128)(2,1)S(1)} %all-to-all-done.1.kv_ref), custom_call_target="tpu_custom_call" | custom-call | flops 536870912 | bytes 2097152 | tf_op jit(solution)/shard_map/attention_first/pallas_call | solution.py:168
  50.6 0.2 collective-permute-done.1.kv_ref
  50.8 2.4 %attention_second.1 = bf16[8,128,512]{2,1,0:T(8,128)(2,1)S(1)} custom-call(bf16[128,256]{1,0:T(8,128)(2,1)S(1)} %copy-done.1, bf16[128,256]{1,0:T(8,128)(2,1)S(1)} %collective-permute-done.partner_ref, bf16[4,32,16,256]{3,2,1,0:T(8,128)(2,1)S(1)} %collective-permute-done.1.kv_ref, f32[2,256,128]{2,1,0:T(8,128)S(1)} %get-tuple-element.12.top_ref, ...), custom_call_target="tpu_custom_call" | custom-call | flops 536870912 | bytes 2097152 | tf_op jit(solution)/shard_map/attention_second/pallas_call | solution.py:177
  53.2 44.4 %all_to_all.16.heads_ref = bf16[8,128,512]{2,1,0:T(8,128)(2,1)S(1)} all-to-all(bf16[8,128,512]{2,1,0:T(8,128)(2,1)S(1)} %attention_second.1), channel_id=1, replica_groups=mesh['y'=4,'yp'=2,'xl'=2,'xp'=2,'z'=8,'xh'=2,'core'=2] {'z'}, dimensions={0} | all-to-all | bytes 2097152 | tf_op jit(solution)/shard_map/all_to_all | solution.py:186
  97.6 3.6 %collective-permute-start.2 = (bf16[8,128,512]{2,1,0:T(8,128)(2,1)S(1)}, bf16[8,128,512]{2,1,0:T(8,128)(2,1)S(1)}, u32[]{:S(2)}, u32[]{:S(2)}) collective-permute-start(bf16[8,128,512]{2,1,0:T(8,128)(2,1)S(1)} %all_to_all.16.heads_ref), channel_id=1, source_target_pairs={{0,1},{1,0},{2,3},{3,2},{4,5},{5,4},{6,7},{7,6},{8,9},{9,8},{10,11... | collective-permute-start | bytes 3145736 | tf_op jit(solution)/shard_map/ppermute | solution.py:187
  101.2 0.0 copy-done.2
  101.2 0.0 copy-done
  101.2 1.1 %project_own.1.part_ref = f32[128,256]{1,0:T(8,128)S(1)} custom-call(s32[2,64]{1,0:T(2,128)S(1)} %bitcast.1, bf16[8,128,512]{2,1,0:T(8,128)(2,1)S(1)} %all_to_all.16.heads_ref, bf16[8192,256]{1,0:T(8,128)(2,1)S(1)} %copy-done), custom_call_target="tpu_custom_call" | custom-call | flops 268435456 | bytes 4194304 | tf_op jit(solution)/shard_map/project_own/pallas_call | solution.py:188
  102.3 1.2 %collective-permute-done.2.heads_ref = bf16[8,128,512]{2,1,0:T(8,128)(2,1)S(1)} collective-permute-done((bf16[8,128,512]{2,1,0:T(8,128)(2,1)S(1)}, bf16[8,128,512]{2,1,0:T(8,128)(2,1)S(1)}, u32[]{:S(2)}, u32[]{:S(2)}) %collective-permute-start.2) | collective-permute-done | bytes 1048608 | tf_op jit(solution)/shard_map/ppermute | solution.py:187
  103.5 1.7 %project_other.1 = bf16[128,256]{1,0:T(8,128)(2,1)} custom-call(s32[2,64]{1,0:T(2,128)S(1)} %bitcast.2, bf16[8,128,512]{2,1,0:T(8,128)(2,1)S(1)} %collective-permute-done.2.heads_ref, bf16[8192,256]{1,0:T(8,128)(2,1)S(1)} %copy-done, f32[128,256]{1,0:T(8,128)S(1)} %project_own.1.part_ref), custom_call_target="tpu_custom_call" | custom-call | flops 268435456 | bytes 4194304 | tf_op jit(solution)/shard_map/project_other/pallas_call | solution.py:197
Async XLA Ops:
  0.0 28.4 %copy-start.1 = (bf16[128,256]{1,0:T(8,128)(2,1)S(1)}, bf16[128,256]{1,0:T(8,128)(2,1)}, u32[]{:S(2)}) copy-start(bf16[128,256]{1,0:T(8,128)(2,1)} %queries_ref.3) | copy-start | bytes 196612
  24.8 76.4 %copy-start.2 = (s32[64,2]{0,1:T(2,128)S(1)}, s32[64,2]{0,1:T(2,128)}, u32[]{:S(2)}) copy-start(s32[64,2]{0,1:T(2,128)} %param.9) | copy-start | bytes 1540
  24.8 18.3 %all-to-all-start.1 = ((bf16[4,32,16,256]{3,2,1,0:T(8,128)(2,1)}), bf16[4,32,16,256]{3,2,1,0:T(8,128)(2,1)S(1)}, u32[]{:S(2)}, u32[]{:S(2)}) async-start(bf16[4,32,16,256]{3,2,1,0:T(8,128)(2,1)} %square.1), calls=%async_computation.1 | async-start | bytes 2097152 | tf_op jit(solution)/shard_map/all_to_all | solution.py:165
  28.4 14.6 %collective-permute-start = (bf16[128,256]{1,0:T(8,128)(2,1)S(1)}, bf16[128,256]{1,0:T(8,128)(2,1)S(1)}, u32[]{:S(2)}, u32[]{:S(2)}) collective-permute-start(bf16[128,256]{1,0:T(8,128)(2,1)S(1)} %copy-done.1), channel_id=1, source_target_pairs={{0,2},{2,0},{1,3},{3,1},{4,6},{6,4},{5,7},{7,5},{8,10},{10,8},{9,1... | collective-permute-start | bytes 196616 | tf_op jit(solution)/shard_map/ppermute | solution.py:147
  43.0 58.2 %copy-start = (bf16[8192,256]{1,0:T(8,128)(2,1)S(1)}, bf16[8192,256]{1,0:T(8,128)(2,1)}, u32[]{:S(2)}) copy-start(bf16[8192,256]{1,0:T(8,128)(2,1)} %weight_ref.3) | copy-start | bytes 12582916
  43.0 7.8 %collective-permute-start.1 = (bf16[4,32,16,256]{3,2,1,0:T(8,128)(2,1)S(1)}, bf16[4,32,16,256]{3,2,1,0:T(8,128)(2,1)S(1)}, u32[]{:S(2)}, u32[]{:S(2)}) collective-permute-start(bf16[4,32,16,256]{3,2,1,0:T(8,128)(2,1)S(1)} %all-to-all-done.1.kv_ref), channel_id=1, source_target_pairs={{0,1},{1,0},{2,3},{3,2},{4,5},{5,4},{6,7},{7,6},{8,9},{9,8},{10,11... | collective-permute-start | bytes 3145736 | tf_op jit(solution)/shard_map/ppermute | solution.py:167
  97.6 5.9 %collective-permute-start.2 = (bf16[8,128,512]{2,1,0:T(8,128)(2,1)S(1)}, bf16[8,128,512]{2,1,0:T(8,128)(2,1)S(1)}, u32[]{:S(2)}, u32[]{:S(2)}) collective-permute-start(bf16[8,128,512]{2,1,0:T(8,128)(2,1)S(1)} %all_to_all.16.heads_ref), channel_id=1, source_target_pairs={{0,1},{1,0},{2,3},{3,2},{4,5},{5,4},{6,7},{7,6},{8,9},{9,8},{10,11... | collective-permute-start | bytes 3145736 | tf_op jit(solution)/shard_map/ppermute | solution.py:187

commit v6 on v4

--- a/solution.py
+++ b/solution.py
@@ -1,3 +1,4 @@
+import functools
 import math
 
 import jax
@@ -95,44 +96,40 @@
             ref[i] = jnp.broadcast_to(value, ref.shape[1:])
 
 
-def attention_second_kernel(queries_ref, partner_ref, kv_ref, top_ref, total_ref, summed_ref, out_ref):
-    core = lax.axis_index("core")
-    heads = []
-    for i, queries in enumerate((queries_ref, partner_ref)):
-        state = top_ref[i, :, :1], total_ref[i, :, :1], summed_ref[i]
-        heads.append(finish(attend(queries, kv_ref, 1 - core, state)))
-    heads = jnp.concatenate(heads, axis=1)
+def attention_second_kernel(which, queries_ref, kv_ref, top_ref, total_ref, summed_ref, out_ref):
+    state = top_ref[which, :, :1], total_ref[which, :, :1], summed_ref[which]
+    heads = finish(attend(queries_ref, kv_ref, 1 - lax.axis_index("core"), state))
     for i in range(N_Z):
         out_ref[i] = heads
 
 
-def project(mask_ref, heads_ref, weight_ref, from_core):
+def project(mask_ref, heads_ref, weight_ref, from_chip, from_core):
     columns = weight_ref.shape[1]
     total = jnp.zeros((heads_ref.shape[1], columns), jnp.float32)
-    xh = lax.axis_index("xh")
     for z in range(N_Z):
         rows = []
-        for chip in (z * 2 + xh, z * 2 + 1 - xh):
-            for i in range(2):
-                block = (chip * 2 + from_core) * 2 + i
-                at = pl.ds(pl.multiple_of(block * BLOCK, BLOCK), BLOCK)
-                line = []
-                for j in range(columns // BLOCK):
-                    keep = mask_ref[j, block].astype(jnp.float32).astype(jnp.bfloat16)
-                    line.append(weight_ref[at, j * BLOCK : (j + 1) * BLOCK] * keep)
-                rows.append(jnp.concatenate(line, axis=1))
+        for i in range(2):
+            block = ((z * 2 + from_chip) * 2 + from_core) * 2 + i
+            at = pl.ds(pl.multiple_of(block * BLOCK, BLOCK), BLOCK)
+            line = []
+            for j in range(columns // BLOCK):
+                keep = mask_ref[j, block].astype(jnp.float32).astype(jnp.bfloat16)
+                line.append(weight_ref[at, j * BLOCK : (j + 1) * BLOCK] * keep)
+            rows.append(jnp.concatenate(line, axis=1))
         pruned = jnp.concatenate(rows, axis=0)
         total += jnp.dot(heads_ref[z], pruned, preferred_element_type=jnp.float32)
     return total
 
 
-def project_own_kernel(mask_ref, heads_ref, weight_ref, out_ref):
-    out_ref[...] = project(mask_ref, heads_ref, weight_ref, lax.axis_index("core"))
-
-
-def project_other_kernel(mask_ref, heads_ref, weight_ref, part_ref, out_ref):
-    rest = project(mask_ref, heads_ref, weight_ref, 1 - lax.axis_index("core"))
-    out_ref[...] = (part_ref[...] + rest).astype(out_ref.dtype)
+def project_kernel(of_partner, of_sibling, mask_ref, heads_ref, weight_ref, *refs):
+    xh, core = lax.axis_index("xh"), lax.axis_index("core")
+    part = project(
+        mask_ref, heads_ref, weight_ref, 1 - xh if of_partner else xh, 1 - core if of_sibling else core
+    )
+    out_ref = refs[-1]
+    for before_ref in refs[:-1]:
+        part = part + before_ref[...]
+    out_ref[...] = part.astype(out_ref.dtype)
 
 
 def per_device(queries, keys, values, out_weight, block_mask):
@@ -174,35 +171,35 @@
         cost_estimate=cost,
         name="attention_first",
     )(queries, partner_queries, own)
-    heads = pl.pallas_call(
-        attention_second_kernel,
-        out_shape=shape((N_Z, rows, 4 * HD), jnp.bfloat16),
-        in_specs=[VMEM] * 6,
-        out_specs=VMEM,
-        compiler_params=params,
-        cost_estimate=cost,
-        name="attention_second",
-    )(queries, partner_queries, other, *state)
-    own_heads = lax.all_to_all(heads, "z", 0, 0, tiled=True)
-    other_heads = lax.ppermute(own_heads, "core", swap)
-    part = pl.pallas_call(
-        project_own_kernel,
-        out_shape=shape((rows, columns), jnp.float32),
-        in_specs=[SMEM, VMEM, VMEM],
-        out_specs=VMEM,
-        compiler_params=params,
-        cost_estimate=pl.CostEstimate(flops=2**28, bytes_accessed=2**22, transcendentals=0),
-        name="project_own",
-    )(mask, own_heads, out_weight)
-    return pl.pallas_call(
-        project_other_kernel,
-        out_shape=shape((rows, columns), jnp.bfloat16),
-        in_specs=[SMEM, VMEM, VMEM, VMEM],
-        out_specs=VMEM,
-        compiler_params=params,
-        cost_estimate=pl.CostEstimate(flops=2**28, bytes_accessed=2**22, transcendentals=0),
-        name="project_other",
-    )(mask, other_heads, out_weight, part)
+    parts = []
+    for which, (name, its_queries) in enumerate((("own", queries), ("partner", partner_queries))):
+        heads = pl.pallas_call(
+            functools.partial(attention_second_kernel, which),
+            out_shape=shape((N_Z, rows, 2 * HD), jnp.bfloat16),
+            in_specs=[VMEM] * 5,
+            out_specs=VMEM,
+            compiler_params=params,
+            cost_estimate=cost,
+            name="attention_second_" + name,
+        )(its_queries, other, *state)
+        along_z = lax.all_to_all(heads, "z", 0, 0, tiled=True)
+        sibling = lax.ppermute(along_z, "core", swap)
+        for of_sibling, got in enumerate((along_z, sibling)):
+            last = which and of_sibling
+            parts = [
+                pl.pallas_call(
+                    functools.partial(project_kernel, which, of_sibling),
+                    out_shape=shape((rows, columns), jnp.bfloat16 if last else jnp.float32),
+                    in_specs=[SMEM] + [VMEM] * (2 + len(parts)),
+                    out_specs=VMEM,
+                    compiler_params=params,
+                    cost_estimate=pl.CostEstimate(
+                        flops=2**27, bytes_accessed=2**21, transcendentals=0
+                    ),
+                    name="project_" + name + "_" + ("sibling" if of_sibling else "self"),
+                )(mask, got, out_weight, *parts)
+            ]
+    return parts[0]
 
 
 def solution(mesh):

time: 100 us -> 115 us (1.15); the launches traced: 100 us -> 114 us
  blocking collectives: 53.2 us -> 11.2 us
  waiting for transfers between devices: 7.84 us -> 38 us
  starting transfers between devices: 30.3 us -> 49 us
  local copies, waits for them, and re-layouts: 0.02 us -> 3.46 us
  Pallas kernels: 8.69 us -> 12.1 us
    all_to_all x1 -> x0, blocking collectives: 41.7 us -> none  [per_device(): own_heads = lax.all_to_all(heads, 'z', 0, 0, tiled=True)]
    all_to_all x0 -> x2, waiting for transfers between devices: none -> 31.3 us  [per_device(): along_z = lax.all_to_all(heads, 'z', 0, 0, tiled=True)]
    all_to_all x0 -> x2, starting transfers between devices: none -> 17.4 us  [per_device(): along_z = lax.all_to_all(heads, 'z', 0, 0, tiled=True)]
    unnamed x6 -> x8, local copies, waits for them, and re-layouts: 0.02 us -> 3.46 us
    pallas_call x3 -> x6, Pallas kernels: 5.07 us -> 8.42 us  [the longest x4 4.26 us: per_device(): pl.pallas_call(functools.partial(project_kernel, which, of_sibling), out_...]
    ppermute x1 -> x2, starting transfers between devices: 3.63 us -> 4.79 us  [per_device(): sibling = lax.ppermute(along_z, 'core', swap)]
  transfers between devices with their start and end apart: 4 -> 7, of which waited for: 4 -> 5; matrix products, arithmetic and copies ran while one was open for 0% -> 0% of each run, Pallas kernels for 3% -> 6%
where the time goes in v6:
time: 115 us; the launch traced here: 114 us
  starting transfers between devices  49 us (43%)
  waiting for transfers between devices  38 us (33%)
  Pallas kernels  12.1 us (11%)
  blocking collectives  11.2 us (10%)
  local copies, waits for them, and re-layouts  3.46 us (3%)
    all_to_all x2, waiting for transfers between devices, per_device(): along_z = lax.all_to_all(heads, 'z', 0, 0, tiled=True)  31.3 us
    all_to_all x2, starting transfers between devices, per_device(): along_z = lax.all_to_all(heads, 'z', 0, 0, tiled=True)  17.4 us
    all_to_all x1, starting transfers between devices, per_device(): piece = lax.all_to_all(spread, SEQ, 0, 0, tiled=True)  11.3 us
    all_to_all x1, blocking collectives, per_device(): own = lax.all_to_all(square, SQUARE, 0, 0, tiled=True)  11.2 us
    ppermute x1, starting transfers between devices, per_device(): other = lax.ppermute(own, 'core', swap)  11.1 us
    ppermute x1, waiting for transfers between devices, per_device(): partner_queries = lax.ppermute(queries, 'xh', swap)  4.81 us
    ppermute x2, starting transfers between devices, per_device(): sibling = lax.ppermute(along_z, 'core', swap)  4.79 us
    ppermute x1, starting transfers between devices, per_device(): partner_queries = lax.ppermute(queries, 'xh', swap)  4.42 us
  transfers between devices with their start and end apart: 7, of which 5 were waited for; matrix products, arithmetic and copies ran while one was open for 0% of the time, Pallas kernels for 6%

profile of v6, /device:TPU:1, one launch (start us, length us, event | category | flops | bytes accessed | tf_op | source)
XLA Modules:
  0.0 113.9 jit_solution(14078504911340033433)
XLA Ops:
  0.0 0.0 copy-start.2
  0.0 1.5 %spread_kv.1 = bf16[32,16,256]{2,1,0:T(8,128)(2,1)} custom-call(bf16[128,1024]{1,0:T(8,128)(2,1)} %keys_ref.1, bf16[128,1024]{1,0:T(8,128)(2,1)} %values_ref.1), custom_call_target="tpu_custom_call" | custom-call | tf_op jit(solution)/shard_map/spread_kv/pallas_call | solution.py:145
  1.6 11.3 %all-to-all-start = ((bf16[32,16,256]{2,1,0:T(8,128)(2,1)}), bf16[32,16,256]{2,1,0:T(8,128)(2,1)S(1)}, u32[]{:S(2)}, u32[]{:S(2)}) async-start(bf16[32,16,256]{2,1,0:T(8,128)(2,1)} %spread_kv.1), calls=%async_computation | async-start | bytes 524288 | tf_op jit(solution)/shard_map/all_to_all | solution.py:153
  12.9 4.4 %collective-permute-start = (bf16[128,256]{1,0:T(8,128)(2,1)}, bf16[128,256]{1,0:T(8,128)(2,1)S(1)}, u32[]{:S(2)}, u32[]{:S(2)}) collective-permute-start(bf16[128,256]{1,0:T(8,128)(2,1)} %queries_ref.3), channel_id=1, source_target_pairs={{0,2},{2,0},{1,3},{3,1},{4,6},{6,4},{5,7},{7,5},{8,10},{10,8},{9,1... | collective-permute-start | bytes 196616 | tf_op jit(solution)/shard_map/ppermute | solution.py:144
  17.3 4.8 %collective-permute-done.partner_ref.queries_ref = bf16[128,256]{1,0:T(8,128)(2,1)S(1)} collective-permute-done((bf16[128,256]{1,0:T(8,128)(2,1)}, bf16[128,256]{1,0:T(8,128)(2,1)S(1)}, u32[]{:S(2)}, u32[]{:S(2)}) %collective-permute-start) | collective-permute-done | bytes 65568 | tf_op jit(solution)/shard_map/ppermute | solution.py:144
  22.1 1.7 %all-to-all-done.piece_ref = bf16[32,16,256]{2,1,0:T(8,128)(2,1)S(1)} async-done(((bf16[32,16,256]{2,1,0:T(8,128)(2,1)}), bf16[32,16,256]{2,1,0:T(8,128)(2,1)S(1)}, u32[]{:S(2)}, u32[]{:S(2)}) %all-to-all-start) | async-done | bytes 262176 | tf_op jit(solution)/shard_map/all_to_all | solution.py:153
  23.7 0.1 square.1
  23.8 11.2 %all_to_all.20.kv_ref = bf16[4,32,16,256]{3,2,1,0:T(8,128)(2,1)S(1)} all-to-all(bf16[4,32,16,256]{3,2,1,0:T(8,128)(2,1)S(1)} %square.1), channel_id=1, replica_groups=mesh['y'=4,'yp'=2,'xl'=2,'xp'=2,'z'=8,'xh'=2,'core'=2] {'yp','xp'}, dimensions={0} | all-to-all | bytes 2097152 | tf_op jit(solution)/shard_map/all_to_all | solution.py:163
  35.0 0.0 copy-start.3
  35.0 11.1 %collective-permute-start.1 = (bf16[4,32,16,256]{3,2,1,0:T(8,128)(2,1)S(1)}, bf16[4,32,16,256]{3,2,1,0:T(8,128)(2,1)S(1)}, u32[]{:S(2)}, u32[]{:S(2)}) collective-permute-start(bf16[4,32,16,256]{3,2,1,0:T(8,128)(2,1)S(1)} %all_to_all.20.kv_ref), channel_id=1, source_target_pairs={{0,1},{1,0},{2,3},{3,2},{4,5},{5,4},{6,7},{7,6},{8,9},{9,8},{10,11... | collective-permute-start | bytes 3145736 | tf_op jit(solution)/shard_map/ppermute | solution.py:164
  46.1 0.0 copy-done.2
  46.1 2.0 %attention_first.1 = (f32[2,256,128]{2,1,0:T(8,128)S(1)}, f32[2,256,128]{2,1,0:T(8,128)S(1)}, f32[2,256,128]{2,1,0:T(8,128)S(1)}) custom-call(bf16[128,256]{1,0:T(8,128)(2,1)S(1)} %copy-done.2, bf16[128,256]{1,0:T(8,128)(2,1)S(1)} %collective-permute-done.partner_ref.queries_ref, bf16[4,32,16,256]{3,2,1,0:T(8,128)(2,1)S(1)} %all_to_all.20.kv_ref), custom_call_target="tpu_custom_call" | custom-call | flops 536870912 | bytes 2097152 | tf_op jit(solution)/shard_map/attention_first/pallas_call | solution.py:165
  48.2 0.2 collective-permute-done.1.kv_ref
  48.4 2.1 %attention_second_own.1 = bf16[8,128,256]{2,1,0:T(8,128)(2,1)} custom-call(bf16[128,256]{1,0:T(8,128)(2,1)S(1)} %copy-done.2, bf16[4,32,16,256]{3,2,1,0:T(8,128)(2,1)S(1)} %collective-permute-done.1.kv_ref, f32[2,256,128]{2,1,0:T(8,128)S(1)} %get-tuple-element.12.top_ref, f32[2,256,128]{2,1,0:T(8,128)S(1)} %get-tuple-element.13.total_ref, ...), custom_call_target="tpu_custom_call" | custom-call | flops 536870912 | bytes 2097152 | tf_op jit(solution)/shard_map/attention_second_own/pallas_call | solution.py:176
  50.5 14.0 %all-to-all-start.3 = ((bf16[8,128,256]{2,1,0:T(8,128)(2,1)}), bf16[8,128,256]{2,1,0:T(8,128)(2,1)S(1)}, u32[]{:S(2)}, u32[]{:S(2)}) async-start(bf16[8,128,256]{2,1,0:T(8,128)(2,1)} %attention_second_own.1), calls=%async_computation.3 | async-start | bytes 1048576 | tf_op jit(solution)/shard_map/all_to_all | solution.py:185
  64.4 2.1 %attention_second_partner.1 = bf16[8,128,256]{2,1,0:T(8,128)(2,1)} custom-call(bf16[128,256]{1,0:T(8,128)(2,1)S(1)} %collective-permute-done.partner_ref.queries_ref, bf16[4,32,16,256]{3,2,1,0:T(8,128)(2,1)S(1)} %collective-permute-done.1.kv_ref, f32[2,256,128]{2,1,0:T(8,128)S(1)} %get-tuple-element.12.top_ref, ...), custom_call_target="tpu_custom_call" | custom-call | flops 536870912 | bytes 2097152 | tf_op jit(solution)/shard_map/attention_second_partner/pallas_call | solution.py:176
  66.5 15.9 %all-to-all-done.3.heads_ref = bf16[8,128,256]{2,1,0:T(8,128)(2,1)S(1)} async-done(((bf16[8,128,256]{2,1,0:T(8,128)(2,1)}), bf16[8,128,256]{2,1,0:T(8,128)(2,1)S(1)}, u32[]{:S(2)}, u32[]{:S(2)}) %all-to-all-start.3) | async-done | bytes 524320 | tf_op jit(solution)/shard_map/all_to_all | solution.py:185
  82.4 3.5 %all-to-all-start.2 = ((bf16[8,128,256]{2,1,0:T(8,128)(2,1)}), bf16[8,128,256]{2,1,0:T(8,128)(2,1)S(1)}, u32[]{:S(2)}, u32[]{:S(2)}) async-start(bf16[8,128,256]{2,1,0:T(8,128)(2,1)} %attention_second_partner.1), calls=%async_computation.2 | async-start | bytes 1048576 | tf_op jit(solution)/shard_map/all_to_all | solution.py:185
  85.9 2.4 %collective-permute-start.3 = (bf16[8,128,256]{2,1,0:T(8,128)(2,1)S(1)}, bf16[8,128,256]{2,1,0:T(8,128)(2,1)S(1)}, u32[]{:S(2)}, u32[]{:S(2)}) collective-permute-start(bf16[8,128,256]{2,1,0:T(8,128)(2,1)S(1)} %all-to-all-done.3.heads_ref), channel_id=1, source_target_pairs={{0,1},{1,0},{2,3},{3,2},{4,5},{5,4},{6,7},{7,6},{8,9},{9,8},{10,11... | collective-permute-start | bytes 1572872 | tf_op jit(solution)/shard_map/ppermute | solution.py:186
  88.3 15.5 %all-to-all-done.2.heads_ref = bf16[8,128,256]{2,1,0:T(8,128)(2,1)S(1)} async-done(((bf16[8,128,256]{2,1,0:T(8,128)(2,1)}), bf16[8,128,256]{2,1,0:T(8,128)(2,1)S(1)}, u32[]{:S(2)}, u32[]{:S(2)}) %all-to-all-start.2) | async-done | bytes 524320 | tf_op jit(solution)/shard_map/all_to_all | solution.py:185
  103.8 2.4 %collective-permute-start.2 = (bf16[8,128,256]{2,1,0:T(8,128)(2,1)S(1)}, bf16[8,128,256]{2,1,0:T(8,128)(2,1)S(1)}, u32[]{:S(2)}, u32[]{:S(2)}) collective-permute-start(bf16[8,128,256]{2,1,0:T(8,128)(2,1)S(1)} %all-to-all-done.2.heads_ref), channel_id=1, source_target_pairs={{0,1},{1,0},{2,3},{3,2},{4,5},{5,4},{6,7},{7,6},{8,9},{9,8},{10,11... | collective-permute-start | bytes 1572872 | tf_op jit(solution)/shard_map/ppermute | solution.py:186
  106.1 0.0 copy-done.3
  106.2 0.0 copy-start
  106.2 2.2 %copy-done = bf16[8192,256]{1,0:T(8,128)(2,1)S(1)} copy-done((bf16[8192,256]{1,0:T(8,128)(2,1)S(1)}, bf16[8192,256]{1,0:T(8,128)(2,1)}, u32[]{:S(2)}) %copy-start) | copy-done | bytes 4194328
  108.3 0.0 copy-start.1
  108.3 0.9 project_own_self.1.refs_0_
  109.3 0.0 collective-permute-done.3.heads_ref
  109.3 1.3 %copy-done.1 = bf16[8192,256]{1,0:T(8,128)(2,1)S(1)} copy-done((bf16[8192,256]{1,0:T(8,128)(2,1)S(1)}, bf16[8192,256]{1,0:T(8,128)(2,1)}, u32[]{:S(2)}) %copy-start.1) | copy-done | bytes 4194328
  110.5 0.9 project_own_sibling.1.refs_0_
  111.4 0.9 project_partner_self.1.refs_0_
  112.4 0.0 collective-permute-done.2.heads_ref
  112.4 1.5 %project_partner_sibling.1 = bf16[128,256]{1,0:T(8,128)(2,1)} custom-call(s32[2,64]{1,0:T(2,128)S(1)} %bitcast.4, bf16[8,128,256]{2,1,0:T(8,128)(2,1)S(1)} %collective-permute-done.2.heads_ref, bf16[8192,256]{1,0:T(8,128)(2,1)S(1)} %copy-done.1, f32[128,256]{1,0:T(8,128)S(1)} %project_partner_self.1.refs_0_), custom_call_target="tpu_custom_call" | custom-call | flops 134217728 | bytes 2097152 | tf_op jit(solution)/shard_map/project_partner_sibling/pallas_call | solution.py:190
Async XLA Ops:
  0.0 46.1 %copy-start.2 = (bf16[128,256]{1,0:T(8,128)(2,1)S(1)}, bf16[128,256]{1,0:T(8,128)(2,1)}, u32[]{:S(2)}) copy-start(bf16[128,256]{1,0:T(8,128)(2,1)} %queries_ref.3) | copy-start | bytes 196612
  1.6 22.2 %all-to-all-start = ((bf16[32,16,256]{2,1,0:T(8,128)(2,1)}), bf16[32,16,256]{2,1,0:T(8,128)(2,1)S(1)}, u32[]{:S(2)}, u32[]{:S(2)}) async-start(bf16[32,16,256]{2,1,0:T(8,128)(2,1)} %spread_kv.1), calls=%async_computation | async-start | bytes 524288 | tf_op jit(solution)/shard_map/all_to_all | solution.py:153
  12.9 9.2 %collective-permute-start = (bf16[128,256]{1,0:T(8,128)(2,1)}, bf16[128,256]{1,0:T(8,128)(2,1)S(1)}, u32[]{:S(2)}, u32[]{:S(2)}) collective-permute-start(bf16[128,256]{1,0:T(8,128)(2,1)} %queries_ref.3), channel_id=1, source_target_pairs={{0,2},{2,0},{1,3},{3,1},{4,6},{6,4},{5,7},{7,5},{8,10},{10,8},{9,1... | collective-permute-start | bytes 196616 | tf_op jit(solution)/shard_map/ppermute | solution.py:144
  35.0 71.1 %copy-start.3 = (s32[64,2]{0,1:T(2,128)S(1)}, s32[64,2]{0,1:T(2,128)}, u32[]{:S(2)}) copy-start(s32[64,2]{0,1:T(2,128)} %param.9) | copy-start | bytes 1540
  35.0 13.4 %collective-permute-start.1 = (bf16[4,32,16,256]{3,2,1,0:T(8,128)(2,1)S(1)}, bf16[4,32,16,256]{3,2,1,0:T(8,128)(2,1)S(1)}, u32[]{:S(2)}, u32[]{:S(2)}) collective-permute-start(bf16[4,32,16,256]{3,2,1,0:T(8,128)(2,1)S(1)} %all_to_all.20.kv_ref), channel_id=1, source_target_pairs={{0,1},{1,0},{2,3},{3,2},{4,5},{5,4},{6,7},{7,6},{8,9},{9,8},{10,11... | collective-permute-start | bytes 3145736 | tf_op jit(solution)/shard_map/ppermute | solution.py:164
  50.5 31.9 %all-to-all-start.3 = ((bf16[8,128,256]{2,1,0:T(8,128)(2,1)}), bf16[8,128,256]{2,1,0:T(8,128)(2,1)S(1)}, u32[]{:S(2)}, u32[]{:S(2)}) async-start(bf16[8,128,256]{2,1,0:T(8,128)(2,1)} %attention_second_own.1), calls=%async_computation.3 | async-start | bytes 1048576 | tf_op jit(solution)/shard_map/all_to_all | solution.py:185
  82.4 21.4 %all-to-all-start.2 = ((bf16[8,128,256]{2,1,0:T(8,128)(2,1)}), bf16[8,128,256]{2,1,0:T(8,128)(2,1)S(1)}, u32[]{:S(2)}, u32[]{:S(2)}) async-start(bf16[8,128,256]{2,1,0:T(8,128)(2,1)} %attention_second_partner.1), calls=%async_computation.2 | async-start | bytes 1048576 | tf_op jit(solution)/shard_map/all_to_all | solution.py:185
  85.9 23.4 %collective-permute-start.3 = (bf16[8,128,256]{2,1,0:T(8,128)(2,1)S(1)}, bf16[8,128,256]{2,1,0:T(8,128)(2,1)S(1)}, u32[]{:S(2)}, u32[]{:S(2)}) collective-permute-start(bf16[8,128,256]{2,1,0:T(8,128)(2,1)S(1)} %all-to-all-done.3.heads_ref), channel_id=1, source_target_pairs={{0,1},{1,0},{2,3},{3,2},{4,5},{5,4},{6,7},{7,6},{8,9},{9,8},{10,11... | collective-permute-start | bytes 1572872 | tf_op jit(solution)/shard_map/ppermute | solution.py:186
  103.8 8.6 %collective-permute-start.2 = (bf16[8,128,256]{2,1,0:T(8,128)(2,1)S(1)}, bf16[8,128,256]{2,1,0:T(8,128)(2,1)S(1)}, u32[]{:S(2)}, u32[]{:S(2)}) collective-permute-start(bf16[8,128,256]{2,1,0:T(8,128)(2,1)S(1)} %all-to-all-done.2.heads_ref), channel_id=1, source_target_pairs={{0,1},{1,0},{2,3},{3,2},{4,5},{5,4},{6,7},{7,6},{8,9},{9,8},{10,11... | collective-permute-start | bytes 1572872 | tf_op jit(solution)/shard_map/ppermute | solution.py:186
  106.2 2.2 %copy-start = (bf16[8192,256]{1,0:T(8,128)(2,1)S(1)}, bf16[8192,256]{1,0:T(8,128)(2,1)}, u32[]{:S(2)}) copy-start(bf16[8192,256]{1,0:T(8,128)(2,1)} %weight_ref.7) | copy-start | bytes 12582916
  108.3 2.2 %copy-start.1 = (bf16[8192,256]{1,0:T(8,128)(2,1)S(1)}, bf16[8192,256]{1,0:T(8,128)(2,1)}, u32[]{:S(2)}) copy-start(bf16[8192,256]{1,0:T(8,128)(2,1)} %weight_ref.7) | copy-start | bytes 12582916

commit v7 on v4

--- a/solution.py
+++ b/solution.py
@@ -13,8 +13,9 @@
 SIZES = (4, 2, 2, 2, 8, 2, 2)
 AXES = ("y", "yp", "xl", "xp", "z", "xh", "core")
 SEQ = ("y", "yp", "xl", "xp")
-SQUARE = ("yp", "xp")
 N_SQUARE = 4
+PLANE = ("y", "yp", "xl", "xp", "xh", "core")
+RING = ("z", "core")
 FSDP = ("z", "xh", "core")
 N_SEQ = 32
 N_Z = 8
@@ -23,6 +24,29 @@
 ANY = pl.BlockSpec(memory_space=pl.ANY)
 VMEM = pl.BlockSpec(memory_space=pltpu.VMEM)
 SMEM = pl.BlockSpec(memory_space=pltpu.SMEM)
+
+
+def square_groups():
+    groups = []
+    for core in range(2):
+        for top in range(core, 8, 2):
+            for left in range(core, 8, 2):
+                group = [None] * N_SQUARE
+                for y in (top, (top + 1) % 8):
+                    for x in (left, (left + 1) % 8):
+                        flat = (y * 4 + x % 4) * 2 + x // 4
+                        group[y % 2 * 2 + x % 2] = flat * 2 + core
+                groups.append(group)
+    return groups
+
+
+def z_pairs():
+    pairs = []
+    for z in range(8):
+        for core in range(2):
+            other = z ^ 1 if core == 0 else (((z + 1) ^ 1) - 1) % 8
+            pairs.append((z * 2 + core, other * 2 + core))
+    return pairs
 
 
 def spread_kernel(keys_ref, values_ref, out_ref, block, sems):
@@ -101,38 +125,45 @@
     for i, queries in enumerate((queries_ref, partner_ref)):
         state = top_ref[i, :, :1], total_ref[i, :, :1], summed_ref[i]
         heads.append(finish(attend(queries, kv_ref, 1 - core, state)))
-    heads = jnp.concatenate(heads, axis=1)
+    first = lax.axis_index("xh") == 0
+    heads = [jnp.where(first, heads[0], heads[1]), jnp.where(first, heads[1], heads[0])]
     for i in range(N_Z):
-        out_ref[i] = heads
-
-
-def project(mask_ref, heads_ref, weight_ref, from_core):
+        out_ref[i] = heads[i % 2]
+
+
+def project(mask_ref, heads_ref, weight_ref, of_pair, of_sibling):
     columns = weight_ref.shape[1]
+    parity, core = lax.rem(lax.axis_index("z"), 2), lax.axis_index("core")
+    from_chip = 1 - parity if of_pair else parity
+    from_core = 1 - core if of_sibling else core
     total = jnp.zeros((heads_ref.shape[1], columns), jnp.float32)
-    xh = lax.axis_index("xh")
     for z in range(N_Z):
         rows = []
-        for chip in (z * 2 + xh, z * 2 + 1 - xh):
-            for i in range(2):
-                block = (chip * 2 + from_core) * 2 + i
-                at = pl.ds(pl.multiple_of(block * BLOCK, BLOCK), BLOCK)
-                line = []
-                for j in range(columns // BLOCK):
-                    keep = mask_ref[j, block].astype(jnp.float32).astype(jnp.bfloat16)
-                    line.append(weight_ref[at, j * BLOCK : (j + 1) * BLOCK] * keep)
-                rows.append(jnp.concatenate(line, axis=1))
+        for i in range(2):
+            block = ((z * 2 + from_chip) * 2 + from_core) * 2 + i
+            at = pl.ds(pl.multiple_of(block * BLOCK, BLOCK), BLOCK)
+            line = []
+            for j in range(columns // BLOCK):
+                keep = mask_ref[j, block].astype(jnp.float32).astype(jnp.bfloat16)
+                line.append(weight_ref[at, j * BLOCK : (j + 1) * BLOCK] * keep)
+            rows.append(jnp.concatenate(line, axis=1))
         pruned = jnp.concatenate(rows, axis=0)
         total += jnp.dot(heads_ref[z], pruned, preferred_element_type=jnp.float32)
     return total
 
 
-def project_own_kernel(mask_ref, heads_ref, weight_ref, out_ref):
-    out_ref[...] = project(mask_ref, heads_ref, weight_ref, lax.axis_index("core"))
-
-
-def project_other_kernel(mask_ref, heads_ref, weight_ref, part_ref, out_ref):
-    rest = project(mask_ref, heads_ref, weight_ref, 1 - lax.axis_index("core"))
-    out_ref[...] = (part_ref[...] + rest).astype(out_ref.dtype)
+def project_first_kernel(mask_ref, weight_ref, self_ref, out_ref):
+    out_ref[...] = project(mask_ref, self_ref, weight_ref, False, False)
+
+
+def project_second_kernel(mask_ref, weight_ref, sibling_ref, pair_ref, part_ref, out_ref):
+    part = part_ref[...] + project(mask_ref, sibling_ref, weight_ref, False, True)
+    out_ref[...] = part + project(mask_ref, pair_ref, weight_ref, True, False)
+
+
+def project_third_kernel(mask_ref, weight_ref, sibling_ref, part_ref, out_ref):
+    part = part_ref[...] + project(mask_ref, sibling_ref, weight_ref, True, True)
+    out_ref[...] = part.astype(out_ref.dtype)
 
 
 def per_device(queries, keys, values, out_weight, block_mask):
@@ -163,7 +194,7 @@
         compiler_params=params,
         name="square",
     )(piece)
-    own = lax.all_to_all(square, SQUARE, 0, 0, tiled=True)
+    own = lax.all_to_all(square, PLANE, 0, 0, axis_index_groups=square_groups(), tiled=True)
     other = lax.ppermute(own, "core", swap)
     state = pl.pallas_call(
         attention_first_kernel,
@@ -176,33 +207,32 @@
     )(queries, partner_queries, own)
     heads = pl.pallas_call(
         attention_second_kernel,
-        out_shape=shape((N_Z, rows, 4 * HD), jnp.bfloat16),
+        out_shape=shape((N_Z, rows, 2 * HD), jnp.bfloat16),
         in_specs=[VMEM] * 6,
         out_specs=VMEM,
         compiler_params=params,
         cost_estimate=cost,
         name="attention_second",
     )(queries, partner_queries, other, *state)
-    own_heads = lax.all_to_all(heads, "z", 0, 0, tiled=True)
-    other_heads = lax.ppermute(own_heads, "core", swap)
-    part = pl.pallas_call(
-        project_own_kernel,
-        out_shape=shape((rows, columns), jnp.float32),
-        in_specs=[SMEM, VMEM, VMEM],
-        out_specs=VMEM,
-        compiler_params=params,
-        cost_estimate=pl.CostEstimate(flops=2**28, bytes_accessed=2**22, transcendentals=0),
-        name="project_own",
-    )(mask, own_heads, out_weight)
-    return pl.pallas_call(
-        project_other_kernel,
-        out_shape=shape((rows, columns), jnp.bfloat16),
-        in_specs=[SMEM, VMEM, VMEM, VMEM],
-        out_specs=VMEM,
-        compiler_params=params,
-        cost_estimate=pl.CostEstimate(flops=2**28, bytes_accessed=2**22, transcendentals=0),
-        name="project_other",
-    )(mask, other_heads, out_weight, part)
+    along_z = lax.all_to_all(heads, "z", 0, 0, tiled=True)
+    from_pair = lax.ppermute(along_z, RING, z_pairs())
+    sibling = lax.ppermute(along_z, "core", swap)
+    pair_sibling = lax.ppermute(from_pair, "core", swap)
+
+    def call(kernel, name, dtype, *arrays):
+        return pl.pallas_call(
+            kernel,
+            out_shape=shape((rows, columns), dtype),
+            in_specs=[SMEM] + [VMEM] * (1 + len(arrays)),
+            out_specs=VMEM,
+            compiler_params=params,
+            cost_estimate=pl.CostEstimate(flops=2**27, bytes_accessed=2**21, transcendentals=0),
+            name=name,
+        )(mask, out_weight, *arrays)
+
+    first = call(project_first_kernel, "project_first", jnp.float32, along_z)
+    second = call(project_second_kernel, "project_second", jnp.float32, sibling, from_pair, first)
+    return call(project_third_kernel, "project_third", jnp.bfloat16, pair_sibling, second)
 
 
 def solution(mesh):

time: 100 us -> 98.4 us (0.984)
  blocking collectives: 53.2 us -> 46.1 us
  waiting for transfers between devices: 7.84 us -> 12.9 us
    all_to_all x2, blocking collectives: 53.2 us -> 46.1 us  [the longest x1 30.2 us: per_device(): along_z = lax.all_to_all(heads, 'z', 0, 0, tiled=True)]
    ppermute x1 -> x3, waiting for transfers between devices: 1.15 us -> 6.19 us  [the longest x1 6.18 us: per_device(): from_pair = lax.ppermute(along_z, RING, z_pairs())]
    ppermute x1, starting transfers between devices: 11 us -> 6.47 us  [per_device(): other = lax.ppermute(own, 'core', swap)]
    ppermute x1 -> x3, starting transfers between devices: 3.63 us -> 7.31 us  [the longest x1 3.01 us: per_device(): sibling = lax.ppermute(along_z, 'core', swap)]
    pallas_call x3 -> x4, Pallas kernels: 5.07 us -> 5.76 us  [the longest x3 3.49 us: call(): pl.pallas_call(kernel, out_shape=shape((rows, columns), dtype), in_specs=...]
  transfers between devices with their start and end apart: 4 -> 6, of which waited for: 4 -> 4; matrix products, arithmetic and copies ran while one was open for 0% -> 0% of each run, Pallas kernels for 3% -> 4%
where the time goes in v7:
time: 98.4 us; the launch traced here: 98 us
  blocking collectives  46.1 us (47%)
  starting transfers between devices  29.5 us (30%)
  waiting for transfers between devices  12.9 us (13%)
  Pallas kernels  9.4 us (10%)
    all_to_all x1, blocking collectives, per_device(): along_z = lax.all_to_all(heads, 'z', 0, 0, tiled=True)  30.2 us
    all_to_all x1, blocking collectives, per_device(): lax.all_to_all(square, PLANE, 0, 0, axis_index_groups=square_groups(), ti...  15.9 us
    all_to_all x1, starting transfers between devices, per_device(): piece = lax.all_to_all(spread, SEQ, 0, 0, tiled=True)  11.3 us
    ppermute x1, starting transfers between devices, per_device(): other = lax.ppermute(own, 'core', swap)  6.47 us
    ppermute x1, waiting for transfers between devices, per_device(): from_pair = lax.ppermute(along_z, RING, z_pairs())  6.18 us
    ppermute x1, waiting for transfers between devices, per_device(): partner_queries = lax.ppermute(queries, 'xh', swap)  4.81 us
    ppermute x1, starting transfers between devices, per_device(): partner_queries = lax.ppermute(queries, 'xh', swap)  4.42 us
    pallas_call x3, Pallas kernels, call(): pl.pallas_call(kernel, out_shape=shape((rows, columns), dtype), in_specs=...  3.49 us
  transfers between devices with their start and end apart: 6, of which 4 were waited for; matrix products, arithmetic and copies ran while one was open for 0% of the time, Pallas kernels for 4%

profile of v7, /device:TPU:1, one launch (start us, length us, event | category | flops | bytes accessed | tf_op | source)
XLA Modules:
  0.0 98.0 jit_solution(2842017003041741790)
XLA Ops:
  0.0 0.0 copy-start.1
  0.0 1.6 %spread_kv.1 = bf16[32,16,256]{2,1,0:T(8,128)(2,1)} custom-call(bf16[128,1024]{1,0:T(8,128)(2,1)} %keys_ref.1, bf16[128,1024]{1,0:T(8,128)(2,1)} %values_ref.1), custom_call_target="tpu_custom_call" | custom-call | tf_op jit(solution)/shard_map/spread_kv/pallas_call | solution.py:179
  1.6 11.3 %all-to-all-start = ((bf16[32,16,256]{2,1,0:T(8,128)(2,1)}), bf16[32,16,256]{2,1,0:T(8,128)(2,1)S(1)}, u32[]{:S(2)}, u32[]{:S(2)}) async-start(bf16[32,16,256]{2,1,0:T(8,128)(2,1)} %spread_kv.1), calls=%async_computation | async-start | bytes 524288 | tf_op jit(solution)/shard_map/all_to_all | solution.py:187
  12.9 0.0 copy-start.2
  12.9 4.4 %collective-permute-start = (bf16[128,256]{1,0:T(8,128)(2,1)}, bf16[128,256]{1,0:T(8,128)(2,1)S(1)}, u32[]{:S(2)}, u32[]{:S(2)}) collective-permute-start(bf16[128,256]{1,0:T(8,128)(2,1)} %queries_ref.3), channel_id=1, source_target_pairs={{0,2},{2,0},{1,3},{3,1},{4,6},{6,4},{5,7},{7,5},{8,10},{10,8},{9,1... | collective-permute-start | bytes 196616 | tf_op jit(solution)/shard_map/ppermute | solution.py:178
  17.3 4.8 %collective-permute-done.partner_ref = bf16[128,256]{1,0:T(8,128)(2,1)S(1)} collective-permute-done((bf16[128,256]{1,0:T(8,128)(2,1)}, bf16[128,256]{1,0:T(8,128)(2,1)S(1)}, u32[]{:S(2)}, u32[]{:S(2)}) %collective-permute-start) | collective-permute-done | bytes 65568 | tf_op jit(solution)/shard_map/ppermute | solution.py:178
  22.1 1.6 %all-to-all-done.piece_ref = bf16[32,16,256]{2,1,0:T(8,128)(2,1)S(1)} async-done(((bf16[32,16,256]{2,1,0:T(8,128)(2,1)}), bf16[32,16,256]{2,1,0:T(8,128)(2,1)S(1)}, u32[]{:S(2)}, u32[]{:S(2)}) %all-to-all-start) | async-done | bytes 262176 | tf_op jit(solution)/shard_map/all_to_all | solution.py:187
  23.7 0.0 copy-start
  23.8 0.1 square.1
  23.8 15.9 %all_to_all.15.kv_ref = bf16[4,32,16,256]{3,2,1,0:T(8,128)(2,1)S(1)} all-to-all(bf16[4,32,16,256]{3,2,1,0:T(8,128)(2,1)S(1)} %square.1), channel_id=1, replica_groups={{0,32,128,160},{64,96,192,224},{2,34,130,162},{66,98,194,226},{256,288,..., dimensions={0} | all-to-all | bytes 2097152 | tf_op jit(solution)/shard_map/all_to_all | solution.py:197
  39.7 6.5 %collective-permute-start.1 = (bf16[4,32,16,256]{3,2,1,0:T(8,128)(2,1)S(1)}, bf16[4,32,16,256]{3,2,1,0:T(8,128)(2,1)S(1)}, u32[]{:S(2)}, u32[]{:S(2)}) collective-permute-start(bf16[4,32,16,256]{3,2,1,0:T(8,128)(2,1)S(1)} %all_to_all.15.kv_ref), channel_id=1, source_target_pairs={{0,1},{1,0},{2,3},{3,2},{4,5},{5,4},{6,7},{7,6},{8,9},{9,8},{10,11... | collective-permute-start | bytes 3145736 | tf_op jit(solution)/shard_map/ppermute | solution.py:198
  46.2 0.0 copy-done.1
  46.2 2.0 %attention_first.1 = (f32[2,256,128]{2,1,0:T(8,128)S(1)}, f32[2,256,128]{2,1,0:T(8,128)S(1)}, f32[2,256,128]{2,1,0:T(8,128)S(1)}) custom-call(bf16[128,256]{1,0:T(8,128)(2,1)S(1)} %copy-done.1, bf16[128,256]{1,0:T(8,128)(2,1)S(1)} %collective-permute-done.partner_ref, bf16[4,32,16,256]{3,2,1,0:T(8,128)(2,1)S(1)} %all_to_all.15.kv_ref), custom_call_target="tpu_custom_call" | custom-call | flops 536870912 | bytes 2097152 | tf_op jit(solution)/shard_map/attention_first/pallas_call | solution.py:199
  48.2 0.2 collective-permute-done.1.kv_ref
  48.4 2.3 %attention_second.1 = bf16[8,128,256]{2,1,0:T(8,128)(2,1)S(1)} custom-call(bf16[128,256]{1,0:T(8,128)(2,1)S(1)} %copy-done.1, bf16[128,256]{1,0:T(8,128)(2,1)S(1)} %collective-permute-done.partner_ref, bf16[4,32,16,256]{3,2,1,0:T(8,128)(2,1)S(1)} %collective-permute-done.1.kv_ref, f32[2,256,128]{2,1,0:T(8,128)S(1)} %get-tuple-element.12.top_ref, ...), custom_call_target="tpu_custom_call" | custom-call | flops 536870912 | bytes 2097152 | tf_op jit(solution)/shard_map/attention_second/pallas_call | solution.py:208
  50.7 30.2 %all_to_all.16.self_ref = bf16[8,128,256]{2,1,0:T(8,128)(2,1)S(1)} all-to-all(bf16[8,128,256]{2,1,0:T(8,128)(2,1)S(1)} %attention_second.1), channel_id=1, replica_groups=mesh['y'=4,'yp'=2,'xl'=2,'xp'=2,'z'=8,'xh'=2,'core'=2] {'z'}, dimensions={0} | all-to-all | bytes 1048576 | tf_op jit(solution)/shard_map/all_to_all | solution.py:217
  80.9 1.9 %collective-permute-start.2 = (bf16[8,128,256]{2,1,0:T(8,128)(2,1)S(1)}, bf16[8,128,256]{2,1,0:T(8,128)(2,1)S(1)}, u32[]{:S(2)}, u32[]{:S(2)}) collective-permute-start(bf16[8,128,256]{2,1,0:T(8,128)(2,1)S(1)} %all_to_all.16.self_ref), channel_id=1, source_target_pairs={{0,4},{1,29},{4,0},{5,9},{8,12},{9,5},{12,8},{13,17},{16,20},{17,1... | collective-permute-start | bytes 1572872 | tf_op jit(solution)/shard_map/ppermute | solution.py:218
  82.8 3.0 %collective-permute-start.4 = (bf16[8,128,256]{2,1,0:T(8,128)(2,1)S(1)}, bf16[8,128,256]{2,1,0:T(8,128)(2,1)S(1)}, u32[]{:S(2)}, u32[]{:S(2)}) collective-permute-start(bf16[8,128,256]{2,1,0:T(8,128)(2,1)S(1)} %all_to_all.16.self_ref), channel_id=1, source_target_pairs={{0,1},{1,0},{2,3},{3,2},{4,5},{5,4},{6,7},{7,6},{8,9},{9,8},{10,11... | collective-permute-start | bytes 1572872 | tf_op jit(solution)/shard_map/ppermute | solution.py:219
  85.8 6.2 %collective-permute-done.2.pair_ref = bf16[8,128,256]{2,1,0:T(8,128)(2,1)S(1)} collective-permute-done((bf16[8,128,256]{2,1,0:T(8,128)(2,1)S(1)}, bf16[8,128,256]{2,1,0:T(8,128)(2,1)S(1)}, u32[]{:S(2)}, u32[]{:S(2)}) %collective-permute-start.2) | collective-permute-done | bytes 524320 | tf_op jit(solution)/shard_map/ppermute | solution.py:218
  92.0 2.4 %collective-permute-start.3 = (bf16[8,128,256]{2,1,0:T(8,128)(2,1)S(1)}, bf16[8,128,256]{2,1,0:T(8,128)(2,1)S(1)}, u32[]{:S(2)}, u32[]{:S(2)}) collective-permute-start(bf16[8,128,256]{2,1,0:T(8,128)(2,1)S(1)} %collective-permute-done.2.pair_ref), channel_id=1, source_target_pairs={{0,1},{1,0},{2,3},{3,2},{4,5},{5,4},{6,7},{7,6},{8,9},{9,8},{10,11... | collective-permute-start | bytes 1572872 | tf_op jit(solution)/shard_map/ppermute | solution.py:220
  94.4 0.0 copy-done.2
  94.4 0.0 copy-done
  94.4 0.9 project_first.1.part_ref
  95.3 0.0 collective-permute-done.4.sibling_ref
  95.4 1.1 %project_second.1.part_ref = f32[128,256]{1,0:T(8,128)S(1)} custom-call(s32[2,64]{1,0:T(2,128)S(1)} %bitcast.2, bf16[8192,256]{1,0:T(8,128)(2,1)S(1)} %copy-done, bf16[8,128,256]{2,1,0:T(8,128)(2,1)S(1)} %collective-permute-done.4.sibling_ref, bf16[8,128,256]{2,1,0:T(8,128)(2,1)S(1)} %collective-permute-done.2.pair_ref, f32[128,256]{1,0:T(8,128)S(1)} %project_first.1.part_ref), custom_call_target="tpu_custom_call" | custom-call | flops 134217728 | bytes 2097152 | tf_op jit(solution)/shard_map/project_second/pallas_call | solution.py:223
  96.4 0.0 collective-permute-done.3.sibling_ref
  96.4 1.5 %project_third.1 = bf16[128,256]{1,0:T(8,128)(2,1)} custom-call(s32[2,64]{1,0:T(2,128)S(1)} %bitcast.3, bf16[8192,256]{1,0:T(8,128)(2,1)S(1)} %copy-done, bf16[8,128,256]{2,1,0:T(8,128)(2,1)S(1)} %collective-permute-done.3.sibling_ref, f32[128,256]{1,0:T(8,128)S(1)} %project_second.1.part_ref), custom_call_target="tpu_custom_call" | custom-call | flops 134217728 | bytes 2097152 | tf_op jit(solution)/shard_map/project_third/pallas_call | solution.py:223
Async XLA Ops:
  0.0 46.2 %copy-start.1 = (bf16[128,256]{1,0:T(8,128)(2,1)S(1)}, bf16[128,256]{1,0:T(8,128)(2,1)}, u32[]{:S(2)}) copy-start(bf16[128,256]{1,0:T(8,128)(2,1)} %queries_ref.3) | copy-start | bytes 196612
  1.6 22.2 %all-to-all-start = ((bf16[32,16,256]{2,1,0:T(8,128)(2,1)}), bf16[32,16,256]{2,1,0:T(8,128)(2,1)S(1)}, u32[]{:S(2)}, u32[]{:S(2)}) async-start(bf16[32,16,256]{2,1,0:T(8,128)(2,1)} %spread_kv.1), calls=%async_computation | async-start | bytes 524288 | tf_op jit(solution)/shard_map/all_to_all | solution.py:187
  12.9 81.6 %copy-start.2 = (s32[64,2]{0,1:T(2,128)S(1)}, s32[64,2]{0,1:T(2,128)}, u32[]{:S(2)}) copy-start(s32[64,2]{0,1:T(2,128)} %param.9) | copy-start | bytes 1540
  12.9 9.2 %collective-permute-start = (bf16[128,256]{1,0:T(8,128)(2,1)}, bf16[128,256]{1,0:T(8,128)(2,1)S(1)}, u32[]{:S(2)}, u32[]{:S(2)}) collective-permute-start(bf16[128,256]{1,0:T(8,128)(2,1)} %queries_ref.3), channel_id=1, source_target_pairs={{0,2},{2,0},{1,3},{3,1},{4,6},{6,4},{5,7},{7,5},{8,10},{10,8},{9,1... | collective-permute-start | bytes 196616 | tf_op jit(solution)/shard_map/ppermute | solution.py:178
  23.7 70.7 %copy-start = (bf16[8192,256]{1,0:T(8,128)(2,1)S(1)}, bf16[8192,256]{1,0:T(8,128)(2,1)}, u32[]{:S(2)}) copy-start(bf16[8192,256]{1,0:T(8,128)(2,1)} %weight_ref.5) | copy-start | bytes 12582916
  39.7 8.7 %collective-permute-start.1 = (bf16[4,32,16,256]{3,2,1,0:T(8,128)(2,1)S(1)}, bf16[4,32,16,256]{3,2,1,0:T(8,128)(2,1)S(1)}, u32[]{:S(2)}, u32[]{:S(2)}) collective-permute-start(bf16[4,32,16,256]{3,2,1,0:T(8,128)(2,1)S(1)} %all_to_all.15.kv_ref), channel_id=1, source_target_pairs={{0,1},{1,0},{2,3},{3,2},{4,5},{5,4},{6,7},{7,6},{8,9},{9,8},{10,11... | collective-permute-start | bytes 3145736 | tf_op jit(solution)/shard_map/ppermute | solution.py:198
  80.9 11.1 %collective-permute-start.2 = (bf16[8,128,256]{2,1,0:T(8,128)(2,1)S(1)}, bf16[8,128,256]{2,1,0:T(8,128)(2,1)S(1)}, u32[]{:S(2)}, u32[]{:S(2)}) collective-permute-start(bf16[8,128,256]{2,1,0:T(8,128)(2,1)S(1)} %all_to_all.16.self_ref), channel_id=1, source_target_pairs={{0,4},{1,29},{4,0},{5,9},{8,12},{9,5},{12,8},{13,17},{16,20},{17,1... | collective-permute-start | bytes 1572872 | tf_op jit(solution)/shard_map/ppermute | solution.py:218
  82.8 12.5 %collective-permute-start.4 = (bf16[8,128,256]{2,1,0:T(8,128)(2,1)S(1)}, bf16[8,128,256]{2,1,0:T(8,128)(2,1)S(1)}, u32[]{:S(2)}, u32[]{:S(2)}) collective-permute-start(bf16[8,128,256]{2,1,0:T(8,128)(2,1)S(1)} %all_to_all.16.self_ref), channel_id=1, source_target_pairs={{0,1},{1,0},{2,3},{3,2},{4,5},{5,4},{6,7},{7,6},{8,9},{9,8},{10,11... | collective-permute-start | bytes 1572872 | tf_op jit(solution)/shard_map/ppermute | solution.py:219
  92.0 4.4 %collective-permute-start.3 = (bf16[8,128,256]{2,1,0:T(8,128)(2,1)S(1)}, bf16[8,128,256]{2,1,0:T(8,128)(2,1)S(1)}, u32[]{:S(2)}, u32[]{:S(2)}) collective-permute-start(bf16[8,128,256]{2,1,0:T(8,128)(2,1)S(1)} %collective-permute-done.2.pair_ref), channel_id=1, source_target_pairs={{0,1},{1,0},{2,3},{3,2},{4,5},{5,4},{6,7},{7,6},{8,9},{9,8},{10,11... | collective-permute-start | bytes 1572872 | tf_op jit(solution)/shard_map/ppermute | solution.py:220

commit v8 on v7

--- a/solution.py
+++ b/solution.py
@@ -13,8 +13,8 @@
 SIZES = (4, 2, 2, 2, 8, 2, 2)
 AXES = ("y", "yp", "xl", "xp", "z", "xh", "core")
 SEQ = ("y", "yp", "xl", "xp")
-N_SQUARE = 4
-PLANE = ("y", "yp", "xl", "xp", "xh", "core")
+N_PAIR = 2
+COLUMN = ("y", "yp", "core")
 RING = ("z", "core")
 FSDP = ("z", "xh", "core")
 N_SEQ = 32
@@ -26,17 +26,12 @@
 SMEM = pl.BlockSpec(memory_space=pltpu.SMEM)
 
 
-def square_groups():
+def y_pairs():
     groups = []
     for core in range(2):
-        for top in range(core, 8, 2):
-            for left in range(core, 8, 2):
-                group = [None] * N_SQUARE
-                for y in (top, (top + 1) % 8):
-                    for x in (left, (left + 1) % 8):
-                        flat = (y * 4 + x % 4) * 2 + x // 4
-                        group[y % 2 * 2 + x % 2] = flat * 2 + core
-                groups.append(group)
+        for first in range(core, 8, 2):
+            members = sorted((first, (first + 1) % 8), key=lambda y: y % 2)
+            groups.append([y * 2 + core for y in members])
     return groups
 
 
@@ -65,21 +60,21 @@
         copy.wait()
     pieces = [
         block[pl.ds(pl.multiple_of((place * 2 + core) * part, part), part), :]
-        for place in range(N_SQUARE)
+        for place in range(N_PAIR)
     ]
     for i in range(N_SEQ):
-        out_ref[i] = pieces[i // 4 % 2 * 2 + i % 2]
-
-
-def square_kernel(piece_ref, out_ref):
-    for i in range(N_SQUARE):
+        out_ref[i] = pieces[i // 4 % 2]
+
+
+def pair_kernel(piece_ref, out_ref):
+    for i in range(N_PAIR):
         out_ref[i] = piece_ref[...]
 
 
 def attend(queries_ref, kv_ref, from_core, state):
     rows = queries_ref.shape[0]
     part = kv_ref.shape[2]
-    width = N_SQUARE * N_SEQ * part
+    width = N_PAIR * N_SEQ * part
     seq = lax.axis_index("y") * 8 + lax.axis_index("yp") * 4 + lax.axis_index("xl") * 2
     start = (seq + lax.axis_index("xp")) * rows
     q = jnp.concatenate([queries_ref[:, :HD], queries_ref[:, HD:]], axis=0)
@@ -169,7 +164,7 @@
 def per_device(queries, keys, values, out_weight, block_mask):
     rows = queries.shape[0]
     columns = out_weight.shape[1]
-    part = rows // (2 * N_SQUARE)
+    part = rows // (2 * N_PAIR)
     mask = block_mask.T
     params = pltpu.CompilerParams(vmem_limit_bytes=32 * 2**20)
     shape = jax.ShapeDtypeStruct
@@ -186,15 +181,15 @@
     )(keys, values)
     piece = lax.all_to_all(spread, SEQ, 0, 0, tiled=True)
     piece, partner_queries = lax.optimization_barrier((piece, partner_queries))
-    square = pl.pallas_call(
-        square_kernel,
-        out_shape=shape((N_SQUARE, N_SEQ, part, 2 * HD), jnp.bfloat16),
+    pair = pl.pallas_call(
+        pair_kernel,
+        out_shape=shape((N_PAIR, N_SEQ, part, 2 * HD), jnp.bfloat16),
         in_specs=[VMEM],
         out_specs=VMEM,
         compiler_params=params,
-        name="square",
+        name="pair",
     )(piece)
-    own = lax.all_to_all(square, PLANE, 0, 0, axis_index_groups=square_groups(), tiled=True)
+    own = lax.all_to_all(pair, COLUMN, 0, 0, axis_index_groups=y_pairs(), tiled=True)
     other = lax.ppermute(own, "core", swap)
     state = pl.pallas_call(
         attention_first_kernel,
@@ -217,7 +212,6 @@
     along_z = lax.all_to_all(heads, "z", 0, 0, tiled=True)
     from_pair = lax.ppermute(along_z, RING, z_pairs())
     sibling = lax.ppermute(along_z, "core", swap)
-    pair_sibling = lax.ppermute(from_pair, "core", swap)
 
     def call(kernel, name, dtype, *arrays):
         return pl.pallas_call(
@@ -231,6 +225,8 @@
         )(mask, out_weight, *arrays)
 
     first = call(project_first_kernel, "project_first", jnp.float32, along_z)
+    from_pair, first = lax.optimization_barrier((from_pair, first))
+    pair_sibling = lax.ppermute(from_pair, "core", swap)
     second = call(project_second_kernel, "project_second", jnp.float32, sibling, from_pair, first)
     return call(project_third_kernel, "project_third", jnp.bfloat16, pair_sibling, second)
 

time: 98.4 us -> 104 us (1.057)
  starting transfers between devices: 29.5 us -> 34.4 us
    ppermute x1, waiting for transfers between devices: 4.81 us -> 8.38 us  [per_device(): partner_queries = lax.ppermute(queries, 'xh', swap)]
    all_to_all x1, blocking collectives: 30.2 us -> 33.6 us  [per_device(): along_z = lax.all_to_all(heads, 'z', 0, 0, tiled=True)]
    all_to_all x1, blocking collectives: 15.9 us -> 12.8 us  [per_device(): lax.all_to_all(pair, COLUMN, 0, 0, axis_index_groups=y_pairs(), tiled=True)]
    ppermute x1, starting transfers between devices: 6.47 us -> 9.06 us  [per_device(): other = lax.ppermute(own, 'core', swap)]
    ppermute x1, waiting for transfers between devices: 6.18 us -> 4.07 us  [per_device(): from_pair = lax.ppermute(along_z, RING, z_pairs())]
    all_to_all x1, waiting for transfers between devices: 1.64 us -> 0.23 us  [per_device(): piece = lax.all_to_all(spread, SEQ, 0, 0, tiled=True)]
    ppermute x1, starting transfers between devices: 3.01 us -> 4.2 us  [per_device(): sibling = lax.ppermute(along_z, 'core', swap)]
    ppermute x1, starting transfers between devices: 2.39 us -> 3.57 us  [per_device(): pair_sibling = lax.ppermute(from_pair, 'core', swap)]
  transfers between devices with their start and end apart: 6 -> 6, of which waited for: 4 -> 5; matrix products, arithmetic and copies ran while one was open for 0% -> 0% of each run, Pallas kernels for 4% -> 4%
where the time goes in v8:
time: 104 us
  blocking collectives  46.4 us (45%)
  starting transfers between devices  34.4 us (33%)
  waiting for transfers between devices  13.4 us (13%)
  Pallas kernels  9.51 us (9%)
    all_to_all x1, blocking collectives, per_device(): along_z = lax.all_to_all(heads, 'z', 0, 0, tiled=True)  33.6 us
    all_to_all x1, blocking collectives, per_device(): lax.all_to_all(pair, COLUMN, 0, 0, axis_index_groups=y_pairs(), tiled=True)  12.8 us
    all_to_all x1, starting transfers between devices, per_device(): piece = lax.all_to_all(spread, SEQ, 0, 0, tiled=True)  11.3 us
    ppermute x1, starting transfers between devices, per_device(): other = lax.ppermute(own, 'core', swap)  9.06 us
    ppermute x1, waiting for transfers between devices, per_device(): partner_queries = lax.ppermute(queries, 'xh', swap)  8.38 us
    ppermute x1, starting transfers between devices, per_device(): partner_queries = lax.ppermute(queries, 'xh', swap)  4.42 us
    ppermute x1, starting transfers between devices, per_device(): sibling = lax.ppermute(along_z, 'core', swap)  4.2 us
    ppermute x1, waiting for transfers between devices, per_device(): from_pair = lax.ppermute(along_z, RING, z_pairs())  4.07 us
  transfers between devices with their start and end apart: 6, of which 5 were waited for; matrix products, arithmetic and copies ran while one was open for 0% of the time, Pallas kernels for 4%

profile of v8, /device:TPU:1, one launch (start us, length us, event | category | flops | bytes accessed | tf_op | source)
XLA Modules:
  0.0 103.8 jit_solution(11749254841181772994)
XLA Ops:
  0.0 0.0 copy-start.1
  0.0 1.7 %spread_kv.1 = bf16[32,32,256]{2,1,0:T(8,128)(2,1)} custom-call(bf16[128,1024]{1,0:T(8,128)(2,1)} %keys_ref.1, bf16[128,1024]{1,0:T(8,128)(2,1)} %values_ref.1), custom_call_target="tpu_custom_call" | custom-call | tf_op jit(solution)/shard_map/spread_kv/pallas_call | solution.py:174
  1.7 11.3 %all-to-all-start = ((bf16[32,32,256]{2,1,0:T(8,128)(2,1)}), bf16[32,32,256]{2,1,0:T(8,128)(2,1)S(1)}, u32[]{:S(2)}, u32[]{:S(2)}) async-start(bf16[32,32,256]{2,1,0:T(8,128)(2,1)} %spread_kv.1), calls=%async_computation | async-start | bytes 1048576 | tf_op jit(solution)/shard_map/all_to_all | solution.py:182
  13.0 4.4 %collective-permute-start = (bf16[128,256]{1,0:T(8,128)(2,1)}, bf16[128,256]{1,0:T(8,128)(2,1)S(1)}, u32[]{:S(2)}, u32[]{:S(2)}) collective-permute-start(bf16[128,256]{1,0:T(8,128)(2,1)} %queries_ref.3), channel_id=1, source_target_pairs={{0,2},{2,0},{1,3},{3,1},{4,6},{6,4},{5,7},{7,5},{8,10},{10,8},{9,1... | collective-permute-start | bytes 196616 | tf_op jit(solution)/shard_map/ppermute | solution.py:173
  17.4 8.4 %collective-permute-done.partner_ref = bf16[128,256]{1,0:T(8,128)(2,1)S(1)} collective-permute-done((bf16[128,256]{1,0:T(8,128)(2,1)}, bf16[128,256]{1,0:T(8,128)(2,1)S(1)}, u32[]{:S(2)}, u32[]{:S(2)}) %collective-permute-start) | collective-permute-done | bytes 65568 | tf_op jit(solution)/shard_map/ppermute | solution.py:173
  25.8 0.2 all-to-all-done.piece_ref
  26.0 0.1 pair.1
  26.1 0.0 copy-start
  26.1 0.0 copy-start.2
  26.1 12.8 %all_to_all.15.kv_ref = bf16[2,32,32,256]{3,2,1,0:T(8,128)(2,1)S(1)} all-to-all(bf16[2,32,32,256]{3,2,1,0:T(8,128)(2,1)S(1)} %pair.1), channel_id=1, replica_groups={{0,128},{256,384},{512,640},{768,896},{257,129},{513,385},{769,641},{1,..., dimensions={0} | all-to-all | bytes 2097152 | tf_op jit(solution)/shard_map/all_to_all | solution.py:192
  38.9 9.1 %collective-permute-start.1 = (bf16[2,32,32,256]{3,2,1,0:T(8,128)(2,1)S(1)}, bf16[2,32,32,256]{3,2,1,0:T(8,128)(2,1)S(1)}, u32[]{:S(2)}, u32[]{:S(2)}) collective-permute-start(bf16[2,32,32,256]{3,2,1,0:T(8,128)(2,1)S(1)} %all_to_all.15.kv_ref), channel_id=1, source_target_pairs={{0,1},{1,0},{2,3},{3,2},{4,5},{5,4},{6,7},{7,6},{8,9},{9,8},{10,11... | collective-permute-start | bytes 3145736 | tf_op jit(solution)/shard_map/ppermute | solution.py:193
  48.0 0.0 copy-done.1
  48.0 2.0 %attention_first.1 = (f32[2,256,128]{2,1,0:T(8,128)S(1)}, f32[2,256,128]{2,1,0:T(8,128)S(1)}, f32[2,256,128]{2,1,0:T(8,128)S(1)}) custom-call(bf16[128,256]{1,0:T(8,128)(2,1)S(1)} %copy-done.1, bf16[128,256]{1,0:T(8,128)(2,1)S(1)} %collective-permute-done.partner_ref, bf16[2,32,32,256]{3,2,1,0:T(8,128)(2,1)S(1)} %all_to_all.15.kv_ref), custom_call_target="tpu_custom_call" | custom-call | flops 536870912 | bytes 2097152 | tf_op jit(solution)/shard_map/attention_first/pallas_call | solution.py:194
  50.0 0.2 collective-permute-done.1.kv_ref
  50.3 2.3 %attention_second.1 = bf16[8,128,256]{2,1,0:T(8,128)(2,1)S(1)} custom-call(bf16[128,256]{1,0:T(8,128)(2,1)S(1)} %copy-done.1, bf16[128,256]{1,0:T(8,128)(2,1)S(1)} %collective-permute-done.partner_ref, bf16[2,32,32,256]{3,2,1,0:T(8,128)(2,1)S(1)} %collective-permute-done.1.kv_ref, f32[2,256,128]{2,1,0:T(8,128)S(1)} %get-tuple-element.14.top_ref, ...), custom_call_target="tpu_custom_call" | custom-call | flops 536870912 | bytes 2097152 | tf_op jit(solution)/shard_map/attention_second/pallas_call | solution.py:203
  52.5 33.6 %all_to_all.16.self_ref = bf16[8,128,256]{2,1,0:T(8,128)(2,1)S(1)} all-to-all(bf16[8,128,256]{2,1,0:T(8,128)(2,1)S(1)} %attention_second.1), channel_id=1, replica_groups=mesh['y'=4,'yp'=2,'xl'=2,'xp'=2,'z'=8,'xh'=2,'core'=2] {'z'}, dimensions={0} | all-to-all | bytes 1048576 | tf_op jit(solution)/shard_map/all_to_all | solution.py:212
  86.1 1.9 %collective-permute-start.2 = (bf16[8,128,256]{2,1,0:T(8,128)(2,1)S(1)}, bf16[8,128,256]{2,1,0:T(8,128)(2,1)S(1)}, u32[]{:S(2)}, u32[]{:S(2)}) collective-permute-start(bf16[8,128,256]{2,1,0:T(8,128)(2,1)S(1)} %all_to_all.16.self_ref), channel_id=1, source_target_pairs={{0,4},{1,29},{4,0},{5,9},{8,12},{9,5},{12,8},{13,17},{16,20},{17,1... | collective-permute-start | bytes 1572872 | tf_op jit(solution)/shard_map/ppermute | solution.py:213
  88.0 4.2 %collective-permute-start.4 = (bf16[8,128,256]{2,1,0:T(8,128)(2,1)S(1)}, bf16[8,128,256]{2,1,0:T(8,128)(2,1)S(1)}, u32[]{:S(2)}, u32[]{:S(2)}) collective-permute-start(bf16[8,128,256]{2,1,0:T(8,128)(2,1)S(1)} %all_to_all.16.self_ref), channel_id=1, source_target_pairs={{0,1},{1,0},{2,3},{3,2},{4,5},{5,4},{6,7},{7,6},{8,9},{9,8},{10,11... | collective-permute-start | bytes 1572872 | tf_op jit(solution)/shard_map/ppermute | solution.py:214
  92.2 0.0 copy-done
  92.2 0.0 copy-done.2
  92.2 0.9 project_first.1.part_ref
  93.1 4.1 %collective-permute-done.2.pair_ref = bf16[8,128,256]{2,1,0:T(8,128)(2,1)S(1)} collective-permute-done((bf16[8,128,256]{2,1,0:T(8,128)(2,1)S(1)}, bf16[8,128,256]{2,1,0:T(8,128)(2,1)S(1)}, u32[]{:S(2)}, u32[]{:S(2)}) %collective-permute-start.2) | collective-permute-done | bytes 524320 | tf_op jit(solution)/shard_map/ppermute | solution.py:213
  97.2 3.6 %collective-permute-start.3 = (bf16[8,128,256]{2,1,0:T(8,128)(2,1)S(1)}, bf16[8,128,256]{2,1,0:T(8,128)(2,1)S(1)}, u32[]{:S(2)}, u32[]{:S(2)}) collective-permute-start(bf16[8,128,256]{2,1,0:T(8,128)(2,1)S(1)} %collective-permute-done.2.pair_ref), channel_id=1, source_target_pairs={{0,1},{1,0},{2,3},{3,2},{4,5},{5,4},{6,7},{7,6},{8,9},{9,8},{10,11... | collective-permute-start | bytes 1572872 | tf_op jit(solution)/shard_map/ppermute | solution.py:229
  100.8 0.0 collective-permute-done.4.sibling_ref
  100.8 1.1 %project_second.1.part_ref = f32[128,256]{1,0:T(8,128)S(1)} custom-call(s32[2,64]{1,0:T(2,128)S(1)} %bitcast.2, bf16[8192,256]{1,0:T(8,128)(2,1)S(1)} %copy-done, bf16[8,128,256]{2,1,0:T(8,128)(2,1)S(1)} %collective-permute-done.4.sibling_ref, bf16[8,128,256]{2,1,0:T(8,128)(2,1)S(1)} %collective-permute-done.2.pair_ref, f32[128,256]{1,0:T(8,128)S(1)} %project_first.1.part_ref), custom_call_target="tpu_custom_call" | custom-call | flops 134217728 | bytes 2097152 | tf_op jit(solution)/shard_map/project_second/pallas_call | solution.py:217
  101.9 0.4 collective-permute-done.3.sibling_ref
  102.3 1.5 %project_third.1 = bf16[128,256]{1,0:T(8,128)(2,1)} custom-call(s32[2,64]{1,0:T(2,128)S(1)} %bitcast.3, bf16[8192,256]{1,0:T(8,128)(2,1)S(1)} %copy-done, bf16[8,128,256]{2,1,0:T(8,128)(2,1)S(1)} %collective-permute-done.3.sibling_ref, f32[128,256]{1,0:T(8,128)S(1)} %project_second.1.part_ref), custom_call_target="tpu_custom_call" | custom-call | flops 134217728 | bytes 2097152 | tf_op jit(solution)/shard_map/project_third/pallas_call | solution.py:217
Async XLA Ops:
  0.0 48.0 %copy-start.1 = (bf16[128,256]{1,0:T(8,128)(2,1)S(1)}, bf16[128,256]{1,0:T(8,128)(2,1)}, u32[]{:S(2)}) copy-start(bf16[128,256]{1,0:T(8,128)(2,1)} %queries_ref.3) | copy-start | bytes 196612
  1.7 24.3 %all-to-all-start = ((bf16[32,32,256]{2,1,0:T(8,128)(2,1)}), bf16[32,32,256]{2,1,0:T(8,128)(2,1)S(1)}, u32[]{:S(2)}, u32[]{:S(2)}) async-start(bf16[32,32,256]{2,1,0:T(8,128)(2,1)} %spread_kv.1), calls=%async_computation | async-start | bytes 1048576 | tf_op jit(solution)/shard_map/all_to_all | solution.py:182
  13.0 12.8 %collective-permute-start = (bf16[128,256]{1,0:T(8,128)(2,1)}, bf16[128,256]{1,0:T(8,128)(2,1)S(1)}, u32[]{:S(2)}, u32[]{:S(2)}) collective-permute-start(bf16[128,256]{1,0:T(8,128)(2,1)} %queries_ref.3), channel_id=1, source_target_pairs={{0,2},{2,0},{1,3},{3,1},{4,6},{6,4},{5,7},{7,5},{8,10},{10,8},{9,1... | collective-permute-start | bytes 196616 | tf_op jit(solution)/shard_map/ppermute | solution.py:173
  26.1 66.1 %copy-start = (bf16[8192,256]{1,0:T(8,128)(2,1)S(1)}, bf16[8192,256]{1,0:T(8,128)(2,1)}, u32[]{:S(2)}) copy-start(bf16[8192,256]{1,0:T(8,128)(2,1)} %weight_ref.5) | copy-start | bytes 12582916
  26.1 66.1 %copy-start.2 = (s32[64,2]{0,1:T(2,128)S(1)}, s32[64,2]{0,1:T(2,128)}, u32[]{:S(2)}) copy-start(s32[64,2]{0,1:T(2,128)} %param.9) | copy-start | bytes 1540
  38.9 11.3 %collective-permute-start.1 = (bf16[2,32,32,256]{3,2,1,0:T(8,128)(2,1)S(1)}, bf16[2,32,32,256]{3,2,1,0:T(8,128)(2,1)S(1)}, u32[]{:S(2)}, u32[]{:S(2)}) collective-permute-start(bf16[2,32,32,256]{3,2,1,0:T(8,128)(2,1)S(1)} %all_to_all.15.kv_ref), channel_id=1, source_target_pairs={{0,1},{1,0},{2,3},{3,2},{4,5},{5,4},{6,7},{7,6},{8,9},{9,8},{10,11... | collective-permute-start | bytes 3145736 | tf_op jit(solution)/shard_map/ppermute | solution.py:193
  86.1 11.1 %collective-permute-start.2 = (bf16[8,128,256]{2,1,0:T(8,128)(2,1)S(1)}, bf16[8,128,256]{2,1,0:T(8,128)(2,1)S(1)}, u32[]{:S(2)}, u32[]{:S(2)}) collective-permute-start(bf16[8,128,256]{2,1,0:T(8,128)(2,1)S(1)} %all_to_all.16.self_ref), channel_id=1, source_target_pairs={{0,4},{1,29},{4,0},{5,9},{8,12},{9,5},{12,8},{13,17},{16,20},{17,1... | collective-permute-start | bytes 1572872 | tf_op jit(solution)/shard_map/ppermute | solution.py:213
  88.0 12.8 %collective-permute-start.4 = (bf16[8,128,256]{2,1,0:T(8,128)(2,1)S(1)}, bf16[8,128,256]{2,1,0:T(8,128)(2,1)S(1)}, u32[]{:S(2)}, u32[]{:S(2)}) collective-permute-start(bf16[8,128,256]{2,1,0:T(8,128)(2,1)S(1)} %all_to_all.16.self_ref), channel_id=1, source_target_pairs={{0,1},{1,0},{2,3},{3,2},{4,5},{5,4},{6,7},{7,6},{8,9},{9,8},{10,11... | collective-permute-start | bytes 1572872 | tf_op jit(solution)/shard_map/ppermute | solution.py:214
  97.2 5.1 %collective-permute-start.3 = (bf16[8,128,256]{2,1,0:T(8,128)(2,1)S(1)}, bf16[8,128,256]{2,1,0:T(8,128)(2,1)S(1)}, u32[]{:S(2)}, u32[]{:S(2)}) collective-permute-start(bf16[8,128,256]{2,1,0:T(8,128)(2,1)S(1)} %collective-permute-done.2.pair_ref), channel_id=1, source_target_pairs={{0,1},{1,0},{2,3},{3,2},{4,5},{5,4},{6,7},{7,6},{8,9},{9,8},{10,11... | collective-permute-start | bytes 1572872 | tf_op jit(solution)/shard_map/ppermute | solution.py:229

commit v9 on v7

--- a/solution.py
+++ b/solution.py
@@ -76,13 +76,19 @@
         out_ref[i] = piece_ref[...]
 
 
-def attend(queries_ref, kv_ref, from_core, state):
+def stack_kernel(queries_ref, partner_ref, out_ref):
     rows = queries_ref.shape[0]
+    for i, ref in enumerate((queries_ref, partner_ref)):
+        for head in range(2):
+            out_ref[i, head * rows : (head + 1) * rows] = ref[:, head * HD : (head + 1) * HD]
+
+
+def attend(q, kv_ref, from_core, state):
+    rows = q.shape[0] // 2
     part = kv_ref.shape[2]
     width = N_SQUARE * N_SEQ * part
     seq = lax.axis_index("y") * 8 + lax.axis_index("yp") * 4 + lax.axis_index("xl") * 2
     start = (seq + lax.axis_index("xp")) * rows
-    q = jnp.concatenate([queries_ref[:, :HD], queries_ref[:, HD:]], axis=0)
     query_pos = start + lax.broadcasted_iota(jnp.int32, (2 * rows, 1), 0) % rows
     column = lax.broadcasted_iota(jnp.int32, (1, width), 1)
     block = column // part
@@ -112,19 +118,19 @@
     return jnp.concatenate([normed[:rows], normed[rows:]], axis=1)
 
 
-def attention_first_kernel(queries_ref, partner_ref, kv_ref, *state_refs):
+def attention_first_kernel(queries_ref, kv_ref, *state_refs):
     core = lax.axis_index("core")
-    for i, queries in enumerate((queries_ref, partner_ref)):
-        for ref, value in zip(state_refs, attend(queries, kv_ref, core, None)):
+    for i in range(2):
+        for ref, value in zip(state_refs, attend(queries_ref[i], kv_ref, core, None)):
             ref[i] = jnp.broadcast_to(value, ref.shape[1:])
 
 
-def attention_second_kernel(queries_ref, partner_ref, kv_ref, top_ref, total_ref, summed_ref, out_ref):
+def attention_second_kernel(queries_ref, kv_ref, top_ref, total_ref, summed_ref, out_ref):
     core = lax.axis_index("core")
     heads = []
-    for i, queries in enumerate((queries_ref, partner_ref)):
+    for i in range(2):
         state = top_ref[i, :, :1], total_ref[i, :, :1], summed_ref[i]
-        heads.append(finish(attend(queries, kv_ref, 1 - core, state)))
+        heads.append(finish(attend(queries_ref[i], kv_ref, 1 - core, state)))
     first = lax.axis_index("xh") == 0
     heads = [jnp.where(first, heads[0], heads[1]), jnp.where(first, heads[1], heads[0])]
     for i in range(N_Z):
@@ -185,7 +191,16 @@
         name="spread_kv",
     )(keys, values)
     piece = lax.all_to_all(spread, SEQ, 0, 0, tiled=True)
-    piece, partner_queries = lax.optimization_barrier((piece, partner_queries))
+    stacked = pl.pallas_call(
+        stack_kernel,
+        out_shape=shape((2, 2 * rows, HD), jnp.bfloat16),
+        in_specs=[VMEM] * 2,
+        out_specs=VMEM,
+        compiler_params=params,
+        cost_estimate=pl.CostEstimate(flops=2**36, bytes_accessed=2**18, transcendentals=0),
+        name="stack_queries",
+    )(queries, partner_queries)
+    piece, stacked = lax.optimization_barrier((piece, stacked))
     square = pl.pallas_call(
         square_kernel,
         out_shape=shape((N_SQUARE, N_SEQ, part, 2 * HD), jnp.bfloat16),
@@ -199,21 +214,21 @@
     state = pl.pallas_call(
         attention_first_kernel,
         out_shape=[shape((2, 2 * rows, HD), jnp.float32)] * 3,
-        in_specs=[VMEM] * 3,
+        in_specs=[VMEM] * 2,
         out_specs=[VMEM] * 3,
         compiler_params=params,
         cost_estimate=cost,
         name="attention_first",
-    )(queries, partner_queries, own)
+    )(stacked, own)
     heads = pl.pallas_call(
         attention_second_kernel,
         out_shape=shape((N_Z, rows, 2 * HD), jnp.bfloat16),
-        in_specs=[VMEM] * 6,
+        in_specs=[VMEM] * 5,
         out_specs=VMEM,
         compiler_params=params,
         cost_estimate=cost,
         name="attention_second",
-    )(queries, partner_queries, other, *state)
+    )(stacked, other, *state)
     along_z = lax.all_to_all(heads, "z", 0, 0, tiled=True)
     from_pair = lax.ppermute(along_z, RING, z_pairs())
     sibling = lax.ppermute(along_z, "core", swap)

time: 98.4 us -> 102 us (1.037)
  waiting for transfers between devices: 12.9 us -> 16.4 us
    all_to_all x1, waiting for transfers between devices: 1.64 us -> 9.94 us  [per_device(): piece = lax.all_to_all(spread, SEQ, 0, 0, tiled=True)]
    ppermute x1, waiting for transfers between devices: 4.81 us -> 0.01 us  [per_device(): partner_queries = lax.ppermute(queries, 'xh', swap)]
    all_to_all x1, starting transfers between devices: 11.3 us -> 7.76 us  [per_device(): piece = lax.all_to_all(spread, SEQ, 0, 0, tiled=True)]
    ppermute x1, starting transfers between devices: 4.42 us -> 7.93 us  [per_device(): partner_queries = lax.ppermute(queries, 'xh', swap)]
    all_to_all x1, blocking collectives: 30.2 us -> 32.3 us  [per_device(): along_z = lax.all_to_all(heads, 'z', 0, 0, tiled=True)]
    all_to_all x1, blocking collectives: 15.9 us -> 13.9 us  [per_device(): lax.all_to_all(square, PLANE, 0, 0, axis_index_groups=square_groups(), ti...]
  transfers between devices with their start and end apart: 6 -> 6, of which waited for: 4 -> 3; matrix products, arithmetic and copies ran while one was open for 0% -> 0% of each run, Pallas kernels for 4% -> 5%
where the time goes in v9:
time: 102 us
  blocking collectives  46.2 us (45%)
  starting transfers between devices  29 us (28%)
  waiting for transfers between devices  16.4 us (16%)
  Pallas kernels  9.39 us (9%)
    all_to_all x1, blocking collectives, per_device(): along_z = lax.all_to_all(heads, 'z', 0, 0, tiled=True)  32.3 us
    all_to_all x1, blocking collectives, per_device(): lax.all_to_all(square, PLANE, 0, 0, axis_index_groups=square_groups(), ti...  13.9 us
    all_to_all x1, waiting for transfers between devices, per_device(): piece = lax.all_to_all(spread, SEQ, 0, 0, tiled=True)  9.94 us
    ppermute x1, starting transfers between devices, per_device(): partner_queries = lax.ppermute(queries, 'xh', swap)  7.93 us
    all_to_all x1, starting transfers between devices, per_device(): piece = lax.all_to_all(spread, SEQ, 0, 0, tiled=True)  7.76 us
    ppermute x1, waiting for transfers between devices, per_device(): from_pair = lax.ppermute(along_z, RING, z_pairs())  6.18 us
    ppermute x1, starting transfers between devices, per_device(): other = lax.ppermute(own, 'core', swap)  5.99 us
    pallas_call x3, Pallas kernels, call(): pl.pallas_call(kernel, out_shape=shape((rows, columns), dtype), in_specs=...  3.49 us
  transfers between devices with their start and end apart: 6, of which 3 were waited for; matrix products, arithmetic and copies ran while one was open for 0% of the time, Pallas kernels for 5%

profile of v9, /device:TPU:1, one launch (start us, length us, event | category | flops | bytes accessed | tf_op | source)
XLA Modules:
  0.0 101.9 jit_solution(1409746055549179842)
XLA Ops:
  0.0 7.9 %collective-permute-start = (bf16[128,256]{1,0:T(8,128)(2,1)}, bf16[128,256]{1,0:T(8,128)(2,1)S(1)}, u32[]{:S(2)}, u32[]{:S(2)}) collective-permute-start(bf16[128,256]{1,0:T(8,128)(2,1)} %queries_ref.1), channel_id=1, source_target_pairs={{0,2},{2,0},{1,3},{3,1},{4,6},{6,4},{5,7},{7,5},{8,10},{10,8},{9,1... | collective-permute-start | bytes 196616 | tf_op jit(solution)/shard_map/ppermute | solution.py:184
  7.9 1.5 %spread_kv.1 = bf16[32,16,256]{2,1,0:T(8,128)(2,1)} custom-call(bf16[128,1024]{1,0:T(8,128)(2,1)} %keys_ref.1, bf16[128,1024]{1,0:T(8,128)(2,1)} %values_ref.1), custom_call_target="tpu_custom_call" | custom-call | tf_op jit(solution)/shard_map/spread_kv/pallas_call | solution.py:185
  9.5 7.8 %all-to-all-start = ((bf16[32,16,256]{2,1,0:T(8,128)(2,1)}), bf16[32,16,256]{2,1,0:T(8,128)(2,1)S(1)}, u32[]{:S(2)}, u32[]{:S(2)}) async-start(bf16[32,16,256]{2,1,0:T(8,128)(2,1)} %spread_kv.1), calls=%async_computation | async-start | bytes 524288 | tf_op jit(solution)/shard_map/all_to_all | solution.py:193
  17.2 0.0 collective-permute-done.partner_ref
  17.3 0.0 copy-start.2
  17.3 0.8 copy-done.2
  18.1 0.0 copy-start.1
  18.1 9.9 %all-to-all-done.piece_ref = bf16[32,16,256]{2,1,0:T(8,128)(2,1)S(1)} async-done(((bf16[32,16,256]{2,1,0:T(8,128)(2,1)}), bf16[32,16,256]{2,1,0:T(8,128)(2,1)S(1)}, u32[]{:S(2)}, u32[]{:S(2)}) %all-to-all-start) | async-done | bytes 262176 | tf_op jit(solution)/shard_map/all_to_all | solution.py:193
  28.1 0.0 copy-start
  28.1 0.1 square.1
  28.2 13.9 %all_to_all.15.kv_ref = bf16[4,32,16,256]{3,2,1,0:T(8,128)(2,1)S(1)} all-to-all(bf16[4,32,16,256]{3,2,1,0:T(8,128)(2,1)S(1)} %square.1), channel_id=1, replica_groups={{0,32,128,160},{64,96,192,224},{2,34,130,162},{66,98,194,226},{256,288,..., dimensions={0} | all-to-all | bytes 2097152 | tf_op jit(solution)/shard_map/all_to_all | solution.py:212
  42.0 6.0 %collective-permute-start.1 = (bf16[4,32,16,256]{3,2,1,0:T(8,128)(2,1)S(1)}, bf16[4,32,16,256]{3,2,1,0:T(8,128)(2,1)S(1)}, u32[]{:S(2)}, u32[]{:S(2)}) collective-permute-start(bf16[4,32,16,256]{3,2,1,0:T(8,128)(2,1)S(1)} %all_to_all.15.kv_ref), channel_id=1, source_target_pairs={{0,1},{1,0},{2,3},{3,2},{4,5},{5,4},{6,7},{7,6},{8,9},{9,8},{10,11... | collective-permute-start | bytes 3145736 | tf_op jit(solution)/shard_map/ppermute | solution.py:213
  48.0 2.0 %attention_first.1 = (f32[2,256,128]{2,1,0:T(8,128)S(1)}, f32[2,256,128]{2,1,0:T(8,128)S(1)}, f32[2,256,128]{2,1,0:T(8,128)S(1)}) custom-call(bf16[2,256,128]{2,1,0:T(8,128)(2,1)S(1)} %stack_queries.1.queries_ref, bf16[4,32,16,256]{3,2,1,0:T(8,128)(2,1)S(1)} %all_to_all.15.kv_ref), custom_call_target="tpu_custom_call" | custom-call | flops 536870912 | bytes 2097152 | tf_op jit(solution)/shard_map/attention_first/pallas_call | solution.py:214
  50.1 0.3 collective-permute-done.1.kv_ref
  50.3 2.3 %attention_second.1 = bf16[8,128,256]{2,1,0:T(8,128)(2,1)S(1)} custom-call(bf16[2,256,128]{2,1,0:T(8,128)(2,1)S(1)} %stack_queries.1.queries_ref, bf16[4,32,16,256]{3,2,1,0:T(8,128)(2,1)S(1)} %collective-permute-done.1.kv_ref, f32[2,256,128]{2,1,0:T(8,128)S(1)} %get-tuple-element.12.top_ref, f32[2,256,128]{2,1,0:T(8,128)S(1)} %get-tuple-element.13.total_ref, ...), custom_call_target="tpu_custom_call" | custom-call | flops 536870912 | bytes 2097152 | tf_op jit(solution)/shard_map/attention_second/pallas_call | solution.py:223
  52.6 32.3 %all_to_all.16.self_ref = bf16[8,128,256]{2,1,0:T(8,128)(2,1)S(1)} all-to-all(bf16[8,128,256]{2,1,0:T(8,128)(2,1)S(1)} %attention_second.1), channel_id=1, replica_groups=mesh['y'=4,'yp'=2,'xl'=2,'xp'=2,'z'=8,'xh'=2,'core'=2] {'z'}, dimensions={0} | all-to-all | bytes 1048576 | tf_op jit(solution)/shard_map/all_to_all | solution.py:232
  84.8 1.9 %collective-permute-start.2 = (bf16[8,128,256]{2,1,0:T(8,128)(2,1)S(1)}, bf16[8,128,256]{2,1,0:T(8,128)(2,1)S(1)}, u32[]{:S(2)}, u32[]{:S(2)}) collective-permute-start(bf16[8,128,256]{2,1,0:T(8,128)(2,1)S(1)} %all_to_all.16.self_ref), channel_id=1, source_target_pairs={{0,4},{1,29},{4,0},{5,9},{8,12},{9,5},{12,8},{13,17},{16,20},{17,1... | collective-permute-start | bytes 1572872 | tf_op jit(solution)/shard_map/ppermute | solution.py:233
  86.8 3.0 %collective-permute-start.4 = (bf16[8,128,256]{2,1,0:T(8,128)(2,1)S(1)}, bf16[8,128,256]{2,1,0:T(8,128)(2,1)S(1)}, u32[]{:S(2)}, u32[]{:S(2)}) collective-permute-start(bf16[8,128,256]{2,1,0:T(8,128)(2,1)S(1)} %all_to_all.16.self_ref), channel_id=1, source_target_pairs={{0,1},{1,0},{2,3},{3,2},{4,5},{5,4},{6,7},{7,6},{8,9},{9,8},{10,11... | collective-permute-start | bytes 1572872 | tf_op jit(solution)/shard_map/ppermute | solution.py:234
  89.8 6.2 %collective-permute-done.2.pair_ref = bf16[8,128,256]{2,1,0:T(8,128)(2,1)S(1)} collective-permute-done((bf16[8,128,256]{2,1,0:T(8,128)(2,1)S(1)}, bf16[8,128,256]{2,1,0:T(8,128)(2,1)S(1)}, u32[]{:S(2)}, u32[]{:S(2)}) %collective-permute-start.2) | collective-permute-done | bytes 524320 | tf_op jit(solution)/shard_map/ppermute | solution.py:233
  96.0 2.4 %collective-permute-start.3 = (bf16[8,128,256]{2,1,0:T(8,128)(2,1)S(1)}, bf16[8,128,256]{2,1,0:T(8,128)(2,1)S(1)}, u32[]{:S(2)}, u32[]{:S(2)}) collective-permute-start(bf16[8,128,256]{2,1,0:T(8,128)(2,1)S(1)} %collective-permute-done.2.pair_ref), channel_id=1, source_target_pairs={{0,1},{1,0},{2,3},{3,2},{4,5},{5,4},{6,7},{7,6},{8,9},{9,8},{10,11... | collective-permute-start | bytes 1572872 | tf_op jit(solution)/shard_map/ppermute | solution.py:235
  98.4 0.0 copy-done.1
  98.4 0.0 copy-done
  98.4 0.9 project_first.1.part_ref
  99.3 0.0 collective-permute-done.4.sibling_ref
  99.3 1.1 %project_second.1.part_ref = f32[128,256]{1,0:T(8,128)S(1)} custom-call(s32[2,64]{1,0:T(2,128)S(1)} %bitcast.2, bf16[8192,256]{1,0:T(8,128)(2,1)S(1)} %copy-done, bf16[8,128,256]{2,1,0:T(8,128)(2,1)S(1)} %collective-permute-done.4.sibling_ref, bf16[8,128,256]{2,1,0:T(8,128)(2,1)S(1)} %collective-permute-done.2.pair_ref, f32[128,256]{1,0:T(8,128)S(1)} %project_first.1.part_ref), custom_call_target="tpu_custom_call" | custom-call | flops 134217728 | bytes 2097152 | tf_op jit(solution)/shard_map/project_second/pallas_call | solution.py:238
  100.4 0.0 collective-permute-done.3.sibling_ref
  100.4 1.5 %project_third.1 = bf16[128,256]{1,0:T(8,128)(2,1)} custom-call(s32[2,64]{1,0:T(2,128)S(1)} %bitcast.3, bf16[8192,256]{1,0:T(8,128)(2,1)S(1)} %copy-done, bf16[8,128,256]{2,1,0:T(8,128)(2,1)S(1)} %collective-permute-done.3.sibling_ref, f32[128,256]{1,0:T(8,128)S(1)} %project_second.1.part_ref), custom_call_target="tpu_custom_call" | custom-call | flops 134217728 | bytes 2097152 | tf_op jit(solution)/shard_map/project_third/pallas_call | solution.py:238
  (1 shorter events, 0.0 us)
Async XLA Ops:
  0.0 17.2 %collective-permute-start = (bf16[128,256]{1,0:T(8,128)(2,1)}, bf16[128,256]{1,0:T(8,128)(2,1)S(1)}, u32[]{:S(2)}, u32[]{:S(2)}) collective-permute-start(bf16[128,256]{1,0:T(8,128)(2,1)} %queries_ref.1), channel_id=1, source_target_pairs={{0,2},{2,0},{1,3},{3,1},{4,6},{6,4},{5,7},{7,5},{8,10},{10,8},{9,1... | collective-permute-start | bytes 196616 | tf_op jit(solution)/shard_map/ppermute | solution.py:184
  9.5 18.6 %all-to-all-start = ((bf16[32,16,256]{2,1,0:T(8,128)(2,1)}), bf16[32,16,256]{2,1,0:T(8,128)(2,1)S(1)}, u32[]{:S(2)}, u32[]{:S(2)}) async-start(bf16[32,16,256]{2,1,0:T(8,128)(2,1)} %spread_kv.1), calls=%async_computation | async-start | bytes 524288 | tf_op jit(solution)/shard_map/all_to_all | solution.py:193
  17.3 0.8 copy-start.2
  18.1 80.2 %copy-start.1 = (s32[64,2]{0,1:T(2,128)S(1)}, s32[64,2]{0,1:T(2,128)}, u32[]{:S(2)}) copy-start(s32[64,2]{0,1:T(2,128)} %param.9) | copy-start | bytes 1540
  28.1 70.3 %copy-start = (bf16[8192,256]{1,0:T(8,128)(2,1)S(1)}, bf16[8192,256]{1,0:T(8,128)(2,1)}, u32[]{:S(2)}) copy-start(bf16[8192,256]{1,0:T(8,128)(2,1)} %weight_ref.5) | copy-start | bytes 12582916
  42.0 8.3 %collective-permute-start.1 = (bf16[4,32,16,256]{3,2,1,0:T(8,128)(2,1)S(1)}, bf16[4,32,16,256]{3,2,1,0:T(8,128)(2,1)S(1)}, u32[]{:S(2)}, u32[]{:S(2)}) collective-permute-start(bf16[4,32,16,256]{3,2,1,0:T(8,128)(2,1)S(1)} %all_to_all.15.kv_ref), channel_id=1, source_target_pairs={{0,1},{1,0},{2,3},{3,2},{4,5},{5,4},{6,7},{7,6},{8,9},{9,8},{10,11... | collective-permute-start | bytes 3145736 | tf_op jit(solution)/shard_map/ppermute | solution.py:213
  84.8 11.1 %collective-permute-start.2 = (bf16[8,128,256]{2,1,0:T(8,128)(2,1)S(1)}, bf16[8,128,256]{2,1,0:T(8,128)(2,1)S(1)}, u32[]{:S(2)}, u32[]{:S(2)}) collective-permute-start(bf16[8,128,256]{2,1,0:T(8,128)(2,1)S(1)} %all_to_all.16.self_ref), channel_id=1, source_target_pairs={{0,4},{1,29},{4,0},{5,9},{8,12},{9,5},{12,8},{13,17},{16,20},{17,1... | collective-permute-start | bytes 1572872 | tf_op jit(solution)/shard_map/ppermute | solution.py:233
  86.8 12.5 %collective-permute-start.4 = (bf16[8,128,256]{2,1,0:T(8,128)(2,1)S(1)}, bf16[8,128,256]{2,1,0:T(8,128)(2,1)S(1)}, u32[]{:S(2)}, u32[]{:S(2)}) collective-permute-start(bf16[8,128,256]{2,1,0:T(8,128)(2,1)S(1)} %all_to_all.16.self_ref), channel_id=1, source_target_pairs={{0,1},{1,0},{2,3},{3,2},{4,5},{5,4},{6,7},{7,6},{8,9},{9,8},{10,11... | collective-permute-start | bytes 1572872 | tf_op jit(solution)/shard_map/ppermute | solution.py:234
  96.0 4.4 %collective-permute-start.3 = (bf16[8,128,256]{2,1,0:T(8,128)(2,1)S(1)}, bf16[8,128,256]{2,1,0:T(8,128)(2,1)S(1)}, u32[]{:S(2)}, u32[]{:S(2)}) collective-permute-start(bf16[8,128,256]{2,1,0:T(8,128)(2,1)S(1)} %collective-permute-done.2.pair_ref), channel_id=1, source_target_pairs={{0,1},{1,0},{2,3},{3,2},{4,5},{5,4},{6,7},{7,6},{8,9},{9,8},{10,11... | collective-permute-start | bytes 1572872 | tf_op jit(solution)/shard_map/ppermute | solution.py:235

commit v10 on v7

--- a/solution.py
+++ b/solution.py
@@ -1,3 +1,4 @@
+import functools
 import math
 
 import jax
@@ -21,6 +22,7 @@
 N_Z = 8
 FACTOR = math.log2(math.e) / math.sqrt(HD)
 LOWEST = -1e30
+CHUNK = 256
 ANY = pl.BlockSpec(memory_space=pl.ANY)
 VMEM = pl.BlockSpec(memory_space=pltpu.VMEM)
 SMEM = pl.BlockSpec(memory_space=pltpu.SMEM)
@@ -84,20 +86,27 @@
     start = (seq + lax.axis_index("xp")) * rows
     q = jnp.concatenate([queries_ref[:, :HD], queries_ref[:, HD:]], axis=0)
     query_pos = start + lax.broadcasted_iota(jnp.int32, (2 * rows, 1), 0) % rows
-    column = lax.broadcasted_iota(jnp.int32, (1, width), 1)
-    block = column // part
-    place = block // N_SEQ * 2 + from_core
-    key_pos = block % N_SEQ * rows + place * part + column % part
-    key = kv_ref[:, :, :, :HD].reshape(width, HD)
-    value = kv_ref[:, :, :, HD:].reshape(width, HD)
-    score = lax.dot_general(q, key, (((1,), (1,)), ((), ())), preferred_element_type=jnp.float32)
-    score = jnp.where(query_pos >= key_pos, score, jnp.float32(LOWEST))
-    top = jnp.max(score, axis=1, keepdims=True)
-    if state is not None:
-        top = jnp.maximum(state[0], top)
-    expo = jnp.exp2((score - top) * FACTOR)
-    total = jnp.sum(expo, axis=1, keepdims=True)
-    summed = jnp.dot(expo.astype(jnp.bfloat16), value, preferred_element_type=jnp.float32)
+    chunks = []
+    for first in range(0, width, CHUNK):
+        place, entry = divmod(first // part, N_SEQ)
+        entries = kv_ref[place, entry : entry + CHUNK // part]
+        column = first + lax.broadcasted_iota(jnp.int32, (1, CHUNK), 1)
+        block = column // part
+        token = (place * 2 + from_core) * part + column % part
+        key_pos = block % N_SEQ * rows + token
+        key = entries[:, :, :HD].reshape(CHUNK, HD)
+        score = lax.dot_general(q, key, (((1,), (1,)), ((), ())), preferred_element_type=jnp.float32)
+        score = jnp.where(query_pos >= key_pos, score, jnp.float32(LOWEST))
+        chunks.append((score, entries[:, :, HD:].reshape(CHUNK, HD)))
+    tops = [jnp.max(score, axis=1, keepdims=True) for score, _ in chunks]
+    top = functools.reduce(jnp.maximum, tops if state is None else tops + [state[0]])
+    total = summed = 0.0
+    for score, value in chunks:
+        expo = jnp.exp2((score - top) * FACTOR)
+        total = total + jnp.sum(expo, axis=1, keepdims=True)
+        summed = summed + jnp.dot(
+            expo.astype(jnp.bfloat16), value, preferred_element_type=jnp.float32
+        )
     if state is not None:
         fix = jnp.exp2((state[0] - top) * FACTOR)
         total = total + state[1] * fix
@@ -217,7 +226,6 @@
     along_z = lax.all_to_all(heads, "z", 0, 0, tiled=True)
     from_pair = lax.ppermute(along_z, RING, z_pairs())
     sibling = lax.ppermute(along_z, "core", swap)
-    pair_sibling = lax.ppermute(from_pair, "core", swap)
 
     def call(kernel, name, dtype, *arrays):
         return pl.pallas_call(
@@ -231,6 +239,8 @@
         )(mask, out_weight, *arrays)
 
     first = call(project_first_kernel, "project_first", jnp.float32, along_z)
+    from_pair, first = lax.optimization_barrier((from_pair, first))
+    pair_sibling = lax.ppermute(from_pair, "core", swap)
     second = call(project_second_kernel, "project_second", jnp.float32, sibling, from_pair, first)
     return call(project_third_kernel, "project_third", jnp.bfloat16, pair_sibling, second)
 

time: 98.4 us -> 97.6 us (level)
  transfers between devices with their start and end apart: 6 -> 6, of which waited for: 4 -> 5; matrix products, arithmetic and copies ran while one was open for 0% -> 0% of each run, Pallas kernels for 4% -> 4%
where the time goes in v10:
time: 97.6 us; the launch traced here: 97.2 us
  blocking collectives  46.1 us (47%)
  starting transfers between devices  29.5 us (30%)
  waiting for transfers between devices  12.6 us (13%)
  Pallas kernels  8.83 us (9%)
    all_to_all x1, blocking collectives, per_device(): along_z = lax.all_to_all(heads, 'z', 0, 0, tiled=True)  30.2 us
    all_to_all x1, blocking collectives, per_device(): lax.all_to_all(square, PLANE, 0, 0, axis_index_groups=square_groups(), ti...  15.9 us
    all_to_all x1, starting transfers between devices, per_device(): piece = lax.all_to_all(spread, SEQ, 0, 0, tiled=True)  11.3 us
    ppermute x1, starting transfers between devices, per_device(): other = lax.ppermute(own, 'core', swap)  6.47 us
    ppermute x1, waiting for transfers between devices, per_device(): from_pair = lax.ppermute(along_z, RING, z_pairs())  5.26 us
    ppermute x1, waiting for transfers between devices, per_device(): partner_queries = lax.ppermute(queries, 'xh', swap)  4.81 us
    ppermute x1, starting transfers between devices, per_device(): partner_queries = lax.ppermute(queries, 'xh', swap)  4.42 us
    pallas_call x3, Pallas kernels, call(): pl.pallas_call(kernel, out_shape=shape((rows, columns), dtype), in_specs=...  3.49 us
  transfers between devices with their start and end apart: 6, of which 5 were waited for; matrix products, arithmetic and copies ran while one was open for 0% of the time, Pallas kernels for 4%

profile of v10, /device:TPU:1, one launch (start us, length us, event | category | flops | bytes accessed | tf_op | source)
XLA Modules:
  0.0 97.2 jit_solution(15959166551527930116)
XLA Ops:
  0.0 0.0 copy-start.1
  0.0 1.6 %spread_kv.1 = bf16[32,16,256]{2,1,0:T(8,128)(2,1)} custom-call(bf16[128,1024]{1,0:T(8,128)(2,1)} %keys_ref.1, bf16[128,1024]{1,0:T(8,128)(2,1)} %values_ref.1), custom_call_target="tpu_custom_call" | custom-call | tf_op jit(solution)/shard_map/spread_kv/pallas_call | solution.py:188
  1.6 11.3 %all-to-all-start = ((bf16[32,16,256]{2,1,0:T(8,128)(2,1)}), bf16[32,16,256]{2,1,0:T(8,128)(2,1)S(1)}, u32[]{:S(2)}, u32[]{:S(2)}) async-start(bf16[32,16,256]{2,1,0:T(8,128)(2,1)} %spread_kv.1), calls=%async_computation | async-start | bytes 524288 | tf_op jit(solution)/shard_map/all_to_all | solution.py:196
  12.9 0.0 copy-start.2
  12.9 4.4 %collective-permute-start = (bf16[128,256]{1,0:T(8,128)(2,1)}, bf16[128,256]{1,0:T(8,128)(2,1)S(1)}, u32[]{:S(2)}, u32[]{:S(2)}) collective-permute-start(bf16[128,256]{1,0:T(8,128)(2,1)} %queries_ref.3), channel_id=1, source_target_pairs={{0,2},{2,0},{1,3},{3,1},{4,6},{6,4},{5,7},{7,5},{8,10},{10,8},{9,1... | collective-permute-start | bytes 196616 | tf_op jit(solution)/shard_map/ppermute | solution.py:187
  17.3 4.8 %collective-permute-done.partner_ref = bf16[128,256]{1,0:T(8,128)(2,1)S(1)} collective-permute-done((bf16[128,256]{1,0:T(8,128)(2,1)}, bf16[128,256]{1,0:T(8,128)(2,1)S(1)}, u32[]{:S(2)}, u32[]{:S(2)}) %collective-permute-start) | collective-permute-done | bytes 65568 | tf_op jit(solution)/shard_map/ppermute | solution.py:187
  22.1 1.6 %all-to-all-done.piece_ref = bf16[32,16,256]{2,1,0:T(8,128)(2,1)S(1)} async-done(((bf16[32,16,256]{2,1,0:T(8,128)(2,1)}), bf16[32,16,256]{2,1,0:T(8,128)(2,1)S(1)}, u32[]{:S(2)}, u32[]{:S(2)}) %all-to-all-start) | async-done | bytes 262176 | tf_op jit(solution)/shard_map/all_to_all | solution.py:196
  23.7 0.0 copy-start
  23.8 0.1 square.1
  23.8 15.9 %all_to_all.15.kv_ref = bf16[4,32,16,256]{3,2,1,0:T(8,128)(2,1)S(1)} all-to-all(bf16[4,32,16,256]{3,2,1,0:T(8,128)(2,1)S(1)} %square.1), channel_id=1, replica_groups={{0,32,128,160},{64,96,192,224},{2,34,130,162},{66,98,194,226},{256,288,..., dimensions={0} | all-to-all | bytes 2097152 | tf_op jit(solution)/shard_map/all_to_all | solution.py:206
  39.7 6.5 %collective-permute-start.1 = (bf16[4,32,16,256]{3,2,1,0:T(8,128)(2,1)S(1)}, bf16[4,32,16,256]{3,2,1,0:T(8,128)(2,1)S(1)}, u32[]{:S(2)}, u32[]{:S(2)}) collective-permute-start(bf16[4,32,16,256]{3,2,1,0:T(8,128)(2,1)S(1)} %all_to_all.15.kv_ref), channel_id=1, source_target_pairs={{0,1},{1,0},{2,3},{3,2},{4,5},{5,4},{6,7},{7,6},{8,9},{9,8},{10,11... | collective-permute-start | bytes 3145736 | tf_op jit(solution)/shard_map/ppermute | solution.py:207
  46.2 0.0 copy-done.1
  46.2 1.8 %attention_first.1 = (f32[2,256,128]{2,1,0:T(8,128)S(1)}, f32[2,256,128]{2,1,0:T(8,128)S(1)}, f32[2,256,128]{2,1,0:T(8,128)S(1)}) custom-call(bf16[128,256]{1,0:T(8,128)(2,1)S(1)} %copy-done.1, bf16[128,256]{1,0:T(8,128)(2,1)S(1)} %collective-permute-done.partner_ref, bf16[4,32,16,256]{3,2,1,0:T(8,128)(2,1)S(1)} %all_to_all.15.kv_ref), custom_call_target="tpu_custom_call" | custom-call | flops 536870912 | bytes 2097152 | tf_op jit(solution)/shard_map/attention_first/pallas_call | solution.py:208
  47.9 0.5 collective-permute-done.1.kv_ref
  48.4 2.0 %attention_second.1 = bf16[8,128,256]{2,1,0:T(8,128)(2,1)S(1)} custom-call(bf16[128,256]{1,0:T(8,128)(2,1)S(1)} %copy-done.1, bf16[128,256]{1,0:T(8,128)(2,1)S(1)} %collective-permute-done.partner_ref, bf16[4,32,16,256]{3,2,1,0:T(8,128)(2,1)S(1)} %collective-permute-done.1.kv_ref, f32[2,256,128]{2,1,0:T(8,128)S(1)} %get-tuple-element.14.top_ref, ...), custom_call_target="tpu_custom_call" | custom-call | flops 536870912 | bytes 2097152 | tf_op jit(solution)/shard_map/attention_second/pallas_call | solution.py:217
  50.4 30.2 %all_to_all.16.self_ref = bf16[8,128,256]{2,1,0:T(8,128)(2,1)S(1)} all-to-all(bf16[8,128,256]{2,1,0:T(8,128)(2,1)S(1)} %attention_second.1), channel_id=1, replica_groups=mesh['y'=4,'yp'=2,'xl'=2,'xp'=2,'z'=8,'xh'=2,'core'=2] {'z'}, dimensions={0} | all-to-all | bytes 1048576 | tf_op jit(solution)/shard_map/all_to_all | solution.py:226
  80.6 1.9 %collective-permute-start.2 = (bf16[8,128,256]{2,1,0:T(8,128)(2,1)S(1)}, bf16[8,128,256]{2,1,0:T(8,128)(2,1)S(1)}, u32[]{:S(2)}, u32[]{:S(2)}) collective-permute-start(bf16[8,128,256]{2,1,0:T(8,128)(2,1)S(1)} %all_to_all.16.self_ref), channel_id=1, source_target_pairs={{0,4},{1,29},{4,0},{5,9},{8,12},{9,5},{12,8},{13,17},{16,20},{17,1... | collective-permute-start | bytes 1572872 | tf_op jit(solution)/shard_map/ppermute | solution.py:227
  82.5 3.0 %collective-permute-start.4 = (bf16[8,128,256]{2,1,0:T(8,128)(2,1)S(1)}, bf16[8,128,256]{2,1,0:T(8,128)(2,1)S(1)}, u32[]{:S(2)}, u32[]{:S(2)}) collective-permute-start(bf16[8,128,256]{2,1,0:T(8,128)(2,1)S(1)} %all_to_all.16.self_ref), channel_id=1, source_target_pairs={{0,1},{1,0},{2,3},{3,2},{4,5},{5,4},{6,7},{7,6},{8,9},{9,8},{10,11... | collective-permute-start | bytes 1572872 | tf_op jit(solution)/shard_map/ppermute | solution.py:228
  85.5 0.0 copy-done.2
  85.5 0.0 copy-done
  85.6 0.9 project_first.1.part_ref
  86.5 5.3 %collective-permute-done.2.pair_ref = bf16[8,128,256]{2,1,0:T(8,128)(2,1)S(1)} collective-permute-done((bf16[8,128,256]{2,1,0:T(8,128)(2,1)S(1)}, bf16[8,128,256]{2,1,0:T(8,128)(2,1)S(1)}, u32[]{:S(2)}, u32[]{:S(2)}) %collective-permute-start.2) | collective-permute-done | bytes 524320 | tf_op jit(solution)/shard_map/ppermute | solution.py:227
  91.7 2.4 %collective-permute-start.3 = (bf16[8,128,256]{2,1,0:T(8,128)(2,1)S(1)}, bf16[8,128,256]{2,1,0:T(8,128)(2,1)S(1)}, u32[]{:S(2)}, u32[]{:S(2)}) collective-permute-start(bf16[8,128,256]{2,1,0:T(8,128)(2,1)S(1)} %collective-permute-done.2.pair_ref), channel_id=1, source_target_pairs={{0,1},{1,0},{2,3},{3,2},{4,5},{5,4},{6,7},{7,6},{8,9},{9,8},{10,11... | collective-permute-start | bytes 1572872 | tf_op jit(solution)/shard_map/ppermute | solution.py:243
  94.1 0.0 collective-permute-done.4.sibling_ref
  94.1 1.1 %project_second.1.part_ref = f32[128,256]{1,0:T(8,128)S(1)} custom-call(s32[2,64]{1,0:T(2,128)S(1)} %bitcast.2, bf16[8192,256]{1,0:T(8,128)(2,1)S(1)} %copy-done, bf16[8,128,256]{2,1,0:T(8,128)(2,1)S(1)} %collective-permute-done.4.sibling_ref, bf16[8,128,256]{2,1,0:T(8,128)(2,1)S(1)} %collective-permute-done.2.pair_ref, f32[128,256]{1,0:T(8,128)S(1)} %project_first.1.part_ref), custom_call_target="tpu_custom_call" | custom-call | flops 134217728 | bytes 2097152 | tf_op jit(solution)/shard_map/project_second/pallas_call | solution.py:231
  95.2 0.4 collective-permute-done.3.sibling_ref
  95.6 1.5 %project_third.1 = bf16[128,256]{1,0:T(8,128)(2,1)} custom-call(s32[2,64]{1,0:T(2,128)S(1)} %bitcast.3, bf16[8192,256]{1,0:T(8,128)(2,1)S(1)} %copy-done, bf16[8,128,256]{2,1,0:T(8,128)(2,1)S(1)} %collective-permute-done.3.sibling_ref, f32[128,256]{1,0:T(8,128)S(1)} %project_second.1.part_ref), custom_call_target="tpu_custom_call" | custom-call | flops 134217728 | bytes 2097152 | tf_op jit(solution)/shard_map/project_third/pallas_call | solution.py:231
Async XLA Ops:
  0.0 46.2 %copy-start.1 = (bf16[128,256]{1,0:T(8,128)(2,1)S(1)}, bf16[128,256]{1,0:T(8,128)(2,1)}, u32[]{:S(2)}) copy-start(bf16[128,256]{1,0:T(8,128)(2,1)} %queries_ref.3) | copy-start | bytes 196612
  1.6 22.2 %all-to-all-start = ((bf16[32,16,256]{2,1,0:T(8,128)(2,1)}), bf16[32,16,256]{2,1,0:T(8,128)(2,1)S(1)}, u32[]{:S(2)}, u32[]{:S(2)}) async-start(bf16[32,16,256]{2,1,0:T(8,128)(2,1)} %spread_kv.1), calls=%async_computation | async-start | bytes 524288 | tf_op jit(solution)/shard_map/all_to_all | solution.py:196
  12.9 72.7 %copy-start.2 = (s32[64,2]{0,1:T(2,128)S(1)}, s32[64,2]{0,1:T(2,128)}, u32[]{:S(2)}) copy-start(s32[64,2]{0,1:T(2,128)} %param.9) | copy-start | bytes 1540
  12.9 9.2 %collective-permute-start = (bf16[128,256]{1,0:T(8,128)(2,1)}, bf16[128,256]{1,0:T(8,128)(2,1)S(1)}, u32[]{:S(2)}, u32[]{:S(2)}) collective-permute-start(bf16[128,256]{1,0:T(8,128)(2,1)} %queries_ref.3), channel_id=1, source_target_pairs={{0,2},{2,0},{1,3},{3,1},{4,6},{6,4},{5,7},{7,5},{8,10},{10,8},{9,1... | collective-permute-start | bytes 196616 | tf_op jit(solution)/shard_map/ppermute | solution.py:187
  23.7 61.8 %copy-start = (bf16[8192,256]{1,0:T(8,128)(2,1)S(1)}, bf16[8192,256]{1,0:T(8,128)(2,1)}, u32[]{:S(2)}) copy-start(bf16[8192,256]{1,0:T(8,128)(2,1)} %weight_ref.5) | copy-start | bytes 12582916
  39.7 8.7 %collective-permute-start.1 = (bf16[4,32,16,256]{3,2,1,0:T(8,128)(2,1)S(1)}, bf16[4,32,16,256]{3,2,1,0:T(8,128)(2,1)S(1)}, u32[]{:S(2)}, u32[]{:S(2)}) collective-permute-start(bf16[4,32,16,256]{3,2,1,0:T(8,128)(2,1)S(1)} %all_to_all.15.kv_ref), channel_id=1, source_target_pairs={{0,1},{1,0},{2,3},{3,2},{4,5},{5,4},{6,7},{7,6},{8,9},{9,8},{10,11... | collective-permute-start | bytes 3145736 | tf_op jit(solution)/shard_map/ppermute | solution.py:207
  80.6 11.1 %collective-permute-start.2 = (bf16[8,128,256]{2,1,0:T(8,128)(2,1)S(1)}, bf16[8,128,256]{2,1,0:T(8,128)(2,1)S(1)}, u32[]{:S(2)}, u32[]{:S(2)}) collective-permute-start(bf16[8,128,256]{2,1,0:T(8,128)(2,1)S(1)} %all_to_all.16.self_ref), channel_id=1, source_target_pairs={{0,4},{1,29},{4,0},{5,9},{8,12},{9,5},{12,8},{13,17},{16,20},{17,1... | collective-permute-start | bytes 1572872 | tf_op jit(solution)/shard_map/ppermute | solution.py:227
  82.5 11.6 %collective-permute-start.4 = (bf16[8,128,256]{2,1,0:T(8,128)(2,1)S(1)}, bf16[8,128,256]{2,1,0:T(8,128)(2,1)S(1)}, u32[]{:S(2)}, u32[]{:S(2)}) collective-permute-start(bf16[8,128,256]{2,1,0:T(8,128)(2,1)S(1)} %all_to_all.16.self_ref), channel_id=1, source_target_pairs={{0,1},{1,0},{2,3},{3,2},{4,5},{5,4},{6,7},{7,6},{8,9},{9,8},{10,11... | collective-permute-start | bytes 1572872 | tf_op jit(solution)/shard_map/ppermute | solution.py:228
  91.7 3.9 %collective-permute-start.3 = (bf16[8,128,256]{2,1,0:T(8,128)(2,1)S(1)}, bf16[8,128,256]{2,1,0:T(8,128)(2,1)S(1)}, u32[]{:S(2)}, u32[]{:S(2)}) collective-permute-start(bf16[8,128,256]{2,1,0:T(8,128)(2,1)S(1)} %collective-permute-done.2.pair_ref), channel_id=1, source_target_pairs={{0,1},{1,0},{2,3},{3,2},{4,5},{5,4},{6,7},{7,6},{8,9},{9,8},{10,11... | collective-permute-start | bytes 1572872 | tf_op jit(solution)/shard_map/ppermute | solution.py:243

commit v11 on v10

--- a/solution.py
+++ b/solution.py
@@ -140,38 +140,39 @@
         out_ref[i] = heads[i % 2]
 
 
-def project(mask_ref, heads_ref, weight_ref, of_pair, of_sibling):
-    columns = weight_ref.shape[1]
+def prune_kernel(mask_ref, weight_ref, out_ref):
+    rows, columns = weight_ref.shape
+    for block in range(rows // BLOCK):
+        for j in range(columns // BLOCK):
+            at = slice(block * BLOCK, (block + 1) * BLOCK), slice(j * BLOCK, (j + 1) * BLOCK)
+            keep = mask_ref[j, block].astype(jnp.float32).astype(jnp.bfloat16)
+            out_ref[at] = weight_ref[at] * keep
+
+
+def project(heads_ref, weight_ref, of_pair, of_sibling):
     parity, core = lax.rem(lax.axis_index("z"), 2), lax.axis_index("core")
     from_chip = 1 - parity if of_pair else parity
     from_core = 1 - core if of_sibling else core
-    total = jnp.zeros((heads_ref.shape[1], columns), jnp.float32)
+    width = heads_ref.shape[2]
+    total = jnp.zeros((heads_ref.shape[1], weight_ref.shape[1]), jnp.float32)
     for z in range(N_Z):
-        rows = []
-        for i in range(2):
-            block = ((z * 2 + from_chip) * 2 + from_core) * 2 + i
-            at = pl.ds(pl.multiple_of(block * BLOCK, BLOCK), BLOCK)
-            line = []
-            for j in range(columns // BLOCK):
-                keep = mask_ref[j, block].astype(jnp.float32).astype(jnp.bfloat16)
-                line.append(weight_ref[at, j * BLOCK : (j + 1) * BLOCK] * keep)
-            rows.append(jnp.concatenate(line, axis=1))
-        pruned = jnp.concatenate(rows, axis=0)
-        total += jnp.dot(heads_ref[z], pruned, preferred_element_type=jnp.float32)
+        part = (z * 2 + from_chip) * 2 + from_core
+        rows = weight_ref[pl.ds(pl.multiple_of(part * width, width), width), :]
+        total += jnp.dot(heads_ref[z], rows, preferred_element_type=jnp.float32)
     return total
 
 
-def project_first_kernel(mask_ref, weight_ref, self_ref, out_ref):
-    out_ref[...] = project(mask_ref, self_ref, weight_ref, False, False)
-
-
-def project_second_kernel(mask_ref, weight_ref, sibling_ref, pair_ref, part_ref, out_ref):
-    part = part_ref[...] + project(mask_ref, sibling_ref, weight_ref, False, True)
-    out_ref[...] = part + project(mask_ref, pair_ref, weight_ref, True, False)
-
-
-def project_third_kernel(mask_ref, weight_ref, sibling_ref, part_ref, out_ref):
-    part = part_ref[...] + project(mask_ref, sibling_ref, weight_ref, True, True)
+def project_first_kernel(weight_ref, self_ref, out_ref):
+    out_ref[...] = project(self_ref, weight_ref, False, False)
+
+
+def project_second_kernel(weight_ref, sibling_ref, pair_ref, part_ref, out_ref):
+    part = part_ref[...] + project(sibling_ref, weight_ref, False, True)
+    out_ref[...] = part + project(pair_ref, weight_ref, True, False)
+
+
+def project_third_kernel(weight_ref, sibling_ref, part_ref, out_ref):
+    part = part_ref[...] + project(sibling_ref, weight_ref, True, True)
     out_ref[...] = part.astype(out_ref.dtype)
 
 
@@ -223,7 +224,18 @@
         cost_estimate=cost,
         name="attention_second",
     )(queries, partner_queries, other, *state)
+    heads, mask = lax.optimization_barrier((heads, mask))
+    pruned = pl.pallas_call(
+        prune_kernel,
+        out_shape=shape(out_weight.shape, jnp.bfloat16),
+        in_specs=[SMEM, VMEM],
+        out_specs=VMEM,
+        compiler_params=params,
+        cost_estimate=pl.CostEstimate(flops=2**30, bytes_accessed=2**23, transcendentals=0),
+        name="prune",
+    )(mask, out_weight)
     along_z = lax.all_to_all(heads, "z", 0, 0, tiled=True)
+    along_z, pruned = lax.optimization_barrier((along_z, pruned))
     from_pair = lax.ppermute(along_z, RING, z_pairs())
     sibling = lax.ppermute(along_z, "core", swap)
 
@@ -231,12 +243,12 @@
         return pl.pallas_call(
             kernel,
             out_shape=shape((rows, columns), dtype),
-            in_specs=[SMEM] + [VMEM] * (1 + len(arrays)),
+            in_specs=[VMEM] * (1 + len(arrays)),
             out_specs=VMEM,
             compiler_params=params,
             cost_estimate=pl.CostEstimate(flops=2**27, bytes_accessed=2**21, transcendentals=0),
             name=name,
-        )(mask, out_weight, *arrays)
+        )(pruned, *arrays)
 
     first = call(project_first_kernel, "project_first", jnp.float32, along_z)
     from_pair, first = lax.optimization_barrier((from_pair, first))

time: 97.6 us -> 97.9 us (level)
  blocking collectives: 46.1 us -> 15.6 us
  starting transfers between devices: 29.5 us -> 41.9 us
  waiting for transfers between devices: 12.6 us -> 24.2 us
  local copies, waits for them, and re-layouts: 0.01 us -> 6.31 us
    all_to_all x1 -> x0, blocking collectives: 30.2 us -> none  [per_device(): along_z = lax.all_to_all(heads, 'z', 0, 0, tiled=True)]
    all_to_all x0 -> x1, starting transfers between devices: none -> 12.5 us  [per_device(): along_z = lax.all_to_all(heads, 'z', 0, 0, tiled=True)]
    all_to_all x0 -> x1, waiting for transfers between devices: none -> 12.4 us  [per_device(): along_z = lax.all_to_all(heads, 'z', 0, 0, tiled=True)]
    unnamed x6 -> x10, local copies, waits for them, and re-layouts: 0.01 us -> 6.31 us
    pallas_call x3, Pallas kernels: 3.49 us -> 1.72 us  [call(): pl.pallas_call(kernel, out_shape=shape((rows, columns), dtype), in_specs=...]
    ppermute x1, waiting for transfers between devices: 5.26 us -> 3.74 us  [per_device(): from_pair = lax.ppermute(along_z, RING, z_pairs())]
    pallas_call x0 -> x1, Pallas kernels: none -> 1.37 us  [per_device(): pl.pallas_call(prune_kernel, out_shape=shape(out_weight.shape, jnp.bfloat...]
  transfers between devices with their start and end apart: 6 -> 7, of which waited for: 5 -> 6; matrix products, arithmetic and copies ran while one was open for 0% -> 0% of each run, Pallas kernels for 4% -> 4%
where the time goes in v11:
time: 97.9 us; the launch traced here: 97.3 us
  starting transfers between devices  41.9 us (43%)
  waiting for transfers between devices  24.2 us (25%)
  blocking collectives  15.6 us (16%)
  Pallas kernels  9.26 us (9%)
  local copies, waits for them, and re-layouts  6.31 us (6%)
    all_to_all x1, blocking collectives, per_device(): lax.all_to_all(square, PLANE, 0, 0, axis_index_groups=square_groups(), ti...  15.6 us
    all_to_all x1, starting transfers between devices, per_device(): along_z = lax.all_to_all(heads, 'z', 0, 0, tiled=True)  12.5 us
    all_to_all x1, waiting for transfers between devices, per_device(): along_z = lax.all_to_all(heads, 'z', 0, 0, tiled=True)  12.4 us
    all_to_all x1, starting transfers between devices, per_device(): piece = lax.all_to_all(spread, SEQ, 0, 0, tiled=True)  11.3 us
    ppermute x1, starting transfers between devices, per_device(): other = lax.ppermute(own, 'core', swap)  6.47 us
    unnamed x10, local copies, waits for them, and re-layouts  6.31 us
    ppermute x1, waiting for transfers between devices, per_device(): partner_queries = lax.ppermute(queries, 'xh', swap)  4.81 us
    ppermute x1, starting transfers between devices, per_device(): partner_queries = lax.ppermute(queries, 'xh', swap)  4.42 us
  transfers between devices with their start and end apart: 7, of which 6 were waited for; matrix products, arithmetic and copies ran while one was open for 0% of the time, Pallas kernels for 4%

profile of v11, /device:TPU:1, one launch (start us, length us, event | category | flops | bytes accessed | tf_op | source)
XLA Modules:
  0.0 97.3 jit_solution(1347650834199404449)
XLA Ops:
  0.0 0.0 copy-start.3
  0.0 1.5 %spread_kv.1 = bf16[32,16,256]{2,1,0:T(8,128)(2,1)} custom-call(bf16[128,1024]{1,0:T(8,128)(2,1)} %keys_ref.1, bf16[128,1024]{1,0:T(8,128)(2,1)} %values_ref.1), custom_call_target="tpu_custom_call" | custom-call | tf_op jit(solution)/shard_map/spread_kv/pallas_call | solution.py:189
  1.6 11.3 %all-to-all-start = ((bf16[32,16,256]{2,1,0:T(8,128)(2,1)}), bf16[32,16,256]{2,1,0:T(8,128)(2,1)S(1)}, u32[]{:S(2)}, u32[]{:S(2)}) async-start(bf16[32,16,256]{2,1,0:T(8,128)(2,1)} %spread_kv.1), calls=%async_computation | async-start | bytes 524288 | tf_op jit(solution)/shard_map/all_to_all | solution.py:197
  12.9 0.0 copy-start.4
  12.9 4.4 %collective-permute-start = (bf16[128,256]{1,0:T(8,128)(2,1)}, bf16[128,256]{1,0:T(8,128)(2,1)S(1)}, u32[]{:S(2)}, u32[]{:S(2)}) collective-permute-start(bf16[128,256]{1,0:T(8,128)(2,1)} %queries_ref.3), channel_id=1, source_target_pairs={{0,2},{2,0},{1,3},{3,1},{4,6},{6,4},{5,7},{7,5},{8,10},{10,8},{9,1... | collective-permute-start | bytes 196616 | tf_op jit(solution)/shard_map/ppermute | solution.py:188
  17.3 4.8 %collective-permute-done.partner_ref = bf16[128,256]{1,0:T(8,128)(2,1)S(1)} collective-permute-done((bf16[128,256]{1,0:T(8,128)(2,1)}, bf16[128,256]{1,0:T(8,128)(2,1)S(1)}, u32[]{:S(2)}, u32[]{:S(2)}) %collective-permute-start) | collective-permute-done | bytes 65568 | tf_op jit(solution)/shard_map/ppermute | solution.py:188
  22.1 1.6 %all-to-all-done.piece_ref = bf16[32,16,256]{2,1,0:T(8,128)(2,1)S(1)} async-done(((bf16[32,16,256]{2,1,0:T(8,128)(2,1)}), bf16[32,16,256]{2,1,0:T(8,128)(2,1)S(1)}, u32[]{:S(2)}, u32[]{:S(2)}) %all-to-all-start) | async-done | bytes 262176 | tf_op jit(solution)/shard_map/all_to_all | solution.py:197
  23.7 0.1 square.1
  23.8 15.6 %all_to_all.15.kv_ref = bf16[4,32,16,256]{3,2,1,0:T(8,128)(2,1)S(1)} all-to-all(bf16[4,32,16,256]{3,2,1,0:T(8,128)(2,1)S(1)} %square.1), channel_id=1, replica_groups={{0,32,128,160},{64,96,192,224},{2,34,130,162},{66,98,194,226},{256,288,..., dimensions={0} | all-to-all | bytes 2097152 | tf_op jit(solution)/shard_map/all_to_all | solution.py:207
  39.4 6.5 %collective-permute-start.1 = (bf16[4,32,16,256]{3,2,1,0:T(8,128)(2,1)S(1)}, bf16[4,32,16,256]{3,2,1,0:T(8,128)(2,1)S(1)}, u32[]{:S(2)}, u32[]{:S(2)}) collective-permute-start(bf16[4,32,16,256]{3,2,1,0:T(8,128)(2,1)S(1)} %all_to_all.15.kv_ref), channel_id=1, source_target_pairs={{0,1},{1,0},{2,3},{3,2},{4,5},{5,4},{6,7},{7,6},{8,9},{9,8},{10,11... | collective-permute-start | bytes 3145736 | tf_op jit(solution)/shard_map/ppermute | solution.py:208
  45.9 0.0 copy-done.3
  45.9 1.8 %attention_first.1 = (f32[2,256,128]{2,1,0:T(8,128)S(1)}, f32[2,256,128]{2,1,0:T(8,128)S(1)}, f32[2,256,128]{2,1,0:T(8,128)S(1)}) custom-call(bf16[128,256]{1,0:T(8,128)(2,1)S(1)} %copy-done.3, bf16[128,256]{1,0:T(8,128)(2,1)S(1)} %collective-permute-done.partner_ref, bf16[4,32,16,256]{3,2,1,0:T(8,128)(2,1)S(1)} %all_to_all.15.kv_ref), custom_call_target="tpu_custom_call" | custom-call | flops 536870912 | bytes 2097152 | tf_op jit(solution)/shard_map/attention_first/pallas_call | solution.py:209
  47.7 0.5 collective-permute-done.1.kv_ref
  48.1 2.8 %attention_second.1 = bf16[8,128,256]{2,1,0:T(8,128)(2,1)} custom-call(bf16[128,256]{1,0:T(8,128)(2,1)S(1)} %copy-done.3, bf16[128,256]{1,0:T(8,128)(2,1)S(1)} %collective-permute-done.partner_ref, bf16[4,32,16,256]{3,2,1,0:T(8,128)(2,1)S(1)} %collective-permute-done.1.kv_ref, f32[2,256,128]{2,1,0:T(8,128)S(1)} %get-tuple-element.18.top_ref, ...), custom_call_target="tpu_custom_call" | custom-call | flops 536870912 | bytes 2097152 | tf_op jit(solution)/shard_map/attention_second/pallas_call | solution.py:218
  50.9 12.5 %all-to-all-start.2 = ((bf16[8,128,256]{2,1,0:T(8,128)(2,1)}), bf16[8,128,256]{2,1,0:T(8,128)(2,1)S(1)}, u32[]{:S(2)}, u32[]{:S(2)}) async-start(bf16[8,128,256]{2,1,0:T(8,128)(2,1)} %attention_second.1), calls=%async_computation.2 | async-start | bytes 1048576 | tf_op jit(solution)/shard_map/all_to_all | solution.py:237
  63.5 0.0 copy-done.4
  63.5 0.0 copy-start.2
  63.5 2.2 %copy-done.2 = bf16[8192,256]{1,0:T(8,128)(2,1)S(1)} copy-done((bf16[8192,256]{1,0:T(8,128)(2,1)S(1)}, bf16[8192,256]{1,0:T(8,128)(2,1)}, u32[]{:S(2)}) %copy-start.2) | copy-done | bytes 4194328
  65.7 1.4 %prune.1.weight_ref = bf16[8192,256]{1,0:T(8,128)(2,1)S(1)} custom-call(s32[2,64]{1,0:T(2,128)S(1)} %bitcast.1, bf16[8192,256]{1,0:T(8,128)(2,1)S(1)} %copy-done.2), custom_call_target="tpu_custom_call" | custom-call | flops 1073741824 | bytes 8388608 | tf_op jit(solution)/shard_map/prune/pallas_call | solution.py:228
  67.0 0.0 copy-start
  67.0 1.9 %copy-done = bf16[8192,256]{1,0:T(8,128)(2,1)} copy-done((bf16[8192,256]{1,0:T(8,128)(2,1)}, bf16[8192,256]{1,0:T(8,128)(2,1)S(1)}, u32[]{:S(2)}) %copy-start) | copy-done | bytes 4194328
  69.0 12.4 %all-to-all-done.2.self_ref = bf16[8,128,256]{2,1,0:T(8,128)(2,1)S(1)} async-done(((bf16[8,128,256]{2,1,0:T(8,128)(2,1)}), bf16[8,128,256]{2,1,0:T(8,128)(2,1)S(1)}, u32[]{:S(2)}, u32[]{:S(2)}) %all-to-all-start.2) | async-done | bytes 524320 | tf_op jit(solution)/shard_map/all_to_all | solution.py:237
  81.4 1.9 %collective-permute-start.2 = (bf16[8,128,256]{2,1,0:T(8,128)(2,1)S(1)}, bf16[8,128,256]{2,1,0:T(8,128)(2,1)S(1)}, u32[]{:S(2)}, u32[]{:S(2)}) collective-permute-start(bf16[8,128,256]{2,1,0:T(8,128)(2,1)S(1)} %all-to-all-done.2.self_ref), channel_id=1, source_target_pairs={{0,4},{1,29},{4,0},{5,9},{8,12},{9,5},{12,8},{13,17},{16,20},{17,1... | collective-permute-start | bytes 1572872 | tf_op jit(solution)/shard_map/ppermute | solution.py:239
  83.4 2.9 %collective-permute-start.4 = (bf16[8,128,256]{2,1,0:T(8,128)(2,1)S(1)}, bf16[8,128,256]{2,1,0:T(8,128)(2,1)S(1)}, u32[]{:S(2)}, u32[]{:S(2)}) collective-permute-start(bf16[8,128,256]{2,1,0:T(8,128)(2,1)S(1)} %all-to-all-done.2.self_ref), channel_id=1, source_target_pairs={{0,1},{1,0},{2,3},{3,2},{4,5},{5,4},{6,7},{7,6},{8,9},{9,8},{10,11... | collective-permute-start | bytes 1572872 | tf_op jit(solution)/shard_map/ppermute | solution.py:240
  86.3 0.0 copy-start.1
  86.3 2.2 %copy-done.1 = bf16[8192,256]{1,0:T(8,128)(2,1)S(1)} copy-done((bf16[8192,256]{1,0:T(8,128)(2,1)S(1)}, bf16[8192,256]{1,0:T(8,128)(2,1)}, u32[]{:S(2)}) %copy-start.1) | copy-done | bytes 4194328
  88.5 0.3 project_first.1.part_ref
  88.8 3.7 %collective-permute-done.2.pair_ref = bf16[8,128,256]{2,1,0:T(8,128)(2,1)S(1)} collective-permute-done((bf16[8,128,256]{2,1,0:T(8,128)(2,1)S(1)}, bf16[8,128,256]{2,1,0:T(8,128)(2,1)S(1)}, u32[]{:S(2)}, u32[]{:S(2)}) %collective-permute-start.2) | collective-permute-done | bytes 524320 | tf_op jit(solution)/shard_map/ppermute | solution.py:239
  92.6 2.3 %collective-permute-start.3 = (bf16[8,128,256]{2,1,0:T(8,128)(2,1)S(1)}, bf16[8,128,256]{2,1,0:T(8,128)(2,1)S(1)}, u32[]{:S(2)}, u32[]{:S(2)}) collective-permute-start(bf16[8,128,256]{2,1,0:T(8,128)(2,1)S(1)} %collective-permute-done.2.pair_ref), channel_id=1, source_target_pairs={{0,1},{1,0},{2,3},{3,2},{4,5},{5,4},{6,7},{7,6},{8,9},{9,8},{10,11... | collective-permute-start | bytes 1572872 | tf_op jit(solution)/shard_map/ppermute | solution.py:255
  94.9 0.0 collective-permute-done.4.sibling_ref
  94.9 0.5 project_second.1.part_ref
  95.4 1.0 %collective-permute-done.3.sibling_ref = bf16[8,128,256]{2,1,0:T(8,128)(2,1)S(1)} collective-permute-done((bf16[8,128,256]{2,1,0:T(8,128)(2,1)S(1)}, bf16[8,128,256]{2,1,0:T(8,128)(2,1)S(1)}, u32[]{:S(2)}, u32[]{:S(2)}) %collective-permute-start.3) | collective-permute-done | bytes 524320 | tf_op jit(solution)/shard_map/ppermute | solution.py:255
  96.4 0.9 project_third.1
Async XLA Ops:
  0.0 45.9 %copy-start.3 = (bf16[128,256]{1,0:T(8,128)(2,1)S(1)}, bf16[128,256]{1,0:T(8,128)(2,1)}, u32[]{:S(2)}) copy-start(bf16[128,256]{1,0:T(8,128)(2,1)} %queries_ref.3) | copy-start | bytes 196612
  1.6 22.2 %all-to-all-start = ((bf16[32,16,256]{2,1,0:T(8,128)(2,1)}), bf16[32,16,256]{2,1,0:T(8,128)(2,1)S(1)}, u32[]{:S(2)}, u32[]{:S(2)}) async-start(bf16[32,16,256]{2,1,0:T(8,128)(2,1)} %spread_kv.1), calls=%async_computation | async-start | bytes 524288 | tf_op jit(solution)/shard_map/all_to_all | solution.py:197
  12.9 50.6 %copy-start.4 = (s32[64,2]{0,1:T(2,128)S(1)}, s32[64,2]{0,1:T(2,128)}, u32[]{:S(2)}) copy-start(s32[64,2]{0,1:T(2,128)} %param.9) | copy-start | bytes 1540
  12.9 9.2 %collective-permute-start = (bf16[128,256]{1,0:T(8,128)(2,1)}, bf16[128,256]{1,0:T(8,128)(2,1)S(1)}, u32[]{:S(2)}, u32[]{:S(2)}) collective-permute-start(bf16[128,256]{1,0:T(8,128)(2,1)} %queries_ref.3), channel_id=1, source_target_pairs={{0,2},{2,0},{1,3},{3,1},{4,6},{6,4},{5,7},{7,5},{8,10},{10,8},{9,1... | collective-permute-start | bytes 196616 | tf_op jit(solution)/shard_map/ppermute | solution.py:188
  39.4 8.7 %collective-permute-start.1 = (bf16[4,32,16,256]{3,2,1,0:T(8,128)(2,1)S(1)}, bf16[4,32,16,256]{3,2,1,0:T(8,128)(2,1)S(1)}, u32[]{:S(2)}, u32[]{:S(2)}) collective-permute-start(bf16[4,32,16,256]{3,2,1,0:T(8,128)(2,1)S(1)} %all_to_all.15.kv_ref), channel_id=1, source_target_pairs={{0,1},{1,0},{2,3},{3,2},{4,5},{5,4},{6,7},{7,6},{8,9},{9,8},{10,11... | collective-permute-start | bytes 3145736 | tf_op jit(solution)/shard_map/ppermute | solution.py:208
  50.9 30.5 %all-to-all-start.2 = ((bf16[8,128,256]{2,1,0:T(8,128)(2,1)}), bf16[8,128,256]{2,1,0:T(8,128)(2,1)S(1)}, u32[]{:S(2)}, u32[]{:S(2)}) async-start(bf16[8,128,256]{2,1,0:T(8,128)(2,1)} %attention_second.1), calls=%async_computation.2 | async-start | bytes 1048576 | tf_op jit(solution)/shard_map/all_to_all | solution.py:237
  63.5 2.2 %copy-start.2 = (bf16[8192,256]{1,0:T(8,128)(2,1)S(1)}, bf16[8192,256]{1,0:T(8,128)(2,1)}, u32[]{:S(2)}) copy-start(bf16[8192,256]{1,0:T(8,128)(2,1)} %weight_ref.1) | copy-start | bytes 12582916
  67.0 1.9 %copy-start = (bf16[8192,256]{1,0:T(8,128)(2,1)}, bf16[8192,256]{1,0:T(8,128)(2,1)S(1)}, u32[]{:S(2)}) copy-start(bf16[8192,256]{1,0:T(8,128)(2,1)S(1)} %prune.1.weight_ref) | copy-start | bytes 12582916
  81.4 11.1 %collective-permute-start.2 = (bf16[8,128,256]{2,1,0:T(8,128)(2,1)S(1)}, bf16[8,128,256]{2,1,0:T(8,128)(2,1)S(1)}, u32[]{:S(2)}, u32[]{:S(2)}) collective-permute-start(bf16[8,128,256]{2,1,0:T(8,128)(2,1)S(1)} %all-to-all-done.2.self_ref), channel_id=1, source_target_pairs={{0,4},{1,29},{4,0},{5,9},{8,12},{9,5},{12,8},{13,17},{16,20},{17,1... | collective-permute-start | bytes 1572872 | tf_op jit(solution)/shard_map/ppermute | solution.py:239
  83.4 11.5 %collective-permute-start.4 = (bf16[8,128,256]{2,1,0:T(8,128)(2,1)S(1)}, bf16[8,128,256]{2,1,0:T(8,128)(2,1)S(1)}, u32[]{:S(2)}, u32[]{:S(2)}) collective-permute-start(bf16[8,128,256]{2,1,0:T(8,128)(2,1)S(1)} %all-to-all-done.2.self_ref), channel_id=1, source_target_pairs={{0,1},{1,0},{2,3},{3,2},{4,5},{5,4},{6,7},{7,6},{8,9},{9,8},{10,11... | collective-permute-start | bytes 1572872 | tf_op jit(solution)/shard_map/ppermute | solution.py:240
  86.3 2.2 %copy-start.1 = (bf16[8192,256]{1,0:T(8,128)(2,1)S(1)}, bf16[8192,256]{1,0:T(8,128)(2,1)}, u32[]{:S(2)}) copy-start(bf16[8192,256]{1,0:T(8,128)(2,1)} %copy-done) | copy-start | bytes 12582916
  92.6 3.8 %collective-permute-start.3 = (bf16[8,128,256]{2,1,0:T(8,128)(2,1)S(1)}, bf16[8,128,256]{2,1,0:T(8,128)(2,1)S(1)}, u32[]{:S(2)}, u32[]{:S(2)}) collective-permute-start(bf16[8,128,256]{2,1,0:T(8,128)(2,1)S(1)} %collective-permute-done.2.pair_ref), channel_id=1, source_target_pairs={{0,1},{1,0},{2,3},{3,2},{4,5},{5,4},{6,7},{7,6},{8,9},{9,8},{10,11... | collective-permute-start | bytes 1572872 | tf_op jit(solution)/shard_map/ppermute | solution.py:255
